TPU v7x, 32 devices: a whole 2x2x4 slice. The times are simulated.
32 devices in a mesh: groups: 2 (over x), leaf: 16 (over z, y, core).
Axes of the slice: x: 2, y: 2, z: 4, core: 2. Of those that a mesh axis runs over, the one named last changes fastest.
Arguments:
- right_side: float32 [65536, 256], P(('groups', 'leaf')), parts along dimension 0, may hold values from -6 to 6
- cotangent: float32 [65536, 256], P(('groups', 'leaf')), parts along dimension 0, may hold values from -6 to 6
- coeff_basis: float32 [4, 64, 65536], P(None, None, ('groups', 'leaf')), parts along dimension 2, may hold values from -1 to 1
- saved_basis: float32 [4, 64, 65536], P(None, None, ('groups', 'leaf')), parts along dimension 2, may hold values from -0.24 to 0.24
- node_inverse: float32 [30, 128, 128], P('groups'), parts along dimension 0, may hold values from -1 to 2.5
- leaf_rows: int32 [32], P(('groups', 'leaf')), parts along dimension 0, may hold values from 1 to 2048, 24576 in all
Outputs:
- solution: float32 [65536, 256], P(('groups', 'leaf')), parts along dimension 0
- grad_left: bfloat16 [4, 64, 65536], P(None, None, ('groups', 'leaf')), parts along dimension 2
- grad_right: bfloat16 [4, 64, 65536], P(None, None, ('groups', 'leaf')), parts along dimension 2
There are 2 independent parts, one for each index of `groups`. A program takes and returns all parts, laid end to end along the dimension named above; each array names one. Nothing has to cross between parts.
Inputs may be any that keep to these rules, and one draw needn't show every extreme that they name: `leaf_rows`: every leaf has at least one live row; the live rows of all leaves sum to 24576, and some leaf has all 2048 rows live.
All inputs are finite; a program needn't handle non-finite values. No bound on the sum of `leaf_rows` on one device may be relied on, other than what follows from the above.
Results may differ from a plain program's by a relative error of at most 0.001.
Values sent between devices are 32-bit elements; how exact they have to be, the bound alone decides.
No kernel may reach another device: no remote copies, remote signals or barrier semaphores. Data moves between devices by JAX's collectives and lax.ppermute only.
A program may use at most 64 MiB of HBM per device.

v0:
```python
import functools

import jax
import jax.numpy as jnp
from jax import lax
from jax.experimental import pallas as pl
from jax.experimental.pallas import tpu as pltpu
from jax.sharding import PartitionSpec as P


HIGH = lax.Precision.HIGH
F32 = jnp.float32


def dot(a, b, dims=((1,), (0,))):
    return lax.dot_general(a, b, (dims, ((), ())), precision=HIGH, preferred_element_type=F32)


def pack(blocks):
    rows = []
    for i in range(0, len(blocks) - 1, 2):
        rows.append(jnp.concatenate([blocks[i], blocks[i + 1]], 1))
    if len(blocks) % 2:
        half = blocks[-1].shape[0] // 2
        rows.append(jnp.concatenate([blocks[-1][:half], blocks[-1][half:]], 1))
    return rows


def pack_rows(count, rank):
    return count // 2 * rank + count % 2 * (rank // 2)


def unpack(ref, start, count, rank):
    blocks = []
    for i in range(count):
        if i == count - 1 and count % 2:
            half = ref[start : start + rank // 2, :]
            blocks.append(jnp.concatenate([half[:, :rank], half[:, rank:]], 0))
        else:
            lane = i % 2 * rank
            blocks.append(ref[start : start + rank, lane : lane + rank])
            start += i % 2 * rank
    return blocks


def solve_rows(level, levels, rank):
    return rank + pack_rows(levels - 1 - level, rank)


def side_rows(level, levels, rank):
    return rank + pack_rows(levels - level, rank)


def local_kernel(dims, rows_ref, x_ref, w_ref, u_ref, q_ref, node_ref, *refs):
    levels, rank, base_bits, chunk = dims
    solve_keep, solve_send, side_keep, side_send, nodes_out, c_acc, k_acc, g_acc, sems = refs
    step = pl.program_id(0)
    position = lax.axis_index("leaf")

    def node_copy(k):
        index = 2**levels - 2 ** (levels - k) + jnp.right_shift(position, base_bits + k + 1)
        return pltpu.make_async_copy(node_ref.at[index], nodes_out.at[k], sems.at[k])

    @pl.when(step == 0)
    def _():
        for k in range(levels):
            node_copy(k).start()
        c_acc[...] = jnp.zeros_like(c_acc)
        k_acc[...] = jnp.zeros_like(k_acc)
        g_acc[...] = jnp.zeros_like(g_acc)

    place = step * chunk + lax.broadcasted_iota(jnp.int32, (1, chunk), 1)
    u = jnp.where(place < rows_ref[0], u_ref[...], 0.0)
    c_acc[...] += dot(u, x_ref[...])
    k_acc[...] += dot(u, w_ref[...])
    g_acc[...] += dot(u, q_ref[...], ((1,), (1,)))

    @pl.when(step == pl.num_programs(0) - 1)
    def _():
        half = c_acc.shape[1] // 2
        is_first = position % 2 == 0

        def block(i, j):
            return g_acc[i * rank : (i + 1) * rank, j * rank : (j + 1) * rank]

        def write(keep, send, acc, blocks_of):
            at = 0
            for k in range(levels):
                low = acc[k * rank : (k + 1) * rank, :half]
                high = acc[k * rank : (k + 1) * rank, half:]
                keep[at : at + rank, :] = jnp.where(is_first, low, high)
                send[at : at + rank, :] = jnp.where(is_first, high, low)
                at += rank
                for rows in pack(blocks_of(k)):
                    keep[at : at + rows.shape[0], :] = rows
                    send[at : at + rows.shape[0], :] = rows
                    at += rows.shape[0]

        write(solve_keep, solve_send, c_acc, lambda k: [block(i, k) for i in range(k + 1, levels)])
        write(side_keep, side_send, k_acc, lambda k: [block(k, j) for j in range(k, levels)])
        for k in range(levels):
            node_copy(k).wait()


def level_kernel(dims, level, own_ref, sib_ref, nodes_ref, z_ref, *next_ref):
    levels, rank, base_bits = dims
    is_lower = jnp.right_shift(lax.axis_index("leaf"), base_bits + level) % 2 == 0
    own, sib = own_ref[:rank, :], sib_ref[:rank, :]
    both = jnp.concatenate([jnp.where(is_lower, own, sib), jnp.where(is_lower, sib, own)], 0)
    mixed = dot(nodes_ref[level], both)
    z_own = jnp.where(is_lower, mixed[:rank], mixed[rank:])
    z_sib = jnp.where(is_lower, mixed[rank:], mixed[:rank])
    z_ref[:rank, :] = z_own
    z_ref[rank:, :] = z_sib
    if not next_ref:
        return
    (out_ref,) = next_ref
    count = levels - 1 - level
    h_own = unpack(own_ref, rank, count, rank)
    h_sib = unpack(sib_ref, rank, count, rank)
    h_both = jnp.concatenate(
        [jnp.concatenate(h_own, 0), jnp.concatenate(h_sib, 0)], 1
    )
    drop = dot(h_both, jnp.concatenate([z_own, z_sib], 0))
    start = solve_rows(level, levels, rank)
    at = 0
    for i in range(count):
        out_ref[at : at + rank, :] = (
            own_ref[start + at : start + at + rank, :]
            + sib_ref[start + at : start + at + rank, :]
            - drop[i * rank : (i + 1) * rank]
        )
        at += rank
        rest = solve_rows(level + 1 + i, levels, rank) - rank
        if rest:
            out_ref[at : at + rest, :] = (
                own_ref[start + at : start + at + rest, :] + sib_ref[start + at : start + at + rest, :]
            )
            at += rest


def end_kernel(dims, scale, pair, *refs):
    levels, rank = dims
    sib_solve, sib_side, z_refs = refs[:levels], refs[levels : 2 * levels], refs[2 * levels : 3 * levels]
    refs = refs[3 * levels :]
    z_all = jnp.concatenate([z_ref[:rank, :] for z_ref in z_refs], 0)

    def lower_term(k, solve_ref, side_ref, z_here):
        blocks = unpack(side_ref, rank, levels - k, rank)
        if k + 1 < levels:
            z_here = jnp.concatenate([z_here, z_all[(k + 1) * rank :]], 0)
        return (solve_ref[:rank, :] - dot(jnp.concatenate(blocks, 1), z_here)) * scale

    def write(out_ref, k, z_term, l_term, k_term):
        for part, term in enumerate((z_term, l_term, k_term)):
            at = (part * levels + k) * rank
            out_ref[at : at + rank, :] = term

    for k in range(levels):
        z_own, z_sib = z_refs[k][:rank, :], z_refs[k][rank:, :]
        terms = (z_own, lower_term(k, sib_solve[k], sib_side[k], z_sib), sib_side[k][:rank, :] * scale)
        write(refs[-1], k, *terms)
        if pair:
            own_solve, own_side, send_ref = refs[:3]
            if k == 0:
                terms = (z_sib, lower_term(0, own_solve, own_side, z_own), own_side[:rank, :] * scale)
            write(send_ref, k, *terms)


def final_kernel(chunk, rows_ref, own_ref, other_ref, x_ref, w_ref, q_ref, sol_ref, left_ref, right_ref):
    is_first = lax.axis_index("leaf") % 2 == 0
    count = own_ref.shape[0] // 3

    def whole(part):
        own = own_ref[part * count : (part + 1) * count, :]
        other = other_ref[part * count : (part + 1) * count, :]
        return jnp.concatenate([jnp.where(is_first, own, other), jnp.where(is_first, other, own)], 1)

    first = pl.program_id(0) * chunk
    live_row = first + lax.broadcasted_iota(jnp.int32, (chunk, 1), 0) < rows_ref[0]
    live_lane = first + lax.broadcasted_iota(jnp.int32, (1, chunk), 1) < rows_ref[0]
    x = x_ref[...] - dot(q_ref[...], whole(0), ((0,), (0,)))
    x = jnp.where(live_row, x, 0.0)
    sol_ref[...] = x
    left = dot(whole(1), w_ref[...], ((1,), (1,)))
    left_ref[...] = jnp.where(live_lane, left, 0.0).astype(left_ref.dtype)
    right_ref[...] = dot(whole(2), x, ((1,), (1,))).astype(right_ref.dtype)


def swapped(value, bit):
    mask = 2**bit
    pairs = [(source, source ^ mask) for source in range(lax.axis_size("leaf"))]
    return lax.ppermute(value, "leaf", pairs)


def body(right_side, cotangent, coeff_basis, saved_basis, node_inverse, leaf_rows):
    row_count, col_count = right_side.shape
    levels, rank = coeff_basis.shape[:2]
    wide = levels * rank
    half = col_count // 2
    base_bits = lax.axis_size("leaf").bit_length() - 1 - levels
    chunk = min(512, row_count)
    steps = row_count // chunk
    u_all = coeff_basis.reshape(wide, row_count)
    q_all = saved_basis.reshape(wide, row_count)

    smem = pl.BlockSpec(memory_space=pltpu.SMEM)
    by_row = pl.BlockSpec((chunk, col_count), lambda i: (i, 0))
    by_lane = pl.BlockSpec((wide, chunk), lambda i: (0, i))

    def fixed(*shape):
        return pl.BlockSpec(shape, lambda i: (0,) * len(shape))

    n_solve = sum(solve_rows(k, levels, rank) for k in range(levels))
    n_side = sum(side_rows(k, levels, rank) for k in range(levels))
    order = 2 * rank
    shapes = [(n_solve, half)] * 2 + [(n_side, half)] * 2 + [(levels, order, order)]
    solve, solve_send, side, side_send, nodes = pl.pallas_call(
        functools.partial(local_kernel, (levels, rank, base_bits, chunk)),
        grid=(steps,),
        out_shape=[jax.ShapeDtypeStruct(s, F32) for s in shapes],
        in_specs=[smem, by_row, by_row, by_lane, by_lane, pl.BlockSpec(memory_space=pl.ANY)],
        out_specs=[fixed(*s) for s in shapes],
        scratch_shapes=[pltpu.VMEM((wide, col_count), F32)] * 2
        + [pltpu.VMEM((wide, wide), F32), pltpu.SemaphoreType.DMA((levels,))],
        name="local_sums",
    )(leaf_rows, right_side, cotangent, u_all, q_all, node_inverse)

    if base_bits == 0:
        sib_solve, sib_side = swapped(solve_send, 0), swapped(side_send, 0)
    else:
        solve, side = solve + swapped(solve_send, 0), side + swapped(side_send, 0)
        for bit in range(1, base_bits):
            solve, side = solve + swapped(solve, bit), side + swapped(side, bit)
        sib_solve, sib_side = swapped(solve, base_bits), swapped(side, base_bits)

    vmem = pl.BlockSpec(memory_space=pltpu.VMEM)
    first_solve, first_side = solve, side
    solves, sides, zs = [], [], []
    for k in range(levels):
        if k > 0:
            sib_solve, sib_side = swapped(solve, base_bits + k), swapped(side, base_bits + k)
        solves.append(sib_solve)
        sides.append(sib_side)
        rows = solve.shape[0] - solve_rows(k, levels, rank)
        out_shape = [jax.ShapeDtypeStruct((order, half), F32)]
        if rows:
            out_shape.append(jax.ShapeDtypeStruct((rows, half), F32))
        outs = pl.pallas_call(
            functools.partial(level_kernel, (levels, rank, base_bits), k),
            out_shape=out_shape,
            in_specs=[vmem] * 3,
            out_specs=[vmem] * len(out_shape),
            name=f"level_{k}",
        )(solve, sib_solve, nodes)
        zs.append(outs[0])
        if rows:
            solve = outs[1]
            side = (side + sib_side)[side_rows(k, levels, rank) :]

    pair = base_bits == 0
    ends = [*solves, *sides, *zs] + ([first_solve, first_side] if pair else [])
    *send, own = pl.pallas_call(
        functools.partial(end_kernel, (levels, rank), 1.0 / col_count**0.5, pair),
        out_shape=[jax.ShapeDtypeStruct((3 * wide, half), F32)] * (2 if pair else 1),
        in_specs=[vmem] * len(ends),
        out_specs=[vmem] * (2 if pair else 1),
        name="end_factors",
    )(*ends)
    other = swapped(send[0] if pair else own, 0)

    sol, left, right = pl.pallas_call(
        functools.partial(final_kernel, chunk),
        grid=(steps,),
        out_shape=[
            jax.ShapeDtypeStruct((row_count, col_count), F32),
            jax.ShapeDtypeStruct((wide, row_count), jnp.bfloat16),
            jax.ShapeDtypeStruct((wide, row_count), jnp.bfloat16),
        ],
        in_specs=[smem, fixed(3 * wide, half), fixed(3 * wide, half), by_row, by_row, by_lane],
        out_specs=[by_row, by_lane, by_lane],
        name="row_outputs",
    )(leaf_rows, own, other, right_side, cotangent, q_all)
    return sol, left.reshape(coeff_basis.shape), right.reshape(coeff_basis.shape)


def solution(mesh):
    in_specs = (
        P(("groups", "leaf"), None),
        P(("groups", "leaf"), None),
        P(None, None, ("groups", "leaf")),
        P(None, None, ("groups", "leaf")),
        P("groups", None, None),
        P(("groups", "leaf")),
    )
    out_specs = (
        P(("groups", "leaf"), None),
        P(None, None, ("groups", "leaf")),
        P(None, None, ("groups", "leaf")),
    )
    return jax.shard_map(body, mesh=mesh, in_specs=in_specs, out_specs=out_specs, check_vma=False)
```

profile of v0, /device:TPU:0, one launch (start us, length us, event | category | flops | bytes accessed | tf_op | source)
XLA Modules:
  0.0 53.8 jit_solution(16866923843880205525)
XLA Ops:
  1.3 6.9 %local_sums.1 = (f32[448,128]{1,0:T(8,128)}, f32[448,128]{1,0:T(8,128)}, f32[576,128]{1,0:T(8,128)}, f32[576,128]{1,0:T(8,128)}, f32[4,128,128]{2,1,0:T(8,128)}) custom-call(s32[1]{0:T(128)S(6)} %copy.9.rows_ref, f32[2048,256]{1,0:T(8,128)} %x_ref.3, f32[2048,256]{1,0:T(8,128)} %w_ref.3, f32[256,2048]{1,0:T(8,128)} %bitcast.6, f32[256,2048]{1,0:T(8,128)} %bitcast.4, ...), custom_call_target="tpu_custom_call" | custom-call | tf_op jit(solution)/shard_map/local_sums/pallas_call | solution.py:218
  8.2 0.5 collective-permute-start.4
  8.7 0.1 collective-permute-start
  8.8 1.3 %collective-permute-done.4.refs_4_ = f32[576,128]{1,0:T(8,128)S(1)} collective-permute-done((f32[576,128]{1,0:T(8,128)}, f32[576,128]{1,0:T(8,128)S(1)}, u32[]{:S(2)}, u32[]{:S(2)}) %collective-permute-start.4) | collective-permute-done | bytes 294944 | tf_op jit(solution)/shard_map/ppermute | solution.py:193
  10.2 0.0 copy-start.1
  10.2 1.1 %slice_add_fusion = f32[384,128]{1,0:T(8,128)S(1)} fusion(f32[576,128]{1,0:T(8,128)S(1)} %collective-permute-done.4.refs_4_, f32[576,128]{1,0:T(8,128)} %get-tuple-element.26.refs_13_), kind=kLoop, calls=%fused_computation | loop fusion | flops 49152 | bytes 589824 | tf_op jit(solution)/shard_map/add | solution.py:259
  11.2 3.0 %collective-permute-start.5 = (f32[384,128]{1,0:T(8,128)S(1)}, f32[384,128]{1,0:T(8,128)S(1)}, u32[]{:S(2)}, u32[]{:S(2)}) collective-permute-start(f32[384,128]{1,0:T(8,128)S(1)} %slice_add_fusion), channel_id=1, source_target_pairs={{0,2},{1,3},{2,0},{3,1},{4,6},{5,7},{6,4},{7,5},{8,10},{9,11},{10,... | collective-permute-start | bytes 589832 | tf_op jit(solution)/shard_map/ppermute | solution.py:193
  14.2 0.0 collective-permute-done.sib_ref.refs_0_
  14.2 0.0 copy-start
  14.2 0.7 %copy-done = f32[448,128]{1,0:T(8,128)} copy-done((f32[448,128]{1,0:T(8,128)}, f32[448,128]{1,0:T(8,128)S(1)}, u32[]{:S(2)}) %copy-start) | copy-done | bytes 229400
  14.9 2.2 %level_0.1 = (f32[128,128]{1,0:T(8,128)}, f32[288,128]{1,0:T(8,128)}) custom-call(f32[448,128]{1,0:T(8,128)} %get-tuple-element.20.own_ref.refs_12_, f32[448,128]{1,0:T(8,128)} %copy-done, f32[4,128,128]{2,1,0:T(8,128)} %get-tuple-element.21.nodes_ref), custom_call_target="tpu_custom_call" | custom-call | tf_op jit(solution)/shard_map/level_0/pallas_call | solution.py:249
  17.1 0.0 collective-permute-start.1
  17.1 2.3 %collective-permute-done.5.refs_5_ = f32[384,128]{1,0:T(8,128)S(1)} collective-permute-done((f32[384,128]{1,0:T(8,128)S(1)}, f32[384,128]{1,0:T(8,128)S(1)}, u32[]{:S(2)}, u32[]{:S(2)}) %collective-permute-start.5) | collective-permute-done | bytes 196640 | tf_op jit(solution)/shard_map/ppermute | solution.py:193
  19.4 0.0 copy-start.3
  19.4 1.8 %collective-permute-start.6 = (f32[224,128]{1,0:T(8,128)S(1)}, f32[224,128]{1,0:T(8,128)S(1)}, u32[]{:S(2)}, u32[]{:S(2)}) collective-permute-start(f32[224,128]{1,0:T(8,128)S(1)} %slice_add_fusion.1), channel_id=1, source_target_pairs={{0,4},{1,5},{2,6},{3,7},{4,0},{5,1},{6,2},{7,3},{8,12},{9,13},{10,... | collective-permute-start | bytes 344072 | tf_op jit(solution)/shard_map/ppermute | solution.py:193
  21.3 1.7 %collective-permute-done.1.sib_ref.refs_1_ = f32[288,128]{1,0:T(8,128)S(1)} collective-permute-done((f32[288,128]{1,0:T(8,128)}, f32[288,128]{1,0:T(8,128)S(1)}, u32[]{:S(2)}, u32[]{:S(2)}) %collective-permute-start.1) | collective-permute-done | bytes 147488 | tf_op jit(solution)/shard_map/ppermute | solution.py:193
  22.9 0.0 copy-start.2
  22.9 0.7 %copy-done.2 = f32[288,128]{1,0:T(8,128)} copy-done((f32[288,128]{1,0:T(8,128)}, f32[288,128]{1,0:T(8,128)S(1)}, u32[]{:S(2)}) %copy-start.2) | copy-done | bytes 147480
  23.6 2.1 %level_1.1 = (f32[128,128]{1,0:T(8,128)}, f32[160,128]{1,0:T(8,128)}) custom-call(f32[288,128]{1,0:T(8,128)} %get-tuple-element.22.own_ref, f32[288,128]{1,0:T(8,128)} %copy-done.2, f32[4,128,128]{2,1,0:T(8,128)} %get-tuple-element.21.nodes_ref), custom_call_target="tpu_custom_call" | custom-call | tf_op jit(solution)/shard_map/level_1/pallas_call | solution.py:249
  25.7 1.6 %collective-permute-start.2 = (f32[160,128]{1,0:T(8,128)}, f32[160,128]{1,0:T(8,128)S(1)}, u32[]{:S(2)}, u32[]{:S(2)}) collective-permute-start(f32[160,128]{1,0:T(8,128)} %get-tuple-element.23.own_ref), channel_id=1, source_target_pairs={{0,4},{1,5},{2,6},{3,7},{4,0},{5,1},{6,2},{7,3},{8,12},{9,13},{10,... | collective-permute-start | bytes 245768 | tf_op jit(solution)/shard_map/ppermute | solution.py:193
  27.3 0.0 collective-permute-done.6.refs_6_
  27.3 0.0 copy-start.6
  27.3 2.7 %collective-permute-start.7 = (f32[96,128]{1,0:T(8,128)S(1)}, f32[96,128]{1,0:T(8,128)S(1)}, u32[]{:S(2)}, u32[]{:S(2)}) collective-permute-start(f32[96,128]{1,0:T(8,128)S(1)} %slice_add_fusion.2), channel_id=1, source_target_pairs={{0,8},{1,9},{2,10},{3,11},{4,12},{5,13},{6,14},{7,15},{8,0},{9,1},... | collective-permute-start | bytes 147464 | tf_op jit(solution)/shard_map/ppermute | solution.py:193
  29.9 0.9 %collective-permute-done.2.sib_ref.refs_2_ = f32[160,128]{1,0:T(8,128)S(1)} collective-permute-done((f32[160,128]{1,0:T(8,128)}, f32[160,128]{1,0:T(8,128)S(1)}, u32[]{:S(2)}, u32[]{:S(2)}) %collective-permute-start.2) | collective-permute-done | bytes 81952 | tf_op jit(solution)/shard_map/ppermute | solution.py:193
  30.9 0.0 copy-start.5
  30.9 0.6 %copy-done.5 = f32[160,128]{1,0:T(8,128)} copy-done((f32[160,128]{1,0:T(8,128)}, f32[160,128]{1,0:T(8,128)S(1)}, u32[]{:S(2)}) %copy-start.5) | copy-done | bytes 81944
  31.5 2.0 %level_2.1 = (f32[128,128]{1,0:T(8,128)}, f32[64,128]{1,0:T(8,128)}) custom-call(f32[160,128]{1,0:T(8,128)} %get-tuple-element.23.own_ref, f32[160,128]{1,0:T(8,128)} %copy-done.5, f32[4,128,128]{2,1,0:T(8,128)} %get-tuple-element.21.nodes_ref), custom_call_target="tpu_custom_call" | custom-call | tf_op jit(solution)/shard_map/level_2/pallas_call | solution.py:249
  33.5 2.1 %collective-permute-start.3 = (f32[64,128]{1,0:T(8,128)}, f32[64,128]{1,0:T(8,128)S(1)}, u32[]{:S(2)}, u32[]{:S(2)}) collective-permute-start(f32[64,128]{1,0:T(8,128)} %get-tuple-element.24.own_ref), channel_id=1, source_target_pairs={{0,8},{1,9},{2,10},{3,11},{4,12},{5,13},{6,14},{7,15},{8,0},{9,1},... | collective-permute-start | bytes 98312 | tf_op jit(solution)/shard_map/ppermute | solution.py:193
  35.6 3.0 %collective-permute-done.3.sib_ref.refs_3_ = f32[64,128]{1,0:T(8,128)S(1)} collective-permute-done((f32[64,128]{1,0:T(8,128)}, f32[64,128]{1,0:T(8,128)S(1)}, u32[]{:S(2)}, u32[]{:S(2)}) %collective-permute-start.3) | collective-permute-done | bytes 32800 | tf_op jit(solution)/shard_map/ppermute | solution.py:193
  38.5 0.0 copy-start.7
  38.5 0.6 %copy-done.7 = f32[64,128]{1,0:T(8,128)} copy-done((f32[64,128]{1,0:T(8,128)}, f32[64,128]{1,0:T(8,128)S(1)}, u32[]{:S(2)}) %copy-start.7) | copy-done | bytes 32792
  39.1 1.8 %level_3.1.refs_11_ = f32[128,128]{1,0:T(8,128)} custom-call(f32[64,128]{1,0:T(8,128)} %get-tuple-element.24.own_ref, f32[64,128]{1,0:T(8,128)} %copy-done.7, f32[4,128,128]{2,1,0:T(8,128)} %get-tuple-element.21.nodes_ref), custom_call_target="tpu_custom_call" | custom-call | tf_op jit(solution)/shard_map/level_3/pallas_call | solution.py:249
  40.9 0.0 collective-permute-done.7.refs_7_
  40.9 0.0 copy-start.8
  40.9 0.0 copy-done.1
  40.9 0.0 copy-done.3
  40.9 0.0 copy-done.6
  41.0 0.6 %copy-done.8 = f32[96,128]{1,0:T(8,128)} copy-done((f32[96,128]{1,0:T(8,128)}, f32[96,128]{1,0:T(8,128)S(1)}, u32[]{:S(2)}) %copy-start.8) | copy-done | bytes 49176
  41.5 2.7 %end_factors.1 = (f32[768,128]{1,0:T(8,128)}, f32[768,128]{1,0:T(8,128)}) custom-call(f32[448,128]{1,0:T(8,128)} %copy-done, f32[288,128]{1,0:T(8,128)} %copy-done.2, f32[160,128]{1,0:T(8,128)} %copy-done.5, f32[64,128]{1,0:T(8,128)} %copy-done.7, f32[576,128]{1,0:T(8,128)} %copy-done.1, f32[384,128]{1,0:T(8,128)} %copy-done.3, f32[224,128]{1,0:T(8,128)} %copy-done.6, ...), custom_call_target="tpu_custom_call" | custom-call | tf_op jit(solution)/shard_map/end_factors/pallas_call | solution.py:263
  44.3 0.0 collective-permute-start.8
  44.3 1.9 %collective-permute-done.8.other_ref = f32[768,128]{1,0:T(8,128)S(1)} collective-permute-done((f32[768,128]{1,0:T(8,128)}, f32[768,128]{1,0:T(8,128)S(1)}, u32[]{:S(2)}, u32[]{:S(2)}) %collective-permute-start.8) | collective-permute-done | bytes 393248 | tf_op jit(solution)/shard_map/ppermute | solution.py:193
  46.2 0.0 copy-start.4
  46.2 0.7 %copy-done.4 = f32[768,128]{1,0:T(8,128)} copy-done((f32[768,128]{1,0:T(8,128)}, f32[768,128]{1,0:T(8,128)S(1)}, u32[]{:S(2)}) %copy-start.4) | copy-done | bytes 393240
  47.0 6.9 %row_outputs.1 = (f32[2048,256]{1,0:T(8,128)}, bf16[256,2048]{1,0:T(8,128)(2,1)}, bf16[256,2048]{1,0:T(8,128)(2,1)}) custom-call(s32[1]{0:T(128)S(6)} %copy.9.rows_ref, f32[768,128]{1,0:T(8,128)} %get-tuple-element.30.own_ref, f32[768,128]{1,0:T(8,128)} %copy-done.4, f32[2048,256]{1,0:T(8,128)} %x_ref.3, f32[2048,256]{1,0:T(8,128)} %w_ref.3, f32[256,2048]{1,0:T(8,128)} %bitcast.5), custom_call_target="tpu_custom_call" | custom-call | tf_op jit(solution)/shard_map/row_outputs/pallas_call | solution.py:272
  (2 shorter events, 0.0 us)
Async XLA Ops:
  8.2 1.9 %collective-permute-start.4 = (f32[576,128]{1,0:T(8,128)}, f32[576,128]{1,0:T(8,128)S(1)}, u32[]{:S(2)}, u32[]{:S(2)}) collective-permute-start(f32[576,128]{1,0:T(8,128)} %get-tuple-element.25), channel_id=1, source_target_pairs={{0,1},{1,0},{2,3},{3,2},{4,5},{5,4},{6,7},{7,6},{8,9},{9,8},{10,11... | collective-permute-start | bytes 884744 | tf_op jit(solution)/shard_map/ppermute | solution.py:193
  8.7 5.4 %collective-permute-start = (f32[448,128]{1,0:T(8,128)}, f32[448,128]{1,0:T(8,128)S(1)}, u32[]{:S(2)}, u32[]{:S(2)}) collective-permute-start(f32[448,128]{1,0:T(8,128)} %get-tuple-element.19), channel_id=1, source_target_pairs={{0,1},{1,0},{2,3},{3,2},{4,5},{5,4},{6,7},{7,6},{8,9},{9,8},{10,11... | collective-permute-start | bytes 688136 | tf_op jit(solution)/shard_map/ppermute | solution.py:193
  10.2 30.8 %copy-start.1 = (f32[576,128]{1,0:T(8,128)}, f32[576,128]{1,0:T(8,128)S(1)}, u32[]{:S(2)}) copy-start(f32[576,128]{1,0:T(8,128)S(1)} %collective-permute-done.4.refs_4_) | copy-start | bytes 884740
  11.2 8.2 %collective-permute-start.5 = (f32[384,128]{1,0:T(8,128)S(1)}, f32[384,128]{1,0:T(8,128)S(1)}, u32[]{:S(2)}, u32[]{:S(2)}) collective-permute-start(f32[384,128]{1,0:T(8,128)S(1)} %slice_add_fusion), channel_id=1, source_target_pairs={{0,2},{1,3},{2,0},{3,1},{4,6},{5,7},{6,4},{7,5},{8,10},{9,11},{10,... | collective-permute-start | bytes 589832 | tf_op jit(solution)/shard_map/ppermute | solution.py:193
  14.2 0.7 %copy-start = (f32[448,128]{1,0:T(8,128)}, f32[448,128]{1,0:T(8,128)S(1)}, u32[]{:S(2)}) copy-start(f32[448,128]{1,0:T(8,128)S(1)} %collective-permute-done.sib_ref.refs_0_) | copy-start | bytes 688132
  17.1 5.8 %collective-permute-start.1 = (f32[288,128]{1,0:T(8,128)}, f32[288,128]{1,0:T(8,128)S(1)}, u32[]{:S(2)}, u32[]{:S(2)}) collective-permute-start(f32[288,128]{1,0:T(8,128)} %get-tuple-element.22.own_ref), channel_id=1, source_target_pairs={{0,2},{1,3},{2,0},{3,1},{4,6},{5,7},{6,4},{7,5},{8,10},{9,11},{10,... | collective-permute-start | bytes 442376 | tf_op jit(solution)/shard_map/ppermute | solution.py:193
  19.4 21.5 %copy-start.3 = (f32[384,128]{1,0:T(8,128)}, f32[384,128]{1,0:T(8,128)S(1)}, u32[]{:S(2)}) copy-start(f32[384,128]{1,0:T(8,128)S(1)} %collective-permute-done.5.refs_5_) | copy-start | bytes 589828
  19.4 7.8 %collective-permute-start.6 = (f32[224,128]{1,0:T(8,128)S(1)}, f32[224,128]{1,0:T(8,128)S(1)}, u32[]{:S(2)}, u32[]{:S(2)}) collective-permute-start(f32[224,128]{1,0:T(8,128)S(1)} %slice_add_fusion.1), channel_id=1, source_target_pairs={{0,4},{1,5},{2,6},{3,7},{4,0},{5,1},{6,2},{7,3},{8,12},{9,13},{10,... | collective-permute-start | bytes 344072 | tf_op jit(solution)/shard_map/ppermute | solution.py:193
  22.9 0.7 %copy-start.2 = (f32[288,128]{1,0:T(8,128)}, f32[288,128]{1,0:T(8,128)S(1)}, u32[]{:S(2)}) copy-start(f32[288,128]{1,0:T(8,128)S(1)} %collective-permute-done.1.sib_ref.refs_1_) | copy-start | bytes 442372
  25.7 5.2 %collective-permute-start.2 = (f32[160,128]{1,0:T(8,128)}, f32[160,128]{1,0:T(8,128)S(1)}, u32[]{:S(2)}, u32[]{:S(2)}) collective-permute-start(f32[160,128]{1,0:T(8,128)} %get-tuple-element.23.own_ref), channel_id=1, source_target_pairs={{0,4},{1,5},{2,6},{3,7},{4,0},{5,1},{6,2},{7,3},{8,12},{9,13},{10,... | collective-permute-start | bytes 245768 | tf_op jit(solution)/shard_map/ppermute | solution.py:193
  27.3 13.7 %copy-start.6 = (f32[224,128]{1,0:T(8,128)}, f32[224,128]{1,0:T(8,128)S(1)}, u32[]{:S(2)}) copy-start(f32[224,128]{1,0:T(8,128)S(1)} %collective-permute-done.6.refs_6_) | copy-start | bytes 344068
  27.3 13.7 %collective-permute-start.7 = (f32[96,128]{1,0:T(8,128)S(1)}, f32[96,128]{1,0:T(8,128)S(1)}, u32[]{:S(2)}, u32[]{:S(2)}) collective-permute-start(f32[96,128]{1,0:T(8,128)S(1)} %slice_add_fusion.2), channel_id=1, source_target_pairs={{0,8},{1,9},{2,10},{3,11},{4,12},{5,13},{6,14},{7,15},{8,0},{9,1},... | collective-permute-start | bytes 147464 | tf_op jit(solution)/shard_map/ppermute | solution.py:193
  30.9 0.6 %copy-start.5 = (f32[160,128]{1,0:T(8,128)}, f32[160,128]{1,0:T(8,128)S(1)}, u32[]{:S(2)}) copy-start(f32[160,128]{1,0:T(8,128)S(1)} %collective-permute-done.2.sib_ref.refs_2_) | copy-start | bytes 245764
  33.5 5.0 %collective-permute-start.3 = (f32[64,128]{1,0:T(8,128)}, f32[64,128]{1,0:T(8,128)S(1)}, u32[]{:S(2)}, u32[]{:S(2)}) collective-permute-start(f32[64,128]{1,0:T(8,128)} %get-tuple-element.24.own_ref), channel_id=1, source_target_pairs={{0,8},{1,9},{2,10},{3,11},{4,12},{5,13},{6,14},{7,15},{8,0},{9,1},... | collective-permute-start | bytes 98312 | tf_op jit(solution)/shard_map/ppermute | solution.py:193
  38.5 0.6 %copy-start.7 = (f32[64,128]{1,0:T(8,128)}, f32[64,128]{1,0:T(8,128)S(1)}, u32[]{:S(2)}) copy-start(f32[64,128]{1,0:T(8,128)S(1)} %collective-permute-done.3.sib_ref.refs_3_) | copy-start | bytes 98308
  40.9 0.6 %copy-start.8 = (f32[96,128]{1,0:T(8,128)}, f32[96,128]{1,0:T(8,128)S(1)}, u32[]{:S(2)}) copy-start(f32[96,128]{1,0:T(8,128)S(1)} %collective-permute-done.7.refs_7_) | copy-start | bytes 147460
  44.3 1.9 %collective-permute-start.8 = (f32[768,128]{1,0:T(8,128)}, f32[768,128]{1,0:T(8,128)S(1)}, u32[]{:S(2)}, u32[]{:S(2)}) collective-permute-start(f32[768,128]{1,0:T(8,128)} %get-tuple-element.31), channel_id=1, source_target_pairs={{0,1},{1,0},{2,3},{3,2},{4,5},{5,4},{6,7},{7,6},{8,9},{9,8},{10,11... | collective-permute-start | bytes 1179656 | tf_op jit(solution)/shard_map/ppermute | solution.py:193
  46.2 0.7 %copy-start.4 = (f32[768,128]{1,0:T(8,128)}, f32[768,128]{1,0:T(8,128)S(1)}, u32[]{:S(2)}) copy-start(f32[768,128]{1,0:T(8,128)S(1)} %collective-permute-done.8.other_ref) | copy-start | bytes 1179652
where the time goes:
time: 54.2 us; the launch traced here: 53.8 us
  Pallas kernels  24.7 us (46%)
  starting transfers between devices  11.7 us (22%)
  waiting for transfers between devices  11.2 us (21%)
  local copies, waits for them, and re-layouts  3.94 us (7%)
  between operations  1.33 us (2%)
  other arithmetic  1.08 us (2%)
    ppermute x9, starting transfers between devices, swapped(): return lax.ppermute(value, 'leaf', pairs)  11.7 us
    ppermute x9, waiting for transfers between devices, swapped(): return lax.ppermute(value, 'leaf', pairs)  11.2 us
    pallas_call x4, Pallas kernels, body(): pl.pallas_call(functools.partial(level_kernel, (levels, rank, base_bits),...  8.13 us
    pallas_call x1, Pallas kernels, body(): pl.pallas_call(functools.partial(local_kernel, (levels, rank, base_bits,...  6.93 us
    pallas_call x1, Pallas kernels, body(): pl.pallas_call(functools.partial(final_kernel, chunk), grid=(steps,), out...  6.89 us
    unnamed x18, local copies, waits for them, and re-layouts  3.94 us
    pallas_call x1, Pallas kernels, body(): pl.pallas_call(functools.partial(end_kernel, (levels, rank), 1.0 / col_co...  2.73 us
  transfers between devices with their start and end apart: 9, of which 6 were waited for; matrix products, arithmetic and copies ran while one was open for 2% of the time, Pallas kernels for 15%

commit v1 on v0

--- a/solution.py
+++ b/solution.py
@@ -10,6 +10,7 @@
 
 HIGH = lax.Precision.HIGH
 F32 = jnp.float32
+MIB = 2**20
 
 
 def dot(a, b, dims=((1,), (0,))):
@@ -51,13 +52,33 @@
     return rank + pack_rows(levels - level, rank)
 
 
-def local_kernel(dims, rows_ref, x_ref, w_ref, u_ref, q_ref, node_ref, *refs):
+def masked(rows_ref, u_ref, chunk):
+    place = pl.program_id(0) * chunk + lax.broadcasted_iota(jnp.int32, (1, chunk), 1)
+    return jnp.where(place < rows_ref[0], u_ref[...], 0.0)
+
+
+def write_state(keep, send, acc, rank, blocks_of):
+    half = acc.shape[1] // 2
+    is_first = lax.axis_index("leaf") % 2 == 0
+    at = 0
+    for k in range(acc.shape[0] // rank):
+        low = acc[k * rank : (k + 1) * rank, :half]
+        high = acc[k * rank : (k + 1) * rank, half:]
+        keep[at : at + rank, :] = jnp.where(is_first, low, high)
+        send[at : at + rank, :] = jnp.where(is_first, high, low)
+        at += rank
+        for rows in pack(blocks_of(k)):
+            keep[at : at + rows.shape[0], :] = rows
+            send[at : at + rows.shape[0], :] = rows
+            at += rows.shape[0]
+
+
+def local_kernel(dims, rows_ref, x_ref, u_ref, q_ref, node_ref, keep, send, g_ref, nodes_out, c_acc, sems):
     levels, rank, base_bits, chunk = dims
-    solve_keep, solve_send, side_keep, side_send, nodes_out, c_acc, k_acc, g_acc, sems = refs
     step = pl.program_id(0)
-    position = lax.axis_index("leaf")
 
     def node_copy(k):
+        position = lax.axis_index("leaf")
         index = 2**levels - 2 ** (levels - k) + jnp.right_shift(position, base_bits + k + 1)
         return pltpu.make_async_copy(node_ref.at[index], nodes_out.at[k], sems.at[k])
 
@@ -66,40 +87,45 @@
         for k in range(levels):
             node_copy(k).start()
         c_acc[...] = jnp.zeros_like(c_acc)
-        k_acc[...] = jnp.zeros_like(k_acc)
-        g_acc[...] = jnp.zeros_like(g_acc)
-
-    place = step * chunk + lax.broadcasted_iota(jnp.int32, (1, chunk), 1)
-    u = jnp.where(place < rows_ref[0], u_ref[...], 0.0)
+        g_ref[...] = jnp.zeros_like(g_ref)
+
+    u = masked(rows_ref, u_ref, chunk)
     c_acc[...] += dot(u, x_ref[...])
-    k_acc[...] += dot(u, w_ref[...])
-    g_acc[...] += dot(u, q_ref[...], ((1,), (1,)))
+    g_ref[...] += dot(u, q_ref[...], ((1,), (1,)))
 
     @pl.when(step == pl.num_programs(0) - 1)
     def _():
-        half = c_acc.shape[1] // 2
-        is_first = position % 2 == 0
-
-        def block(i, j):
-            return g_acc[i * rank : (i + 1) * rank, j * rank : (j + 1) * rank]
-
-        def write(keep, send, acc, blocks_of):
-            at = 0
-            for k in range(levels):
-                low = acc[k * rank : (k + 1) * rank, :half]
-                high = acc[k * rank : (k + 1) * rank, half:]
-                keep[at : at + rank, :] = jnp.where(is_first, low, high)
-                send[at : at + rank, :] = jnp.where(is_first, high, low)
-                at += rank
-                for rows in pack(blocks_of(k)):
-                    keep[at : at + rows.shape[0], :] = rows
-                    send[at : at + rows.shape[0], :] = rows
-                    at += rows.shape[0]
-
-        write(solve_keep, solve_send, c_acc, lambda k: [block(i, k) for i in range(k + 1, levels)])
-        write(side_keep, side_send, k_acc, lambda k: [block(k, j) for j in range(k, levels)])
+        def blocks(k):
+            lane = slice(k * rank, (k + 1) * rank)
+            return [g_ref[i * rank : (i + 1) * rank, lane] for i in range(k + 1, levels)]
+
+        write_state(keep, send, c_acc, rank, blocks)
         for k in range(levels):
             node_copy(k).wait()
+
+
+def side_kernel(dims, rows_ref, w_ref, u_ref, g_ref, keep, send, k_acc):
+    levels, rank, chunk = dims
+    step = pl.program_id(0)
+
+    @pl.when(step == 0)
+    def _():
+        k_acc[...] = jnp.zeros_like(k_acc)
+
+    k_acc[...] += dot(masked(rows_ref, u_ref, chunk), w_ref[...])
+
+    @pl.when(step == pl.num_programs(0) - 1)
+    def _():
+        def blocks(k):
+            row = slice(k * rank, (k + 1) * rank)
+            return [g_ref[row, j * rank : (j + 1) * rank] for j in range(k, levels)]
+
+        write_state(keep, send, k_acc, rank, blocks)
+
+
+def side_sum_kernel(start, own_ref, sib_ref, after_ref, out_ref):
+    del after_ref
+    out_ref[...] = own_ref[start:, :] + sib_ref[start:, :]
 
 
 def level_kernel(dims, level, own_ref, sib_ref, nodes_ref, z_ref, *next_ref):
@@ -214,17 +240,32 @@
     n_solve = sum(solve_rows(k, levels, rank) for k in range(levels))
     n_side = sum(side_rows(k, levels, rank) for k in range(levels))
     order = 2 * rank
-    shapes = [(n_solve, half)] * 2 + [(n_side, half)] * 2 + [(levels, order, order)]
-    solve, solve_send, side, side_send, nodes = pl.pallas_call(
+    params = pltpu.CompilerParams(vmem_limit_bytes=24 * MIB)
+    hbm = [pltpu.with_memory_space_constraint(a, pltpu.HBM) for a in (right_side, u_all, q_all, node_inverse)]
+    shapes = [(n_solve, half)] * 2 + [(wide, wide), (levels, order, order)]
+    solve, solve_send, products, nodes = pl.pallas_call(
         functools.partial(local_kernel, (levels, rank, base_bits, chunk)),
         grid=(steps,),
         out_shape=[jax.ShapeDtypeStruct(s, F32) for s in shapes],
-        in_specs=[smem, by_row, by_row, by_lane, by_lane, pl.BlockSpec(memory_space=pl.ANY)],
+        in_specs=[smem, by_row, by_lane, by_lane, pl.BlockSpec(memory_space=pl.ANY)],
         out_specs=[fixed(*s) for s in shapes],
-        scratch_shapes=[pltpu.VMEM((wide, col_count), F32)] * 2
-        + [pltpu.VMEM((wide, wide), F32), pltpu.SemaphoreType.DMA((levels,))],
+        scratch_shapes=[pltpu.VMEM((wide, col_count), F32), pltpu.SemaphoreType.DMA((levels,))],
+        compiler_params=params,
         name="local_sums",
-    )(leaf_rows, right_side, cotangent, u_all, q_all, node_inverse)
+    )(leaf_rows, *hbm)
+    side, side_send = pl.pallas_call(
+        functools.partial(side_kernel, (levels, rank, chunk)),
+        grid=(steps,),
+        out_shape=[jax.ShapeDtypeStruct((n_side, half), F32)] * 2,
+        in_specs=[smem, by_row, by_lane, fixed(wide, wide)],
+        out_specs=[fixed(n_side, half)] * 2,
+        scratch_shapes=[pltpu.VMEM((wide, col_count), F32)],
+        compiler_params=params,
+        cost_estimate=pl.CostEstimate(
+            flops=6 * wide * row_count * col_count, bytes_accessed=8 * wide * row_count, transcendentals=0
+        ),
+        name="side_sums",
+    )(leaf_rows, cotangent, u_all, products)
 
     if base_bits == 0:
         sib_solve, sib_side = swapped(solve_send, 0), swapped(side_send, 0)
@@ -235,6 +276,7 @@
         sib_solve, sib_side = swapped(solve, base_bits), swapped(side, base_bits)
 
     vmem = pl.BlockSpec(memory_space=pltpu.VMEM)
+    small = pltpu.CompilerParams(vmem_limit_bytes=4 * MIB)
     first_solve, first_side = solve, side
     solves, sides, zs = [], [], []
     for k in range(levels):
@@ -251,12 +293,22 @@
             out_shape=out_shape,
             in_specs=[vmem] * 3,
             out_specs=[vmem] * len(out_shape),
+            compiler_params=small,
+            cost_estimate=pl.CostEstimate(flops=2 * 10**10, bytes_accessed=2 * MIB, transcendentals=0),
             name=f"level_{k}",
         )(solve, sib_solve, nodes)
         zs.append(outs[0])
         if rows:
             solve = outs[1]
-            side = (side + sib_side)[side_rows(k, levels, rank) :]
+            start = side_rows(k, levels, rank)
+            side = pl.pallas_call(
+                functools.partial(side_sum_kernel, start),
+                out_shape=jax.ShapeDtypeStruct((side.shape[0] - start, half), F32),
+                in_specs=[vmem] * 3,
+                out_specs=vmem,
+                compiler_params=small,
+                name=f"side_sum_{k}",
+            )(side, sib_side, outs[0])
 
     pair = base_bits == 0
     ends = [*solves, *sides, *zs] + ([first_solve, first_side] if pair else [])
@@ -265,6 +317,7 @@
         out_shape=[jax.ShapeDtypeStruct((3 * wide, half), F32)] * (2 if pair else 1),
         in_specs=[vmem] * len(ends),
         out_specs=[vmem] * (2 if pair else 1),
+        compiler_params=small,
         name="end_factors",
     )(*ends)
     other = swapped(send[0] if pair else own, 0)
@@ -279,6 +332,7 @@
         ],
         in_specs=[smem, fixed(3 * wide, half), fixed(3 * wide, half), by_row, by_row, by_lane],
         out_specs=[by_row, by_lane, by_lane],
+        compiler_params=params,
         name="row_outputs",
     )(leaf_rows, own, other, right_side, cotangent, q_all)
     return sol, left.reshape(coeff_basis.shape), right.reshape(coeff_basis.shape)

time: 54.2 us -> 37.8 us (0.70)
  Pallas kernels: 24.7 us -> 13.2 us
  local copies, waits for them, and re-layouts: 3.94 us -> 0.02 us
  starting transfers between devices: 11.7 us -> 13.8 us
  waiting for transfers between devices: 11.2 us -> 9.27 us
  other arithmetic: 1.08 us -> 0 us
    pallas_call x4, Pallas kernels: 8.13 us -> 1.29 us  [body(): pl.pallas_call(functools.partial(level_kernel, (levels, rank, base_bits),...]
    unnamed x18 -> x8, local copies, waits for them, and re-layouts: 3.94 us -> 0.02 us
    pallas_call x1, Pallas kernels: 2.73 us -> 0.28 us  [body(): pl.pallas_call(functools.partial(end_kernel, (levels, rank), 1.0 / col_co...]
    pallas_call x1, Pallas kernels: 6.89 us -> 4.65 us  [body(): pl.pallas_call(functools.partial(final_kernel, chunk), grid=(steps,), out...]
    ppermute x9, starting transfers between devices: 11.7 us -> 13.8 us  [swapped(): return lax.ppermute(value, 'leaf', pairs)]
    pallas_call x0 -> x4, Pallas kernels: none -> 1.92 us  [the longest x1 1.88 us: body(): pl.pallas_call(functools.partial(side_kernel, (levels, rank, chunk)), gri...]
    pallas_call x1, Pallas kernels: 6.93 us -> 5.05 us  [body(): pl.pallas_call(functools.partial(local_kernel, (levels, rank, base_bits,...]
    ppermute x9, waiting for transfers between devices: 11.2 us -> 9.27 us  [swapped(): return lax.ppermute(value, 'leaf', pairs)]
  transfers between devices with their start and end apart: 9 -> 9, of which waited for: 6 -> 5; matrix products, arithmetic and copies ran while one was open for 2% -> 0% of each run, Pallas kernels for 15% -> 9%
where the time goes in v1:
time: 37.8 us; the launch traced here: 37.6 us
  starting transfers between devices  13.8 us (37%)
  Pallas kernels  13.2 us (35%)
  waiting for transfers between devices  9.27 us (25%)
  between operations  1.37 us (4%)
    ppermute x9, starting transfers between devices, swapped(): return lax.ppermute(value, 'leaf', pairs)  13.8 us
    ppermute x9, waiting for transfers between devices, swapped(): return lax.ppermute(value, 'leaf', pairs)  9.27 us
    pallas_call x1, Pallas kernels, body(): pl.pallas_call(functools.partial(local_kernel, (levels, rank, base_bits,...  5.05 us
    pallas_call x1, Pallas kernels, body(): pl.pallas_call(functools.partial(final_kernel, chunk), grid=(steps,), out...  4.65 us
    pallas_call x1, Pallas kernels, body(): pl.pallas_call(functools.partial(side_kernel, (levels, rank, chunk)), gri...  1.88 us
    pallas_call x4, Pallas kernels, body(): pl.pallas_call(functools.partial(level_kernel, (levels, rank, base_bits),...  1.29 us
  transfers between devices with their start and end apart: 9, of which 5 were waited for; matrix products, arithmetic and copies ran while one was open for 0% of the time, Pallas kernels for 9%

profile of v1, /device:TPU:0, one launch (start us, length us, event | category | flops | bytes accessed | tf_op | source)
XLA Modules:
  0.0 37.6 jit_solution(2655773456184526077)
XLA Ops:
  1.3 0.0 copy-start.2
  1.3 0.0 copy-start.3
  1.3 5.0 %local_sums.1 = (f32[448,128]{1,0:T(8,128)S(1)}, f32[448,128]{1,0:T(8,128)S(1)}, f32[256,256]{1,0:T(8,128)S(1)}, f32[4,128,128]{2,1,0:T(8,128)S(1)}) custom-call(s32[1]{0:T(128)S(6)} %copy.9.rows_ref, f32[2048,256]{1,0:T(8,128)} %x_ref.3, f32[256,2048]{1,0:T(8,128)} %bitcast.6, f32[256,2048]{1,0:T(8,128)} %bitcast.4, f32[15,128,128]{2,1,0:T(8,128)} %node_ref.1), custom_call_target="tpu_custom_call" | custom-call | tf_op jit(solution)/shard_map/local_sums/pallas_call | solution.py:246
  6.4 0.5 %collective-permute-start = (f32[448,128]{1,0:T(8,128)S(1)}, f32[448,128]{1,0:T(8,128)S(1)}, u32[]{:S(2)}, u32[]{:S(2)}) collective-permute-start(f32[448,128]{1,0:T(8,128)S(1)} %get-tuple-element.20), channel_id=1, source_target_pairs={{0,1},{1,0},{2,3},{3,2},{4,5},{5,4},{6,7},{7,6},{8,9},{9,8},{10,11... | collective-permute-start | bytes 688136 | tf_op jit(solution)/shard_map/ppermute | solution.py:219
  6.9 0.0 copy-done.2
  6.9 0.0 copy-done.3
  6.9 1.9 %side_sums.1 = (f32[576,128]{1,0:T(8,128)S(1)}, f32[576,128]{1,0:T(8,128)S(1)}) custom-call(s32[1]{0:T(128)S(6)} %copy.9.rows_ref, f32[2048,256]{1,0:T(8,128)S(1)} %copy-done.3, f32[256,2048]{1,0:T(8,128)S(1)} %bitcast.7, f32[256,256]{1,0:T(8,128)S(1)} %get-tuple-element.26.g_ref), custom_call_target="tpu_custom_call" | custom-call | flops 805306368 | bytes 4194304 | tf_op jit(solution)/shard_map/side_sums/pallas_call | solution.py:256
  8.8 0.1 collective-permute-start.4
  8.9 0.0 collective-permute-done.sib_ref.refs_0_
  8.9 0.4 %level_0.1 = (f32[128,128]{1,0:T(8,128)S(1)}, f32[288,128]{1,0:T(8,128)S(1)}) custom-call(f32[448,128]{1,0:T(8,128)S(1)} %get-tuple-element.21.own_ref.refs_12_, f32[448,128]{1,0:T(8,128)S(1)} %collective-permute-done.sib_ref.refs_0_, f32[4,128,128]{2,1,0:T(8,128)S(1)} %get-tuple-element.22.nodes_ref), custom_call_target="tpu_custom_call" | custom-call | flops 20000000000 | bytes 2097152 | tf_op jit(solution)/shard_map/level_0/pallas_call | solution.py:291
  9.3 3.0 %collective-permute-start.1 = (f32[288,128]{1,0:T(8,128)S(1)}, f32[288,128]{1,0:T(8,128)S(1)}, u32[]{:S(2)}, u32[]{:S(2)}) collective-permute-start(f32[288,128]{1,0:T(8,128)S(1)} %get-tuple-element.23.own_ref), channel_id=1, source_target_pairs={{0,2},{1,3},{2,0},{3,1},{4,6},{5,7},{6,4},{7,5},{8,10},{9,11},{10,... | collective-permute-start | bytes 442376 | tf_op jit(solution)/shard_map/ppermute | solution.py:219
  12.3 0.0 collective-permute-done.4.sib_ref.refs_4_
  12.3 0.8 %collective-permute-start.5 = (f32[384,128]{1,0:T(8,128)S(1)}, f32[384,128]{1,0:T(8,128)S(1)}, u32[]{:S(2)}, u32[]{:S(2)}) collective-permute-start(f32[384,128]{1,0:T(8,128)S(1)} %side_sum_0.1.own_ref), channel_id=1, source_target_pairs={{0,2},{1,3},{2,0},{3,1},{4,6},{5,7},{6,4},{7,5},{8,10},{9,11},{10,... | collective-permute-start | bytes 589832 | tf_op jit(solution)/shard_map/ppermute | solution.py:219
  13.2 3.8 %collective-permute-done.1.sib_ref.refs_1_ = f32[288,128]{1,0:T(8,128)S(1)} collective-permute-done((f32[288,128]{1,0:T(8,128)S(1)}, f32[288,128]{1,0:T(8,128)S(1)}, u32[]{:S(2)}, u32[]{:S(2)}) %collective-permute-start.1) | collective-permute-done | bytes 147488 | tf_op jit(solution)/shard_map/ppermute | solution.py:219
  17.0 0.4 level_1.1
  17.4 2.2 %collective-permute-start.2 = (f32[160,128]{1,0:T(8,128)S(1)}, f32[160,128]{1,0:T(8,128)S(1)}, u32[]{:S(2)}, u32[]{:S(2)}) collective-permute-start(f32[160,128]{1,0:T(8,128)S(1)} %get-tuple-element.24.own_ref), channel_id=1, source_target_pairs={{0,4},{1,5},{2,6},{3,7},{4,0},{5,1},{6,2},{7,3},{8,12},{9,13},{10,... | collective-permute-start | bytes 245768 | tf_op jit(solution)/shard_map/ppermute | solution.py:219
  19.5 1.1 %collective-permute-done.5.sib_ref.refs_5_ = f32[384,128]{1,0:T(8,128)S(1)} collective-permute-done((f32[384,128]{1,0:T(8,128)S(1)}, f32[384,128]{1,0:T(8,128)S(1)}, u32[]{:S(2)}, u32[]{:S(2)}) %collective-permute-start.5) | collective-permute-done | bytes 196640 | tf_op jit(solution)/shard_map/ppermute | solution.py:219
  20.6 1.9 %collective-permute-start.6 = (f32[224,128]{1,0:T(8,128)S(1)}, f32[224,128]{1,0:T(8,128)S(1)}, u32[]{:S(2)}, u32[]{:S(2)}) collective-permute-start(f32[224,128]{1,0:T(8,128)S(1)} %side_sum_1.1.own_ref), channel_id=1, source_target_pairs={{0,4},{1,5},{2,6},{3,7},{4,0},{5,1},{6,2},{7,3},{8,12},{9,13},{10,... | collective-permute-start | bytes 344072 | tf_op jit(solution)/shard_map/ppermute | solution.py:219
  22.5 0.0 collective-permute-done.2.sib_ref.refs_2_
  22.5 0.4 level_2.1
  22.8 2.6 %collective-permute-start.3 = (f32[64,128]{1,0:T(8,128)S(1)}, f32[64,128]{1,0:T(8,128)S(1)}, u32[]{:S(2)}, u32[]{:S(2)}) collective-permute-start(f32[64,128]{1,0:T(8,128)S(1)} %get-tuple-element.25.own_ref), channel_id=1, source_target_pairs={{0,8},{1,9},{2,10},{3,11},{4,12},{5,13},{6,14},{7,15},{8,0},{9,1},... | collective-permute-start | bytes 98312 | tf_op jit(solution)/shard_map/ppermute | solution.py:219
  25.5 0.4 collective-permute-done.6.sib_ref.refs_6_
  25.8 2.5 %collective-permute-start.7 = (f32[96,128]{1,0:T(8,128)S(1)}, f32[96,128]{1,0:T(8,128)S(1)}, u32[]{:S(2)}, u32[]{:S(2)}) collective-permute-start(f32[96,128]{1,0:T(8,128)S(1)} %side_sum_2.1), channel_id=1, source_target_pairs={{0,8},{1,9},{2,10},{3,11},{4,12},{5,13},{6,14},{7,15},{8,0},{9,1},... | collective-permute-start | bytes 147464 | tf_op jit(solution)/shard_map/ppermute | solution.py:219
  28.3 0.0 collective-permute-done.3.sib_ref.refs_3_
  28.4 0.0 copy-start
  28.4 0.0 copy-start.1
  28.4 0.2 level_3.1.refs_11_
  28.5 2.3 %collective-permute-done.7.refs_7_ = f32[96,128]{1,0:T(8,128)S(1)} collective-permute-done((f32[96,128]{1,0:T(8,128)S(1)}, f32[96,128]{1,0:T(8,128)S(1)}, u32[]{:S(2)}, u32[]{:S(2)}) %collective-permute-start.7) | collective-permute-done | bytes 49184 | tf_op jit(solution)/shard_map/ppermute | solution.py:219
  30.9 0.3 end_factors.1
  31.2 0.1 collective-permute-start.8
  31.2 1.7 %collective-permute-done.8.other_ref = f32[768,128]{1,0:T(8,128)S(1)} collective-permute-done((f32[768,128]{1,0:T(8,128)S(1)}, f32[768,128]{1,0:T(8,128)S(1)}, u32[]{:S(2)}, u32[]{:S(2)}) %collective-permute-start.8) | collective-permute-done | bytes 393248 | tf_op jit(solution)/shard_map/ppermute | solution.py:219
  33.0 0.0 copy-done
  33.0 0.0 copy-done.1
  33.0 4.6 %row_outputs.1 = (f32[2048,256]{1,0:T(8,128)}, bf16[256,2048]{1,0:T(8,128)(2,1)}, bf16[256,2048]{1,0:T(8,128)(2,1)}) custom-call(s32[1]{0:T(128)S(6)} %copy.9.rows_ref, f32[768,128]{1,0:T(8,128)S(1)} %get-tuple-element.32.own_ref, f32[768,128]{1,0:T(8,128)S(1)} %collective-permute-done.8.other_ref, f32[2048,256]{1,0:T(8,128)S(1)} %copy-done, ...), custom_call_target="tpu_custom_call" | custom-call | tf_op jit(solution)/shard_map/row_outputs/pallas_call | solution.py:325
  (3 shorter events, 0.0 us)
Async XLA Ops:
  1.3 5.6 %copy-start.2 = (f32[4,64,2048]{2,1,0:T(8,128)S(1)}, f32[4,64,2048]{2,1,0:T(8,128)}, u32[]{:S(2)}) copy-start(f32[4,64,2048]{2,1,0:T(8,128)} %param.8) | copy-start | bytes 6291460
  1.3 5.6 %copy-start.3 = (f32[2048,256]{1,0:T(8,128)S(1)}, f32[2048,256]{1,0:T(8,128)}, u32[]{:S(2)}) copy-start(f32[2048,256]{1,0:T(8,128)} %w_ref.3) | copy-start | bytes 6291460
  6.4 2.5 %collective-permute-start = (f32[448,128]{1,0:T(8,128)S(1)}, f32[448,128]{1,0:T(8,128)S(1)}, u32[]{:S(2)}, u32[]{:S(2)}) collective-permute-start(f32[448,128]{1,0:T(8,128)S(1)} %get-tuple-element.20), channel_id=1, source_target_pairs={{0,1},{1,0},{2,3},{3,2},{4,5},{5,4},{6,7},{7,6},{8,9},{9,8},{10,11... | collective-permute-start | bytes 688136 | tf_op jit(solution)/shard_map/ppermute | solution.py:219
  8.8 3.6 %collective-permute-start.4 = (f32[576,128]{1,0:T(8,128)S(1)}, f32[576,128]{1,0:T(8,128)S(1)}, u32[]{:S(2)}, u32[]{:S(2)}) collective-permute-start(f32[576,128]{1,0:T(8,128)S(1)} %get-tuple-element.27), channel_id=1, source_target_pairs={{0,1},{1,0},{2,3},{3,2},{4,5},{5,4},{6,7},{7,6},{8,9},{9,8},{10,11... | collective-permute-start | bytes 884744 | tf_op jit(solution)/shard_map/ppermute | solution.py:219
  9.3 7.7 %collective-permute-start.1 = (f32[288,128]{1,0:T(8,128)S(1)}, f32[288,128]{1,0:T(8,128)S(1)}, u32[]{:S(2)}, u32[]{:S(2)}) collective-permute-start(f32[288,128]{1,0:T(8,128)S(1)} %get-tuple-element.23.own_ref), channel_id=1, source_target_pairs={{0,2},{1,3},{2,0},{3,1},{4,6},{5,7},{6,4},{7,5},{8,10},{9,11},{10,... | collective-permute-start | bytes 442376 | tf_op jit(solution)/shard_map/ppermute | solution.py:219
  12.3 8.2 %collective-permute-start.5 = (f32[384,128]{1,0:T(8,128)S(1)}, f32[384,128]{1,0:T(8,128)S(1)}, u32[]{:S(2)}, u32[]{:S(2)}) collective-permute-start(f32[384,128]{1,0:T(8,128)S(1)} %side_sum_0.1.own_ref), channel_id=1, source_target_pairs={{0,2},{1,3},{2,0},{3,1},{4,6},{5,7},{6,4},{7,5},{8,10},{9,11},{10,... | collective-permute-start | bytes 589832 | tf_op jit(solution)/shard_map/ppermute | solution.py:219
  17.4 5.1 %collective-permute-start.2 = (f32[160,128]{1,0:T(8,128)S(1)}, f32[160,128]{1,0:T(8,128)S(1)}, u32[]{:S(2)}, u32[]{:S(2)}) collective-permute-start(f32[160,128]{1,0:T(8,128)S(1)} %get-tuple-element.24.own_ref), channel_id=1, source_target_pairs={{0,4},{1,5},{2,6},{3,7},{4,0},{5,1},{6,2},{7,3},{8,12},{9,13},{10,... | collective-permute-start | bytes 245768 | tf_op jit(solution)/shard_map/ppermute | solution.py:219
  20.6 5.2 %collective-permute-start.6 = (f32[224,128]{1,0:T(8,128)S(1)}, f32[224,128]{1,0:T(8,128)S(1)}, u32[]{:S(2)}, u32[]{:S(2)}) collective-permute-start(f32[224,128]{1,0:T(8,128)S(1)} %side_sum_1.1.own_ref), channel_id=1, source_target_pairs={{0,4},{1,5},{2,6},{3,7},{4,0},{5,1},{6,2},{7,3},{8,12},{9,13},{10,... | collective-permute-start | bytes 344072 | tf_op jit(solution)/shard_map/ppermute | solution.py:219
  22.8 5.5 %collective-permute-start.3 = (f32[64,128]{1,0:T(8,128)S(1)}, f32[64,128]{1,0:T(8,128)S(1)}, u32[]{:S(2)}, u32[]{:S(2)}) collective-permute-start(f32[64,128]{1,0:T(8,128)S(1)} %get-tuple-element.25.own_ref), channel_id=1, source_target_pairs={{0,8},{1,9},{2,10},{3,11},{4,12},{5,13},{6,14},{7,15},{8,0},{9,1},... | collective-permute-start | bytes 98312 | tf_op jit(solution)/shard_map/ppermute | solution.py:219
  25.8 5.0 %collective-permute-start.7 = (f32[96,128]{1,0:T(8,128)S(1)}, f32[96,128]{1,0:T(8,128)S(1)}, u32[]{:S(2)}, u32[]{:S(2)}) collective-permute-start(f32[96,128]{1,0:T(8,128)S(1)} %side_sum_2.1), channel_id=1, source_target_pairs={{0,8},{1,9},{2,10},{3,11},{4,12},{5,13},{6,14},{7,15},{8,0},{9,1},... | collective-permute-start | bytes 147464 | tf_op jit(solution)/shard_map/ppermute | solution.py:219
  28.4 4.6 %copy-start = (f32[2048,256]{1,0:T(8,128)S(1)}, f32[2048,256]{1,0:T(8,128)}, u32[]{:S(2)}) copy-start(f32[2048,256]{1,0:T(8,128)} %x_ref.3) | copy-start | bytes 6291460
  28.4 4.6 %copy-start.1 = (f32[4,64,2048]{2,1,0:T(8,128)S(1)}, f32[4,64,2048]{2,1,0:T(8,128)}, u32[]{:S(2)}) copy-start(f32[4,64,2048]{2,1,0:T(8,128)} %param.9) | copy-start | bytes 6291460
  31.2 1.8 %collective-permute-start.8 = (f32[768,128]{1,0:T(8,128)S(1)}, f32[768,128]{1,0:T(8,128)S(1)}, u32[]{:S(2)}, u32[]{:S(2)}) collective-permute-start(f32[768,128]{1,0:T(8,128)S(1)} %get-tuple-element.33), channel_id=1, source_target_pairs={{0,1},{1,0},{2,3},{3,2},{4,5},{5,4},{6,7},{7,6},{8,9},{9,8},{10,11... | collective-permute-start | bytes 1179656 | tf_op jit(solution)/shard_map/ppermute | solution.py:219

commit v2 on v0

v2 whole, which is shorter than its diff:
```python
import functools

import jax
import jax.numpy as jnp
from jax import lax
from jax.experimental import pallas as pl
from jax.experimental.pallas import tpu as pltpu
from jax.sharding import PartitionSpec as P


HIGH = lax.Precision.HIGH
F32 = jnp.float32
MIB = 2**20


def dot(a, b, dims=((1,), (0,))):
    return lax.dot_general(a, b, (dims, ((), ())), precision=HIGH, preferred_element_type=F32)


def pack(blocks):
    rows = []
    for i in range(0, len(blocks) - 1, 2):
        rows.append(jnp.concatenate([blocks[i], blocks[i + 1]], 1))
    if len(blocks) % 2:
        half = blocks[-1].shape[0] // 2
        rows.append(jnp.concatenate([blocks[-1][:half], blocks[-1][half:]], 1))
    return rows


def pack_rows(count, rank):
    return count // 2 * rank + count % 2 * (rank // 2)


def unpack(ref, start, count, rank):
    blocks = []
    for i in range(count):
        if i == count - 1 and count % 2:
            half = ref[start : start + rank // 2, :]
            blocks.append(jnp.concatenate([half[:, :rank], half[:, rank:]], 0))
        else:
            lane = i % 2 * rank
            blocks.append(ref[start : start + rank, lane : lane + rank])
            start += i % 2 * rank
    return blocks


def side_rows(level, levels, rank):
    return rank + pack_rows(levels - level, rank)


def solve_rows(level, levels, rank):
    return rank + pack_rows(levels - 1 - level, rank)


def write_state(keep, send, acc, rank, blocks_of):
    half = acc.shape[1] // 2
    is_first = lax.axis_index("leaf") % 2 == 0
    at = 0
    for k in range(acc.shape[0] // rank):
        low = acc[k * rank : (k + 1) * rank, :half]
        high = acc[k * rank : (k + 1) * rank, half:]
        keep[at : at + rank, :] = jnp.where(is_first, low, high)
        send[at : at + rank, :] = jnp.where(is_first, high, low)
        at += rank
        for rows in pack(blocks_of(k)):
            keep[at : at + rows.shape[0], :] = rows
            send[at : at + rows.shape[0], :] = rows
            at += rows.shape[0]


def local_kernel(dims, rows_hbm, x_hbm, w_hbm, u_hbm, q_hbm, node_ref, *refs):
    levels, rank, base_bits, chunk, ahead = dims
    keep, send, g_ref, nodes_out, count_out, x_all, w_all, u_all, q_all = refs[:9]
    rows_ref, c_acc, sems, w_sem, row_sem, node_sems = refs[9:]
    position = lax.axis_index("leaf")
    steps = x_all.shape[0] // chunk

    def copies(i):
        part = pl.ds(pl.multiple_of(i * chunk, chunk), chunk)
        pairs = [(u_hbm.at[:, part], u_all.at[:, part]), (x_hbm.at[part], x_all.at[part])]
        pairs.append((q_hbm.at[:, part], q_all.at[:, part]))
        return [pltpu.make_async_copy(a, b, sems.at[i, n]) for n, (a, b) in enumerate(pairs)]

    def node_copy(k):
        index = 2**levels - 2 ** (levels - k) + jnp.right_shift(position, base_bits + k + 1)
        return pltpu.make_async_copy(node_ref.at[index], nodes_out.at[k], node_sems.at[k])

    row_copy = pltpu.make_async_copy(rows_hbm, rows_ref, row_sem)
    w_copy = pltpu.make_async_copy(w_hbm, w_all, w_sem)
    row_copy.start()
    for i in range(min(ahead, steps)):
        for copy in copies(i):
            copy.start()
    for k in range(levels):
        node_copy(k).start()
    c_acc[...] = jnp.zeros_like(c_acc)
    g_ref[...] = jnp.zeros_like(g_ref)
    row_copy.wait()
    count_out[...] = jnp.full(count_out.shape, rows_ref[0], jnp.int32)

    def step(i, carry):
        @pl.when(i + ahead < steps)
        def _():
            for copy in copies(i + ahead):
                copy.start()

        @pl.when(i + ahead == max(steps, ahead))
        def _():
            w_copy.start()

        for copy in copies(i):
            copy.wait()
        part = pl.ds(pl.multiple_of(i * chunk, chunk), chunk)
        place = i * chunk + lax.broadcasted_iota(jnp.int32, (1, chunk), 1)
        u = jnp.where(place < rows_ref[0], u_all[:, part], 0.0)
        c_acc[...] += dot(u, x_all[part, :])
        g_ref[...] += dot(u, q_all[:, part], ((1,), (1,)))
        return carry

    lax.fori_loop(0, steps, step, 0)

    def blocks(k):
        lane = slice(k * rank, (k + 1) * rank)
        return [g_ref[i * rank : (i + 1) * rank, lane] for i in range(k + 1, levels)]

    write_state(keep, send, c_acc, rank, blocks)
    for k in range(levels):
        node_copy(k).wait()
    w_copy.wait()


def side_kernel(dims, count_ref, w_ref, u_ref, g_ref, keep, send, k_acc):
    levels, rank = dims
    place = lax.broadcasted_iota(jnp.int32, (1, u_ref.shape[1]), 1)
    u = jnp.where(place < count_ref[:1, :1], u_ref[...], 0.0)
    k_acc[...] = dot(u, w_ref[...])

    def blocks(k):
        row = slice(k * rank, (k + 1) * rank)
        return [g_ref[row, j * rank : (j + 1) * rank] for j in range(k, levels)]

    write_state(keep, send, k_acc, rank, blocks)


def side_first_kernel(at, own_ref, sib_ref, after_ref, *out_refs):
    del after_ref
    for out_ref in out_refs:
        rows = out_ref.shape[0]
        out_ref[...] = own_ref[at : at + rows, :] + sib_ref[at : at + rows, :]
        at += rows


def side_join_kernel(first, fresh_ref, sent_ref, got_ref, after_ref, out_ref):
    del after_ref
    rows = fresh_ref.shape[0]
    out_ref[:rows, :] = fresh_ref[...]
    out_ref[rows : rows + first, :] = got_ref[:first, :]
    out_ref[rows + first :, :] = sent_ref[first:, :] + got_ref[first:, :]


def side_top_kernel(sent_ref, got_ref, after_ref, out_ref):
    del after_ref
    at = sent_ref.shape[0] - out_ref.shape[0]
    out_ref[...] = sent_ref[at:, :] + got_ref[at:, :]


def level_kernel(dims, level, own_ref, sib_ref, nodes_ref, *refs):
    levels, rank, base_bits, placed = dims
    z_ref, *out_refs = refs[1:] if placed else refs
    is_lower = jnp.right_shift(lax.axis_index("leaf"), base_bits + level) % 2 == 0
    own, sib = own_ref[:rank, :], sib_ref[:rank, :]
    both = jnp.concatenate([jnp.where(is_lower, own, sib), jnp.where(is_lower, sib, own)], 0)
    mixed = dot(nodes_ref[level], both)
    z_own = jnp.where(is_lower, mixed[:rank], mixed[rank:])
    z_sib = jnp.where(is_lower, mixed[rank:], mixed[:rank])
    z_ref[:rank, :] = z_own
    z_ref[rank:, :] = z_sib
    if not out_refs:
        return
    (out_ref,) = out_refs
    count = levels - 1 - level
    h_own = unpack(own_ref, rank, count, rank)
    h_sib = unpack(sib_ref, rank, count, rank)
    h_both = jnp.concatenate([jnp.concatenate(h_own, 0), jnp.concatenate(h_sib, 0)], 1)
    drop = dot(h_both, jnp.concatenate([z_own, z_sib], 0))

    def total(at, rows):
        return own_ref[at : at + rows, :] + sib_ref[at : at + rows, :]

    start = solve_rows(level, levels, rank)
    at = 0
    for i in range(count):
        out_ref[at : at + rank, :] = total(start + at, rank) - drop[i * rank : (i + 1) * rank]
        at += rank
        rest = solve_rows(level + 1 + i, levels, rank) - rank
        if rest:
            out_ref[at : at + rest, :] = total(start + at, rest)
            at += rest


def factor_terms(dims, k, c, side_ref, at, z_here, z_above):
    levels, rank, scale = dims
    blocks = unpack(side_ref, at + rank, levels - k, rank)
    z_here = jnp.concatenate([z_here, *z_above], 0)
    l_term = c - dot(jnp.concatenate(blocks, 1), z_here)
    return l_term * scale, side_ref[at : at + rank, :] * scale


def end_low_kernel(dims, pair, *refs):
    levels, rank, scale = dims
    z_refs, (sib_side, side_sent, side_got, own_side) = refs[:levels], refs[levels : levels + 4]
    out_refs = refs[levels + 4 :]
    for n, out_ref in enumerate(out_refs):
        crossed = pair and n == 0
        at = 0
        for k in range(levels):
            z = z_refs[k][rank:, :] if crossed and k == 0 else z_refs[k][:rank, :]
            out_ref[k * rank : (k + 1) * rank, :] = z
            if k == levels - 1:
                continue
            if k == 0:
                term = (own_side if crossed else sib_side)[:rank, :]
            else:
                term = side_got[at : at + rank, :]
                if k > 1:
                    term = term + side_sent[at : at + rank, :]
                at += side_rows(k, levels, rank)
            out_ref[(levels + k) * rank : (levels + k + 1) * rank, :] = term * scale


def end_kernel(dims, pair, *refs):
    levels, rank, _ = dims
    solves, z_refs = refs[:levels], refs[levels : 2 * levels]
    sib_side, side_sent, side_got, top_side, own_solve, own_side = refs[2 * levels : 2 * levels + 6]
    *out_refs, side_sum = refs[2 * levels + 6 :]
    z_own = [z_ref[:rank, :] for z_ref in z_refs]

    low = side_rows(1, levels, rank)
    rows = side_sum.shape[0]
    side_sum[:low, :] = side_got[:low, :]
    side_sum[low:, :] = side_got[low:rows, :] + side_sent[low:rows, :]
    at = 0
    for k in range(levels):
        where = (side_sum, at)
        if k == 0:
            where = (sib_side, 0)
        elif k == levels - 1:
            where = (top_side, 0)
        else:
            at += side_rows(k, levels, rank)
        l_term, k_term = factor_terms(dims, k, solves[k][:rank, :], *where, z_refs[k][rank:, :], z_own[k + 1 :])
        out_refs[-1][k * rank : (k + 1) * rank, :] = l_term
        if pair:
            if k == 0:
                l_term, _ = factor_terms(dims, 0, own_solve[:rank, :], own_side, 0, z_own[0], z_own[1:])
            out_refs[0][k * rank : (k + 1) * rank, :] = l_term
    for out_ref in out_refs:
        out_ref[levels * rank :, :] = k_term


def whole(own_ref, other_ref, start, rows):
    is_first = lax.axis_index("leaf") % 2 == 0
    own, other = own_ref[start : start + rows, :], other_ref[start : start + rows, :]
    return jnp.concatenate([jnp.where(is_first, own, other), jnp.where(is_first, other, own)], 1)


class Sender:
    def __init__(self, sems):
        self.sems, self.copies = sems, []

    def send(self, source, target):
        copy = pltpu.make_async_copy(source, target, self.sems.at[len(self.copies)])
        copy.start()
        self.copies.append(copy)

    def wait(self):
        for copy in self.copies:
            copy.wait()


def solution_kernel(dims, count_ref, own_ref, other_ref, x_ref, q_ref, sol):
    wide, chunk = dims
    z = whole(own_ref, other_ref, 0, wide)
    for i in range(x_ref.shape[0] // chunk):
        part = slice(i * chunk, (i + 1) * chunk)
        live = i * chunk + lax.broadcasted_iota(jnp.int32, (chunk, 1), 0) < count_ref[:1, :1]
        x = x_ref[part, :] - dot(q_ref[:, part], z, ((0,), (0,)))
        sol[part, :] = jnp.where(live, x, 0.0)


def factor_kernel(dims, count_ref, low_own, low_other, top_own, top_other, x_ref, w_ref, *refs):
    wide, chunk = dims
    sol_out, left_out, right_out, left, right, sems = refs
    sender = Sender(sems)
    sender.send(x_ref, sol_out)
    low = low_own.shape[0] - wide
    l = whole(top_own, top_other, 0, wide)
    k = jnp.concatenate([whole(low_own, low_other, wide, low), whole(top_own, top_other, wide, wide - low)], 0)
    for i in range(x_ref.shape[0] // chunk):
        part, place = slice(i * chunk, (i + 1) * chunk), pl.ds(i * chunk, chunk)
        live = i * chunk + lax.broadcasted_iota(jnp.int32, (1, chunk), 1) < count_ref[:1, :1]
        left_now = dot(l, w_ref[part, :], ((1,), (1,)))
        left[:, part] = jnp.where(live, left_now, 0.0).astype(left.dtype)
        sender.send(left.at[:, place], left_out.at[:, place])
        right[:, part] = dot(k, x_ref[part, :], ((1,), (1,))).astype(right.dtype)
        sender.send(right.at[:, place], right_out.at[:, place])
    sender.wait()


def swapped(value, bit):
    mask = 2**bit
    pairs = [(source, source ^ mask) for source in range(lax.axis_size("leaf"))]
    return lax.ppermute(value, "leaf", pairs)


def shape(*sizes, dtype=F32):
    return jax.ShapeDtypeStruct(sizes, dtype)


def body(right_side, cotangent, coeff_basis, saved_basis, node_inverse, leaf_rows):
    row_count, col_count = right_side.shape
    levels, rank = coeff_basis.shape[:2]
    wide, order, half = levels * rank, 2 * rank, col_count // 2
    low, top = wide - rank, levels - 1
    base_bits = lax.axis_size("leaf").bit_length() - 1 - levels
    pair = base_bits == 0
    chunk = min(512, row_count)
    steps = row_count // chunk
    u_all = coeff_basis.reshape(wide, row_count)
    q_all = saved_basis.reshape(wide, row_count)

    vmem = pl.BlockSpec(memory_space=pltpu.VMEM)
    anywhere = pl.BlockSpec(memory_space=pl.ANY)
    small = pltpu.CompilerParams(vmem_limit_bytes=4 * MIB)
    large = pltpu.CompilerParams(vmem_limit_bytes=20 * MIB)

    def call(kernel, name, out_shape, *operands, out_specs=vmem, scratch=(), params=small, cost=None, **options):
        if isinstance(out_shape, list) and out_specs is vmem:
            out_specs = [vmem] * len(out_shape)
        if cost is not None:
            options["cost_estimate"] = pl.CostEstimate(flops=cost, bytes_accessed=MIB, transcendentals=0)
        return pl.pallas_call(
            kernel,
            out_shape=out_shape,
            in_specs=[vmem] * len(operands),
            out_specs=out_specs,
            scratch_shapes=list(scratch),
            compiler_params=params,
            name=name,
            **options,
        )(*operands)

    n_solve = sum(solve_rows(k, levels, rank) for k in range(levels))
    n_side = [side_rows(k, levels, rank) for k in range(levels)]
    arrays = (right_side, cotangent, u_all, q_all)
    outs = [shape(n_solve, half), shape(n_solve, half), shape(wide, wide), shape(levels, order, order)]
    outs += [shape(8, 128, dtype=jnp.int32)] + [shape(*a.shape) for a in arrays]
    hbm = [pltpu.with_memory_space_constraint(a, pltpu.HBM) for a in (*arrays, node_inverse)]
    solve, solve_send, products, nodes, count, x_vmem, w_vmem, u_vmem, q_vmem = pl.pallas_call(
        functools.partial(local_kernel, (levels, rank, base_bits, chunk, 2)),
        out_shape=outs,
        in_specs=[anywhere] * 6,
        out_specs=[vmem] * 9,
        scratch_shapes=[
            pltpu.SMEM((1,), jnp.int32),
            pltpu.VMEM((wide, col_count), F32),
            pltpu.SemaphoreType.DMA((steps, 3)),
            pltpu.SemaphoreType.DMA,
            pltpu.SemaphoreType.DMA,
            pltpu.SemaphoreType.DMA((levels,)),
        ],
        compiler_params=large,
        name="local_sums",
    )(leaf_rows, *hbm)
    side, side_send = call(
        functools.partial(side_kernel, (levels, rank)),
        "side_sums",
        [shape(sum(n_side), half)] * 2,
        count,
        w_vmem,
        u_vmem,
        products,
        scratch=[pltpu.VMEM((wide, col_count), F32)],
        params=large,
        cost=6 * wide * row_count * col_count,
    )

    if pair:
        sib_solve, sib_side = swapped(solve_send, 0), swapped(side_send, 0)
    else:
        solve, side = solve + swapped(solve_send, 0), side + swapped(side_send, 0)
        for bit in range(1, base_bits):
            solve, side = solve + swapped(solve, bit), side + swapped(side, bit)
        sib_solve, sib_side = swapped(solve, base_bits), swapped(side, base_bits)

    own_solve = solve
    solves, zs, fresh, placed = [], [], {}, []
    sent = got = None
    for k in range(levels):
        if k > 0:
            sib_solve = swapped(solve, base_bits + k)
        solves.append(sib_solve)
        out_shape = [shape(order, half)]
        if k < top:
            out_shape.append(shape(sum(solve_rows(i, levels, rank) for i in range(k + 1, levels)), half))
        outs = call(
            functools.partial(level_kernel, (levels, rank, base_bits, len(placed) > 0), k),
            f"level_{k}",
            out_shape,
            solve,
            sib_solve,
            nodes,
            *placed,
            cost=2 * 10**10,
        )
        zs.append(outs[0])
        if k < top:
            solve = outs[1]
        if k == 0:
            sizes = [*n_side[1 : top - 1], n_side[top - 1] + n_side[top]]
            first = call(
                functools.partial(side_first_kernel, n_side[0]),
                "side_first",
                [shape(size, half) for size in sizes],
                side,
                sib_side,
                outs[0],
            )
            fresh = dict(enumerate(first, 1))
            sent = fresh[top - 1]
            got = swapped(sent, base_bits + top - 1)
        elif k < top - 1:
            bit = top - 1 - k
            sent = call(
                functools.partial(side_join_kernel, n_side[bit + 1]),
                f"side_join_{bit}",
                shape(fresh[bit].shape[0] + sent.shape[0], half),
                fresh[bit],
                sent,
                got,
                outs[0],
            )
            got = swapped(sent, base_bits + bit)
            placed = [sent]
        elif k == top - 1:
            last = call(side_top_kernel, "side_top", shape(n_side[top], half), sent, got, outs[0])
            placed = [last]
    top_side = swapped(last, base_bits + top)

    dims = (levels, rank, 1.0 / col_count**0.5)
    copies = 2 if pair else 1
    *low_other, low_own = call(
        functools.partial(end_low_kernel, dims, pair),
        "end_low",
        [shape(wide + low, half)] * copies,
        *zs,
        sib_side,
        sent,
        got,
        side,
    )
    low_other = swapped(low_other[0] if pair else low_own, 0)
    *top_other, top_own = call(
        functools.partial(end_kernel, dims, pair),
        "end_factors",
        [shape(wide + rank, half)] * copies,
        *solves,
        *zs,
        sib_side,
        sent,
        got,
        top_side,
        own_solve,
        side,
        scratch=[pltpu.VMEM((sum(n_side[1:top]), half), F32)],
        cost=2 * 10**10,
    )
    top_other = swapped(top_other[0] if pair else top_own, 0)

    sol_vmem = call(
        functools.partial(solution_kernel, (wide, chunk)),
        "solution_rows",
        shape(row_count, col_count),
        count,
        low_own,
        low_other,
        x_vmem,
        q_vmem,
        params=large,
        cost=2 * 10**9,
    )
    grad = shape(wide, row_count, dtype=jnp.bfloat16)
    sol, left, right = call(
        functools.partial(factor_kernel, (wide, chunk)),
        "factor_rows",
        [shape(row_count, col_count), grad, grad],
        count,
        low_own,
        low_other,
        top_own,
        top_other,
        sol_vmem,
        w_vmem,
        out_specs=[anywhere] * 3,
        scratch=[pltpu.VMEM(grad.shape, grad.dtype)] * 2 + [pltpu.SemaphoreType.DMA((2 * steps + 1,))],
        params=large,
    )
    return sol, left.reshape(coeff_basis.shape), right.reshape(coeff_basis.shape)


def solution(mesh):
    in_specs = (
        P(("groups", "leaf"), None),
        P(("groups", "leaf"), None),
        P(None, None, ("groups", "leaf")),
        P(None, None, ("groups", "leaf")),
        P("groups", None, None),
        P(("groups", "leaf")),
    )
    out_specs = (
        P(("groups", "leaf"), None),
        P(None, None, ("groups", "leaf")),
        P(None, None, ("groups", "leaf")),
    )
    return jax.shard_map(body, mesh=mesh, in_specs=in_specs, out_specs=out_specs, check_vma=False)
```

time: 54.2 us -> 33 us (0.61)
  Pallas kernels: 24.7 us -> 11.4 us
  waiting for transfers between devices: 11.2 us -> 5.62 us
  local copies, waits for them, and re-layouts: 3.94 us -> 0 us
  starting transfers between devices: 11.7 us -> 14.3 us
  other arithmetic: 1.08 us -> 0 us
    pallas_call x6 -> x12, Pallas kernels: 17.7 us -> 6.93 us  [call(): pl.pallas_call(kernel, out_shape=out_shape, in_specs=[vmem] * len(operand...]
    ppermute x9 -> x10, waiting for transfers between devices: 11.2 us -> 5.62 us  [swapped(): return lax.ppermute(value, 'leaf', pairs)]
    unnamed x18 -> x0, local copies, waits for them, and re-layouts: 3.94 us -> none
    ppermute x9 -> x10, starting transfers between devices: 11.7 us -> 14.3 us  [swapped(): return lax.ppermute(value, 'leaf', pairs)]
    pallas_call x1, Pallas kernels: 6.93 us -> 4.51 us  [body(): pl.pallas_call(functools.partial(local_kernel, (levels, rank, base_bits,...]
    add x3 -> x0, other arithmetic: 1.08 us -> none  [body(): side = (side + sib_side)[side_rows(k, levels, rank):]]
  transfers between devices with their start and end apart: 9 -> 10, of which waited for: 6 -> 3; matrix products, arithmetic and copies ran while one was open for 2% -> 0% of each run, Pallas kernels for 15% -> 13%
where the time goes in v2:
time: 33 us; the launch traced here: 32.8 us
  starting transfers between devices  14.3 us (43%)
  Pallas kernels  11.4 us (35%)
  waiting for transfers between devices  5.62 us (17%)
  between operations  1.38 us (4%)
    ppermute x10, starting transfers between devices, swapped(): return lax.ppermute(value, 'leaf', pairs)  14.3 us
    pallas_call x12, Pallas kernels, call(): pl.pallas_call(kernel, out_shape=out_shape, in_specs=[vmem] * len(operand...  6.93 us
    ppermute x10, waiting for transfers between devices, swapped(): return lax.ppermute(value, 'leaf', pairs)  5.62 us
    pallas_call x1, Pallas kernels, body(): pl.pallas_call(functools.partial(local_kernel, (levels, rank, base_bits,...  4.51 us
  transfers between devices with their start and end apart: 10, of which 3 were waited for; matrix products, arithmetic and copies ran while one was open for 0% of the time, Pallas kernels for 13%

profile of v2, /device:TPU:0, one launch (start us, length us, event | category | flops | bytes accessed | tf_op | source)
XLA Modules:
  0.0 32.8 jit_solution(17848680033053820205)
XLA Ops:
  1.3 4.5 %local_sums.1 = (f32[448,128]{1,0:T(8,128)S(1)}, f32[448,128]{1,0:T(8,128)S(1)}, f32[256,256]{1,0:T(8,128)S(1)}, f32[4,128,128]{2,1,0:T(8,128)S(1)}, s32[8,128]{...) custom-call(s32[1]{0:T(128)S(6)} %copy.9.rows_hbm, ...), custom_call_target="tpu_custom_call" | custom-call | tf_op jit(solution)/shard_map/local_sums/pallas_call | solution.py:359
  5.8 0.5 %collective-permute-start = (f32[448,128]{1,0:T(8,128)S(1)}, f32[448,128]{1,0:T(8,128)S(1)}, u32[]{:S(2)}, u32[]{:S(2)}) collective-permute-start(f32[448,128]{1,0:T(8,128)S(1)} %get-tuple-element.31), channel_id=1, source_target_pairs={{0,1},{1,0},{2,3},{3,2},{4,5},{5,4},{6,7},{7,6},{8,9},{9,8},{10,11... | collective-permute-start | bytes 688136 | tf_op jit(solution)/shard_map/ppermute | solution.py:313
  6.3 1.3 %side_sums.1 = (f32[576,128]{1,0:T(8,128)S(1)}, f32[576,128]{1,0:T(8,128)S(1)}) custom-call(s32[8,128]{1,0:T(8,128)S(1)} %get-tuple-element.29.count_ref, f32[2048,256]{1,0:T(8,128)S(1)} %get-tuple-element.37.w_ref, f32[256,2048]{1,0:T(8,128)S(1)} %get-tuple-element.38.u_ref, f32[256,256]{1,0:T(8,128)S(1)} %get-tuple-element.39.g_ref), custom_call_target="tpu_custom_call" | custom-call | flops 805306368 | bytes 1048576 | tf_op jit(solution)/shard_map/side_sums/pallas_call | solution.py:342
  7.6 0.1 collective-permute-start.3
  7.7 0.0 collective-permute-done.sib_ref.refs_0_
  7.7 0.4 %level_0.1 = (f32[128,128]{1,0:T(8,128)S(1)}, f32[288,128]{1,0:T(8,128)S(1)}) custom-call(f32[448,128]{1,0:T(8,128)S(1)} %get-tuple-element.30.own_ref.refs_12_, f32[448,128]{1,0:T(8,128)S(1)} %collective-permute-done.sib_ref.refs_0_, f32[4,128,128]{2,1,0:T(8,128)S(1)} %get-tuple-element.32.nodes_ref), custom_call_target="tpu_custom_call" | custom-call | flops 20000000000 | bytes 1048576 | tf_op jit(solution)/shard_map/level_0/pallas_call | solution.py:342
  8.1 3.0 %collective-permute-start.1 = (f32[288,128]{1,0:T(8,128)S(1)}, f32[288,128]{1,0:T(8,128)S(1)}, u32[]{:S(2)}, u32[]{:S(2)}) collective-permute-start(f32[288,128]{1,0:T(8,128)S(1)} %get-tuple-element.34.own_ref), channel_id=1, source_target_pairs={{0,2},{1,3},{2,0},{3,1},{4,6},{5,7},{6,4},{7,5},{8,10},{9,11},{10,... | collective-permute-start | bytes 442376 | tf_op jit(solution)/shard_map/ppermute | solution.py:313
  11.2 0.0 collective-permute-done.3.sib_ref.refs_4_.refs_8_
  11.2 1.6 %collective-permute-start.4 = (f32[224,128]{1,0:T(8,128)S(1)}, f32[224,128]{1,0:T(8,128)S(1)}, u32[]{:S(2)}, u32[]{:S(2)}) collective-permute-start(f32[224,128]{1,0:T(8,128)S(1)} %get-tuple-element.43.sent_ref), channel_id=1, source_target_pairs={{0,4},{1,5},{2,6},{3,7},{4,0},{5,1},{6,2},{7,3},{8,12},{9,13},{10,... | collective-permute-start | bytes 344072 | tf_op jit(solution)/shard_map/ppermute | solution.py:313
  12.8 2.4 %collective-permute-done.1.sib_ref.refs_1_ = f32[288,128]{1,0:T(8,128)S(1)} collective-permute-done((f32[288,128]{1,0:T(8,128)S(1)}, f32[288,128]{1,0:T(8,128)S(1)}, u32[]{:S(2)}, u32[]{:S(2)}) %collective-permute-start.1) | collective-permute-done | bytes 147488 | tf_op jit(solution)/shard_map/ppermute | solution.py:313
  15.2 0.4 %level_1.1 = (f32[128,128]{1,0:T(8,128)S(1)}, f32[160,128]{1,0:T(8,128)S(1)}) custom-call(f32[288,128]{1,0:T(8,128)S(1)} %get-tuple-element.34.own_ref, f32[288,128]{1,0:T(8,128)S(1)} %collective-permute-done.1.sib_ref.refs_1_, f32[4,128,128]{2,1,0:T(8,128)S(1)} %get-tuple-element.32.nodes_ref), custom_call_target="tpu_custom_call" | custom-call | flops 20000000000 | bytes 1048576 | tf_op jit(solution)/shard_map/level_1/pallas_call | solution.py:342
  15.6 1.9 %collective-permute-start.2 = (f32[160,128]{1,0:T(8,128)S(1)}, f32[160,128]{1,0:T(8,128)S(1)}, u32[]{:S(2)}, u32[]{:S(2)}) collective-permute-start(f32[160,128]{1,0:T(8,128)S(1)} %get-tuple-element.36.own_ref), channel_id=1, source_target_pairs={{0,4},{1,5},{2,6},{3,7},{4,0},{5,1},{6,2},{7,3},{8,12},{9,13},{10,... | collective-permute-start | bytes 245768 | tf_op jit(solution)/shard_map/ppermute | solution.py:313
  17.4 0.0 collective-permute-done.4.got_ref
  17.5 1.6 %collective-permute-start.6 = (f32[384,128]{1,0:T(8,128)S(1)}, f32[384,128]{1,0:T(8,128)S(1)}, u32[]{:S(2)}, u32[]{:S(2)}) collective-permute-start(f32[384,128]{1,0:T(8,128)S(1)} %side_join_1.1.refs_0_.sent_ref.refs_5_.refs_9_), channel_id=1, source_target_pairs={{0,2},{1,3},{2,0},{3,1},{4,6},{5,7},{6,4},{7,5},{8,10},{9,11},{10,... | collective-permute-start | bytes 589832 | tf_op jit(solution)/shard_map/ppermute | solution.py:313
  19.1 1.0 %collective-permute-done.2.sib_ref.refs_2_ = f32[160,128]{1,0:T(8,128)S(1)} collective-permute-done((f32[160,128]{1,0:T(8,128)S(1)}, f32[160,128]{1,0:T(8,128)S(1)}, u32[]{:S(2)}, u32[]{:S(2)}) %collective-permute-start.2) | collective-permute-done | bytes 81952 | tf_op jit(solution)/shard_map/ppermute | solution.py:313
  20.1 0.4 %level_2.1 = (f32[128,128]{1,0:T(8,128)S(1)}, f32[64,128]{1,0:T(8,128)S(1)}) custom-call(f32[160,128]{1,0:T(8,128)S(1)} %get-tuple-element.36.own_ref, f32[160,128]{1,0:T(8,128)S(1)} %collective-permute-done.2.sib_ref.refs_2_, f32[4,128,128]{2,1,0:T(8,128)S(1)} %get-tuple-element.32.nodes_ref, f32[384,128]{1,0:T(8,128)S(1)} %side_join_1.1.refs_0_.sent_ref.refs_5_.refs_9_), custom_call_target="tpu_custom_call" | custom-call | flops 20000000000 | bytes 1048576 | tf_op jit(solution)/shard_map/level_2/pallas_call | solution.py:342
  20.4 2.9 %collective-permute-start.5 = (f32[64,128]{1,0:T(8,128)S(1)}, f32[64,128]{1,0:T(8,128)S(1)}, u32[]{:S(2)}, u32[]{:S(2)}) collective-permute-start(f32[64,128]{1,0:T(8,128)S(1)} %get-tuple-element.45.own_ref), channel_id=1, source_target_pairs={{0,8},{1,9},{2,10},{3,11},{4,12},{5,13},{6,14},{7,15},{8,0},{9,1},... | collective-permute-start | bytes 98312 | tf_op jit(solution)/shard_map/ppermute | solution.py:313
  23.3 0.0 collective-permute-done.6.got_ref.refs_6_.refs_10_
  23.3 2.6 %collective-permute-start.8 = (f32[96,128]{1,0:T(8,128)S(1)}, f32[96,128]{1,0:T(8,128)S(1)}, u32[]{:S(2)}, u32[]{:S(2)}) collective-permute-start(f32[96,128]{1,0:T(8,128)S(1)} %side_top.1.refs_0_), channel_id=1, source_target_pairs={{0,8},{1,9},{2,10},{3,11},{4,12},{5,13},{6,14},{7,15},{8,0},{9,1},... | collective-permute-start | bytes 147464 | tf_op jit(solution)/shard_map/ppermute | solution.py:313
  25.9 0.0 collective-permute-done.5.sib_ref.refs_3_
  25.9 0.2 level_3.1.refs_3_.refs_7_
  26.1 0.1 collective-permute-start.7
  26.2 2.2 %collective-permute-done.8.refs_11_ = f32[96,128]{1,0:T(8,128)S(1)} collective-permute-done((f32[96,128]{1,0:T(8,128)S(1)}, f32[96,128]{1,0:T(8,128)S(1)}, u32[]{:S(2)}, u32[]{:S(2)}) %collective-permute-start.8) | collective-permute-done | bytes 49184 | tf_op jit(solution)/shard_map/ppermute | solution.py:313
  28.4 0.3 end_factors.1
  28.7 0.1 collective-permute-start.9
  28.7 0.0 collective-permute-done.7.other_ref.low_other
  28.7 1.3 %solution_rows.1.x_ref = f32[2048,256]{1,0:T(8,128)S(1)} custom-call(s32[8,128]{1,0:T(8,128)S(1)} %get-tuple-element.29.count_ref, f32[448,128]{1,0:T(8,128)S(1)} %get-tuple-element.46.own_ref.low_own, f32[448,128]{1,0:T(8,128)S(1)} %collective-permute-done.7.other_ref.low_other, f32[2048,256]{1,0:T(8,128)S(1)} %get-tuple-element.50.x_ref, ...), custom_call_target="tpu_custom_call" | custom-call | flops 2000000000 | bytes 1048576 | tf_op jit(solution)/shard_map/solution_rows/pallas_call | solution.py:342
  30.1 0.0 collective-permute-done.9.top_other
  30.1 2.7 %factor_rows.1 = (f32[2048,256]{1,0:T(8,128)}, bf16[256,2048]{1,0:T(8,128)(2,1)}, bf16[256,2048]{1,0:T(8,128)(2,1)}) custom-call(s32[8,128]{1,0:T(8,128)S(1)} %get-tuple-element.29.count_ref, f32[448,128]{1,0:T(8,128)S(1)} %get-tuple-element.46.own_ref.low_own, f32[448,128]{1,0:T(8,128)S(1)} %collective-permute-done.7.other_ref.low_other, ...), custom_call_target="tpu_custom_call" | custom-call | tf_op jit(solution)/shard_map/factor_rows/pallas_call | solution.py:342
  (4 shorter events, 0.1 us)
Async XLA Ops:
  5.8 1.9 %collective-permute-start = (f32[448,128]{1,0:T(8,128)S(1)}, f32[448,128]{1,0:T(8,128)S(1)}, u32[]{:S(2)}, u32[]{:S(2)}) collective-permute-start(f32[448,128]{1,0:T(8,128)S(1)} %get-tuple-element.31), channel_id=1, source_target_pairs={{0,1},{1,0},{2,3},{3,2},{4,5},{5,4},{6,7},{7,6},{8,9},{9,8},{10,11... | collective-permute-start | bytes 688136 | tf_op jit(solution)/shard_map/ppermute | solution.py:313
  7.6 3.6 %collective-permute-start.3 = (f32[576,128]{1,0:T(8,128)S(1)}, f32[576,128]{1,0:T(8,128)S(1)}, u32[]{:S(2)}, u32[]{:S(2)}) collective-permute-start(f32[576,128]{1,0:T(8,128)S(1)} %get-tuple-element.41), channel_id=1, source_target_pairs={{0,1},{1,0},{2,3},{3,2},{4,5},{5,4},{6,7},{7,6},{8,9},{9,8},{10,11... | collective-permute-start | bytes 884744 | tf_op jit(solution)/shard_map/ppermute | solution.py:313
  8.1 7.1 %collective-permute-start.1 = (f32[288,128]{1,0:T(8,128)S(1)}, f32[288,128]{1,0:T(8,128)S(1)}, u32[]{:S(2)}, u32[]{:S(2)}) collective-permute-start(f32[288,128]{1,0:T(8,128)S(1)} %get-tuple-element.34.own_ref), channel_id=1, source_target_pairs={{0,2},{1,3},{2,0},{3,1},{4,6},{5,7},{6,4},{7,5},{8,10},{9,11},{10,... | collective-permute-start | bytes 442376 | tf_op jit(solution)/shard_map/ppermute | solution.py:313
  11.2 6.3 %collective-permute-start.4 = (f32[224,128]{1,0:T(8,128)S(1)}, f32[224,128]{1,0:T(8,128)S(1)}, u32[]{:S(2)}, u32[]{:S(2)}) collective-permute-start(f32[224,128]{1,0:T(8,128)S(1)} %get-tuple-element.43.sent_ref), channel_id=1, source_target_pairs={{0,4},{1,5},{2,6},{3,7},{4,0},{5,1},{6,2},{7,3},{8,12},{9,13},{10,... | collective-permute-start | bytes 344072 | tf_op jit(solution)/shard_map/ppermute | solution.py:313
  15.6 4.5 %collective-permute-start.2 = (f32[160,128]{1,0:T(8,128)S(1)}, f32[160,128]{1,0:T(8,128)S(1)}, u32[]{:S(2)}, u32[]{:S(2)}) collective-permute-start(f32[160,128]{1,0:T(8,128)S(1)} %get-tuple-element.36.own_ref), channel_id=1, source_target_pairs={{0,4},{1,5},{2,6},{3,7},{4,0},{5,1},{6,2},{7,3},{8,12},{9,13},{10,... | collective-permute-start | bytes 245768 | tf_op jit(solution)/shard_map/ppermute | solution.py:313
  17.5 5.8 %collective-permute-start.6 = (f32[384,128]{1,0:T(8,128)S(1)}, f32[384,128]{1,0:T(8,128)S(1)}, u32[]{:S(2)}, u32[]{:S(2)}) collective-permute-start(f32[384,128]{1,0:T(8,128)S(1)} %side_join_1.1.refs_0_.sent_ref.refs_5_.refs_9_), channel_id=1, source_target_pairs={{0,2},{1,3},{2,0},{3,1},{4,6},{5,7},{6,4},{7,5},{8,10},{9,11},{10,... | collective-permute-start | bytes 589832 | tf_op jit(solution)/shard_map/ppermute | solution.py:313
  20.4 5.5 %collective-permute-start.5 = (f32[64,128]{1,0:T(8,128)S(1)}, f32[64,128]{1,0:T(8,128)S(1)}, u32[]{:S(2)}, u32[]{:S(2)}) collective-permute-start(f32[64,128]{1,0:T(8,128)S(1)} %get-tuple-element.45.own_ref), channel_id=1, source_target_pairs={{0,8},{1,9},{2,10},{3,11},{4,12},{5,13},{6,14},{7,15},{8,0},{9,1},... | collective-permute-start | bytes 98312 | tf_op jit(solution)/shard_map/ppermute | solution.py:313
  23.3 5.1 %collective-permute-start.8 = (f32[96,128]{1,0:T(8,128)S(1)}, f32[96,128]{1,0:T(8,128)S(1)}, u32[]{:S(2)}, u32[]{:S(2)}) collective-permute-start(f32[96,128]{1,0:T(8,128)S(1)} %side_top.1.refs_0_), channel_id=1, source_target_pairs={{0,8},{1,9},{2,10},{3,11},{4,12},{5,13},{6,14},{7,15},{8,0},{9,1},... | collective-permute-start | bytes 147464 | tf_op jit(solution)/shard_map/ppermute | solution.py:313
  26.1 2.6 %collective-permute-start.7 = (f32[448,128]{1,0:T(8,128)S(1)}, f32[448,128]{1,0:T(8,128)S(1)}, u32[]{:S(2)}, u32[]{:S(2)}) collective-permute-start(f32[448,128]{1,0:T(8,128)S(1)} %get-tuple-element.47), channel_id=1, source_target_pairs={{0,1},{1,0},{2,3},{3,2},{4,5},{5,4},{6,7},{7,6},{8,9},{9,8},{10,11... | collective-permute-start | bytes 688136 | tf_op jit(solution)/shard_map/ppermute | solution.py:313
  28.7 1.5 %collective-permute-start.9 = (f32[320,128]{1,0:T(8,128)S(1)}, f32[320,128]{1,0:T(8,128)S(1)}, u32[]{:S(2)}, u32[]{:S(2)}) collective-permute-start(f32[320,128]{1,0:T(8,128)S(1)} %get-tuple-element.49), channel_id=1, source_target_pairs={{0,1},{1,0},{2,3},{3,2},{4,5},{5,4},{6,7},{7,6},{8,9},{9,8},{10,11... | collective-permute-start | bytes 491528 | tf_op jit(solution)/shard_map/ppermute | solution.py:313

commit v3 on v2

--- a/solution.py
+++ b/solution.py
@@ -50,6 +50,14 @@
 
 def solve_rows(level, levels, rank):
     return rank + pack_rows(levels - 1 - level, rank)
+
+
+def row_parts(row_count):
+    eighth = row_count // 8
+    if eighth % 128:
+        return [(0, row_count)]
+    sizes = [eighth, 2 * eighth, 2 * eighth, 2 * eighth, eighth]
+    return [(sum(sizes[:n]), size) for n, size in enumerate(sizes)]
 
 
 def write_state(keep, send, acc, rank, blocks_of):
@@ -68,56 +76,45 @@
             at += rows.shape[0]
 
 
-def local_kernel(dims, rows_hbm, x_hbm, w_hbm, u_hbm, q_hbm, node_ref, *refs):
-    levels, rank, base_bits, chunk, ahead = dims
-    keep, send, g_ref, nodes_out, count_out, x_all, w_all, u_all, q_all = refs[:9]
-    rows_ref, c_acc, sems, w_sem, row_sem, node_sems = refs[9:]
+def local_kernel(dims, parts, ahead, count_ref, x_hbm, w_hbm, u_hbm, q_hbm, node_ref, *refs):
+    levels, rank, base_bits = dims
+    keep, send, g_ref, nodes_out, x_all, w_all, u_all, q_all, c_acc, sems, w_sem, node_sems = refs
     position = lax.axis_index("leaf")
-    steps = x_all.shape[0] // chunk
-
-    def copies(i):
-        part = pl.ds(pl.multiple_of(i * chunk, chunk), chunk)
+
+    def copies(n):
+        part = pl.ds(*parts[n])
         pairs = [(u_hbm.at[:, part], u_all.at[:, part]), (x_hbm.at[part], x_all.at[part])]
         pairs.append((q_hbm.at[:, part], q_all.at[:, part]))
-        return [pltpu.make_async_copy(a, b, sems.at[i, n]) for n, (a, b) in enumerate(pairs)]
+        return [pltpu.make_async_copy(a, b, sems.at[n, i]) for i, (a, b) in enumerate(pairs)]
 
     def node_copy(k):
         index = 2**levels - 2 ** (levels - k) + jnp.right_shift(position, base_bits + k + 1)
         return pltpu.make_async_copy(node_ref.at[index], nodes_out.at[k], node_sems.at[k])
 
-    row_copy = pltpu.make_async_copy(rows_hbm, rows_ref, row_sem)
     w_copy = pltpu.make_async_copy(w_hbm, w_all, w_sem)
-    row_copy.start()
-    for i in range(min(ahead, steps)):
-        for copy in copies(i):
+    for n in range(ahead):
+        for copy in copies(n):
             copy.start()
     for k in range(levels):
         node_copy(k).start()
-    c_acc[...] = jnp.zeros_like(c_acc)
-    g_ref[...] = jnp.zeros_like(g_ref)
-    row_copy.wait()
-    count_out[...] = jnp.full(count_out.shape, rows_ref[0], jnp.int32)
-
-    def step(i, carry):
-        @pl.when(i + ahead < steps)
+
+    for n, (first, size) in enumerate(parts):
+        @pl.when(position >= 0)
         def _():
-            for copy in copies(i + ahead):
-                copy.start()
-
-        @pl.when(i + ahead == max(steps, ahead))
-        def _():
-            w_copy.start()
-
-        for copy in copies(i):
-            copy.wait()
-        part = pl.ds(pl.multiple_of(i * chunk, chunk), chunk)
-        place = i * chunk + lax.broadcasted_iota(jnp.int32, (1, chunk), 1)
-        u = jnp.where(place < rows_ref[0], u_all[:, part], 0.0)
-        c_acc[...] += dot(u, x_all[part, :])
-        g_ref[...] += dot(u, q_all[:, part], ((1,), (1,)))
-        return carry
-
-    lax.fori_loop(0, steps, step, 0)
+            if n + ahead < len(parts):
+                for copy in copies(n + ahead):
+                    copy.start()
+            if n + ahead == len(parts):
+                w_copy.start()
+            for copy in copies(n):
+                copy.wait()
+            part = pl.ds(first, size)
+            place = first + lax.broadcasted_iota(jnp.int32, (1, size), 1)
+            u = jnp.where(place < count_ref[:1, :1], u_all[:, part], 0.0)
+            c = dot(u, x_all[part, :])
+            g = dot(u, q_all[:, part], ((1,), (1,)))
+            c_acc[...] = c if n == 0 else c_acc[...] + c
+            g_ref[...] = g if n == 0 else g_ref[...] + g
 
     def blocks(k):
         lane = slice(k * rank, (k + 1) * rank)
@@ -129,17 +126,20 @@
     w_copy.wait()
 
 
-def side_kernel(dims, count_ref, w_ref, u_ref, g_ref, keep, send, k_acc):
+def side_kernel(count_ref, w_ref, u_ref, k_ref):
+    place = lax.broadcasted_iota(jnp.int32, (1, u_ref.shape[1]), 1)
+    k_ref[...] = dot(jnp.where(place < count_ref[:1, :1], u_ref[...], 0.0), w_ref[...])
+
+
+def side_state_kernel(dims, k_ref, g_ref, after_ref, keep, send):
+    del after_ref
     levels, rank = dims
-    place = lax.broadcasted_iota(jnp.int32, (1, u_ref.shape[1]), 1)
-    u = jnp.where(place < count_ref[:1, :1], u_ref[...], 0.0)
-    k_acc[...] = dot(u, w_ref[...])
 
     def blocks(k):
         row = slice(k * rank, (k + 1) * rank)
         return [g_ref[row, j * rank : (j + 1) * rank] for j in range(k, levels)]
 
-    write_state(keep, send, k_acc, rank, blocks)
+    write_state(keep, send, k_ref, rank, blocks)
 
 
 def side_first_kernel(at, own_ref, sib_ref, after_ref, *out_refs):
@@ -150,12 +150,16 @@
         at += rows
 
 
-def side_join_kernel(first, fresh_ref, sent_ref, got_ref, after_ref, out_ref):
+def side_join_kernel(first, fresh_ref, sent_ref, got_ref, after_ref, *refs):
     del after_ref
-    rows = fresh_ref.shape[0]
-    out_ref[:rows, :] = fresh_ref[...]
-    out_ref[rows : rows + first, :] = got_ref[:first, :]
-    out_ref[rows + first :, :] = sent_ref[first:, :] + got_ref[first:, :]
+    *top_ref, out_ref = refs
+    at, rows = fresh_ref.shape[0], got_ref.shape[0]
+    out_ref[:at, :] = fresh_ref[...]
+    out_ref[at : at + first, :] = got_ref[:first, :]
+    if first < rows:
+        out_ref[at + first : at + rows, :] = sent_ref[first:, :] + got_ref[first:, :]
+    if top_ref:
+        out_ref[at + rows :, :] = top_ref[0][...]
 
 
 def side_top_kernel(sent_ref, got_ref, after_ref, out_ref):
@@ -166,7 +170,7 @@
 
 def level_kernel(dims, level, own_ref, sib_ref, nodes_ref, *refs):
     levels, rank, base_bits, placed = dims
-    z_ref, *out_refs = refs[1:] if placed else refs
+    z_ref, *out_refs = refs[placed:]
     is_lower = jnp.right_shift(lax.axis_index("leaf"), base_bits + level) % 2 == 0
     own, sib = own_ref[:rank, :], sib_ref[:rank, :]
     both = jnp.concatenate([jnp.where(is_lower, own, sib), jnp.where(is_lower, sib, own)], 0)
@@ -231,8 +235,9 @@
 def end_kernel(dims, pair, *refs):
     levels, rank, _ = dims
     solves, z_refs = refs[:levels], refs[levels : 2 * levels]
-    sib_side, side_sent, side_got, top_side, own_solve, own_side = refs[2 * levels : 2 * levels + 6]
-    *out_refs, side_sum = refs[2 * levels + 6 :]
+    sib_side, side_sent, side_got, top_sent, top_got, own_solve, own_side = refs[2 * levels : 2 * levels + 7]
+    *out_refs, side_sum, top_side = refs[2 * levels + 7 :]
+    top_side[...] = top_sent[...] + top_got[...]
     z_own = [z_ref[:rank, :] for z_ref in z_refs]
 
     low = side_rows(1, levels, rank)
@@ -326,6 +331,7 @@
     pair = base_bits == 0
     chunk = min(512, row_count)
     steps = row_count // chunk
+    parts = row_parts(row_count)
     u_all = coeff_basis.reshape(wide, row_count)
     q_all = saved_basis.reshape(wide, row_count)
 
@@ -354,57 +360,78 @@
     n_side = [side_rows(k, levels, rank) for k in range(levels)]
     arrays = (right_side, cotangent, u_all, q_all)
     outs = [shape(n_solve, half), shape(n_solve, half), shape(wide, wide), shape(levels, order, order)]
-    outs += [shape(8, 128, dtype=jnp.int32)] + [shape(*a.shape) for a in arrays]
+    outs += [shape(*a.shape) for a in arrays]
+    count = jnp.broadcast_to(leaf_rows[:, None], (8, 128))
     hbm = [pltpu.with_memory_space_constraint(a, pltpu.HBM) for a in (*arrays, node_inverse)]
-    solve, solve_send, products, nodes, count, x_vmem, w_vmem, u_vmem, q_vmem = pl.pallas_call(
-        functools.partial(local_kernel, (levels, rank, base_bits, chunk, 2)),
+    solve, solve_send, products, nodes, x_vmem, w_vmem, u_vmem, q_vmem = pl.pallas_call(
+        functools.partial(local_kernel, (levels, rank, base_bits), parts, min(3, len(parts))),
         out_shape=outs,
-        in_specs=[anywhere] * 6,
-        out_specs=[vmem] * 9,
+        in_specs=[vmem] + [anywhere] * 5,
+        out_specs=[vmem] * 8,
         scratch_shapes=[
-            pltpu.SMEM((1,), jnp.int32),
             pltpu.VMEM((wide, col_count), F32),
-            pltpu.SemaphoreType.DMA((steps, 3)),
-            pltpu.SemaphoreType.DMA,
+            pltpu.SemaphoreType.DMA((len(parts), 3)),
             pltpu.SemaphoreType.DMA,
             pltpu.SemaphoreType.DMA((levels,)),
         ],
         compiler_params=large,
         name="local_sums",
-    )(leaf_rows, *hbm)
-    side, side_send = call(
-        functools.partial(side_kernel, (levels, rank)),
+    )(count, *hbm)
+    k_sums = call(
+        side_kernel,
         "side_sums",
-        [shape(sum(n_side), half)] * 2,
+        shape(wide, col_count),
         count,
         w_vmem,
         u_vmem,
-        products,
-        scratch=[pltpu.VMEM((wide, col_count), F32)],
         params=large,
         cost=6 * wide * row_count * col_count,
     )
 
-    if pair:
-        sib_solve, sib_side = swapped(solve_send, 0), swapped(side_send, 0)
-    else:
-        solve, side = solve + swapped(solve_send, 0), side + swapped(side_send, 0)
+    def lowest(solve, solve_send):
+        if pair:
+            return solve, swapped(solve_send, 0)
+        solve = solve + swapped(solve_send, 0)
         for bit in range(1, base_bits):
-            solve, side = solve + swapped(solve, bit), side + swapped(side, bit)
-        sib_solve, sib_side = swapped(solve, base_bits), swapped(side, base_bits)
-
+            solve = solve + swapped(solve, bit)
+        return solve, swapped(solve, base_bits)
+
+    solve, sib_solve = lowest(solve, solve_send)
     own_solve = solve
-    solves, zs, fresh, placed = [], [], {}, []
-    sent = got = None
+    solves, zs, fresh = [], [], {}
     for k in range(levels):
         if k > 0:
             sib_solve = swapped(solve, base_bits + k)
         solves.append(sib_solve)
+        placed = []
+        if k == 1:
+            top_got = swapped(fresh[top], base_bits + top)
+            sent = fresh[top - 1]
+            got = swapped(sent, base_bits + top - 1)
+        elif 1 < k < top:
+            bit = top - k
+            sent = call(
+                functools.partial(side_join_kernel, n_side[bit + 1]),
+                f"side_join_{bit}",
+                shape(sum(n_side[bit:]), half),
+                fresh[bit],
+                sent,
+                got,
+                zs[-1],
+                *([top_got] if k == 2 else []),
+                cost=2 * 10**10,
+            )
+            got = swapped(sent, base_bits + bit)
+            placed = [sent]
+        elif k == top:
+            top_sum = call(side_top_kernel, "side_top", shape(n_side[top], half), sent, got, zs[-1])
+            top_got = swapped(top_sum, base_bits + top - 1)
+            placed = [top_sum]
         out_shape = [shape(order, half)]
         if k < top:
             out_shape.append(shape(sum(solve_rows(i, levels, rank) for i in range(k + 1, levels)), half))
         outs = call(
-            functools.partial(level_kernel, (levels, rank, base_bits, len(placed) > 0), k),
+            functools.partial(level_kernel, (levels, rank, base_bits, len(placed)), k),
             f"level_{k}",
             out_shape,
             solve,
@@ -417,35 +444,24 @@
         if k < top:
             solve = outs[1]
         if k == 0:
-            sizes = [*n_side[1 : top - 1], n_side[top - 1] + n_side[top]]
+            side, side_send = call(
+                functools.partial(side_state_kernel, (levels, rank)),
+                "side_state",
+                [shape(sum(n_side), half)] * 2,
+                k_sums,
+                products,
+                outs[0],
+            )
+            side, sib_side = lowest(side, side_send)
             first = call(
                 functools.partial(side_first_kernel, n_side[0]),
                 "side_first",
-                [shape(size, half) for size in sizes],
+                [shape(size, half) for size in n_side[1:]],
                 side,
                 sib_side,
                 outs[0],
             )
             fresh = dict(enumerate(first, 1))
-            sent = fresh[top - 1]
-            got = swapped(sent, base_bits + top - 1)
-        elif k < top - 1:
-            bit = top - 1 - k
-            sent = call(
-                functools.partial(side_join_kernel, n_side[bit + 1]),
-                f"side_join_{bit}",
-                shape(fresh[bit].shape[0] + sent.shape[0], half),
-                fresh[bit],
-                sent,
-                got,
-                outs[0],
-            )
-            got = swapped(sent, base_bits + bit)
-            placed = [sent]
-        elif k == top - 1:
-            last = call(side_top_kernel, "side_top", shape(n_side[top], half), sent, got, outs[0])
-            placed = [last]
-    top_side = swapped(last, base_bits + top)
 
     dims = (levels, rank, 1.0 / col_count**0.5)
     copies = 2 if pair else 1
@@ -469,10 +485,11 @@
         sib_side,
         sent,
         got,
-        top_side,
+        top_sum,
+        top_got,
         own_solve,
         side,
-        scratch=[pltpu.VMEM((sum(n_side[1:top]), half), F32)],
+        scratch=[pltpu.VMEM((sum(n_side[1:top]), half), F32), pltpu.VMEM((n_side[top], half), F32)],
         cost=2 * 10**10,
     )
     top_other = swapped(top_other[0] if pair else top_own, 0)

time: 33 us -> 32.3 us (0.979)
  waiting for transfers between devices: 5.62 us -> 4.09 us
  starting transfers between devices: 14.3 us -> 15.5 us
    ppermute x10 -> x11, waiting for transfers between devices: 5.62 us -> 4.09 us  [swapped(): return lax.ppermute(value, 'leaf', pairs)]
    ppermute x10 -> x11, starting transfers between devices: 14.3 us -> 15.5 us  [swapped(): return lax.ppermute(value, 'leaf', pairs)]
    pallas_call x1, Pallas kernels: 4.51 us -> 3.99 us  [body(): pl.pallas_call(functools.partial(local_kernel, (levels, rank, base_bits),...]
    pallas_call x12 -> x13, Pallas kernels: 6.93 us -> 7.06 us  [call(): pl.pallas_call(kernel, out_shape=out_shape, in_specs=[vmem] * len(operand...]
  transfers between devices with their start and end apart: 10 -> 11, of which waited for: 3 -> 4; matrix products, arithmetic and copies ran while one was open for 0% -> 0% of each run, Pallas kernels for 13% -> 12%
where the time goes in v3:
time: 32.3 us; the launch traced here: 32.1 us
  starting transfers between devices  15.5 us (48%)
  Pallas kernels  11.1 us (34%)
  waiting for transfers between devices  4.09 us (13%)
  between operations  1.4 us (4%)
    ppermute x11, starting transfers between devices, swapped(): return lax.ppermute(value, 'leaf', pairs)  15.5 us
    pallas_call x13, Pallas kernels, call(): pl.pallas_call(kernel, out_shape=out_shape, in_specs=[vmem] * len(operand...  7.06 us
    ppermute x11, waiting for transfers between devices, swapped(): return lax.ppermute(value, 'leaf', pairs)  4.09 us
    pallas_call x1, Pallas kernels, body(): pl.pallas_call(functools.partial(local_kernel, (levels, rank, base_bits),...  3.99 us
  transfers between devices with their start and end apart: 11, of which 4 were waited for; matrix products, arithmetic and copies ran while one was open for 0% of the time, Pallas kernels for 12%

profile of v3, /device:TPU:0, one launch (start us, length us, event | category | flops | bytes accessed | tf_op | source)
XLA Modules:
  0.0 32.1 jit_solution(13576604245115885781)
XLA Ops:
  1.3 4.0 %local_sums.1 = (f32[448,128]{1,0:T(8,128)S(1)}, f32[448,128]{1,0:T(8,128)S(1)}, f32[256,256]{1,0:T(8,128)S(1)}, f32[4,128,128]{2,1,0:T(8,128)S(1)}, f32[2048,25...) custom-call(s32[8,128]{1,0:T(8,128)S(1)} %broadcast_in_dim.9.count_ref, ...), custom_call_target="tpu_custom_call" | custom-call | tf_op jit(solution)/shard_map/local_sums/pallas_call | solution.py:366
  5.3 0.5 %collective-permute-start = (f32[448,128]{1,0:T(8,128)S(1)}, f32[448,128]{1,0:T(8,128)S(1)}, u32[]{:S(2)}, u32[]{:S(2)}) collective-permute-start(f32[448,128]{1,0:T(8,128)S(1)} %get-tuple-element.30), channel_id=1, source_target_pairs={{0,1},{1,0},{2,3},{3,2},{4,5},{5,4},{6,7},{7,6},{8,9},{9,8},{10,11... | collective-permute-start | bytes 688136 | tf_op jit(solution)/shard_map/ppermute | solution.py:318
  5.8 1.3 %side_sums.1.k_ref = f32[256,256]{1,0:T(8,128)S(1)} custom-call(s32[8,128]{1,0:T(8,128)S(1)} %broadcast_in_dim.9.count_ref, f32[2048,256]{1,0:T(8,128)S(1)} %get-tuple-element.36.w_ref, f32[256,2048]{1,0:T(8,128)S(1)} %get-tuple-element.37.u_ref), custom_call_target="tpu_custom_call" | custom-call | flops 805306368 | bytes 1048576 | tf_op jit(solution)/shard_map/side_sums/pallas_call | solution.py:348
  7.1 0.0 collective-permute-done.sib_ref.refs_0_
  7.1 0.4 %level_0.1 = (f32[128,128]{1,0:T(8,128)S(1)}, f32[288,128]{1,0:T(8,128)S(1)}) custom-call(f32[448,128]{1,0:T(8,128)S(1)} %get-tuple-element.29.own_ref.refs_13_, f32[448,128]{1,0:T(8,128)S(1)} %collective-permute-done.sib_ref.refs_0_, f32[4,128,128]{2,1,0:T(8,128)S(1)} %get-tuple-element.31.nodes_ref), custom_call_target="tpu_custom_call" | custom-call | flops 20000000000 | bytes 1048576 | tf_op jit(solution)/shard_map/level_0/pallas_call | solution.py:348
  7.5 0.1 side_state.1
  7.6 0.2 collective-permute-start.3
  7.9 2.8 %collective-permute-start.1 = (f32[288,128]{1,0:T(8,128)S(1)}, f32[288,128]{1,0:T(8,128)S(1)}, u32[]{:S(2)}, u32[]{:S(2)}) collective-permute-start(f32[288,128]{1,0:T(8,128)S(1)} %get-tuple-element.33.own_ref), channel_id=1, source_target_pairs={{0,2},{1,3},{2,0},{3,1},{4,6},{5,7},{6,4},{7,5},{8,10},{9,11},{10,... | collective-permute-start | bytes 442376 | tf_op jit(solution)/shard_map/ppermute | solution.py:318
  10.7 0.0 collective-permute-done.3.sib_ref.refs_4_.refs_8_
  10.7 2.7 %collective-permute-start.5 = (f32[96,128]{1,0:T(8,128)S(1)}, f32[96,128]{1,0:T(8,128)S(1)}, u32[]{:S(2)}, u32[]{:S(2)}) collective-permute-start(f32[96,128]{1,0:T(8,128)S(1)} %get-tuple-element.43), channel_id=1, source_target_pairs={{0,8},{1,9},{2,10},{3,11},{4,12},{5,13},{6,14},{7,15},{8,0},{9,1},... | collective-permute-start | bytes 147464 | tf_op jit(solution)/shard_map/ppermute | solution.py:318
  13.4 1.6 %collective-permute-start.4 = (f32[128,128]{1,0:T(8,128)S(1)}, f32[128,128]{1,0:T(8,128)S(1)}, u32[]{:S(2)}, u32[]{:S(2)}) collective-permute-start(f32[128,128]{1,0:T(8,128)S(1)} %get-tuple-element.42.sent_ref), channel_id=1, source_target_pairs={{0,4},{1,5},{2,6},{3,7},{4,0},{5,1},{6,2},{7,3},{8,12},{9,13},{10,... | collective-permute-start | bytes 196616 | tf_op jit(solution)/shard_map/ppermute | solution.py:318
  15.0 0.0 collective-permute-done.1.sib_ref.refs_1_
  15.0 0.4 %level_1.1 = (f32[128,128]{1,0:T(8,128)S(1)}, f32[160,128]{1,0:T(8,128)S(1)}) custom-call(f32[288,128]{1,0:T(8,128)S(1)} %get-tuple-element.33.own_ref, f32[288,128]{1,0:T(8,128)S(1)} %collective-permute-done.1.sib_ref.refs_1_, f32[4,128,128]{2,1,0:T(8,128)S(1)} %get-tuple-element.31.nodes_ref), custom_call_target="tpu_custom_call" | custom-call | flops 20000000000 | bytes 1048576 | tf_op jit(solution)/shard_map/level_1/pallas_call | solution.py:348
  15.4 1.8 %collective-permute-start.2 = (f32[160,128]{1,0:T(8,128)S(1)}, f32[160,128]{1,0:T(8,128)S(1)}, u32[]{:S(2)}, u32[]{:S(2)}) collective-permute-start(f32[160,128]{1,0:T(8,128)S(1)} %get-tuple-element.35.own_ref), channel_id=1, source_target_pairs={{0,4},{1,5},{2,6},{3,7},{4,0},{5,1},{6,2},{7,3},{8,12},{9,13},{10,... | collective-permute-start | bytes 245768 | tf_op jit(solution)/shard_map/ppermute | solution.py:318
  17.1 0.0 collective-permute-done.5.refs_0_
  17.2 0.6 %collective-permute-done.4.got_ref = f32[128,128]{1,0:T(8,128)S(1)} collective-permute-done((f32[128,128]{1,0:T(8,128)S(1)}, f32[128,128]{1,0:T(8,128)S(1)}, u32[]{:S(2)}, u32[]{:S(2)}) %collective-permute-start.4) | collective-permute-done | bytes 65568 | tf_op jit(solution)/shard_map/ppermute | solution.py:318
  17.8 1.2 %collective-permute-start.7 = (f32[384,128]{1,0:T(8,128)S(1)}, f32[384,128]{1,0:T(8,128)S(1)}, u32[]{:S(2)}, u32[]{:S(2)}) collective-permute-start(f32[384,128]{1,0:T(8,128)S(1)} %side_join_1.1.refs_0_.sent_ref.refs_5_.refs_9_), channel_id=1, source_target_pairs={{0,2},{1,3},{2,0},{3,1},{4,6},{5,7},{6,4},{7,5},{8,10},{9,11},{10,... | collective-permute-start | bytes 589832 | tf_op jit(solution)/shard_map/ppermute | solution.py:318
  19.0 0.9 %collective-permute-done.2.sib_ref.refs_2_ = f32[160,128]{1,0:T(8,128)S(1)} collective-permute-done((f32[160,128]{1,0:T(8,128)S(1)}, f32[160,128]{1,0:T(8,128)S(1)}, u32[]{:S(2)}, u32[]{:S(2)}) %collective-permute-start.2) | collective-permute-done | bytes 81952 | tf_op jit(solution)/shard_map/ppermute | solution.py:318
  19.9 0.4 %level_2.1 = (f32[128,128]{1,0:T(8,128)S(1)}, f32[64,128]{1,0:T(8,128)S(1)}) custom-call(f32[160,128]{1,0:T(8,128)S(1)} %get-tuple-element.35.own_ref, f32[160,128]{1,0:T(8,128)S(1)} %collective-permute-done.2.sib_ref.refs_2_, f32[4,128,128]{2,1,0:T(8,128)S(1)} %get-tuple-element.31.nodes_ref, f32[384,128]{1,0:T(8,128)S(1)} %side_join_1.1.refs_0_.sent_ref.refs_5_.refs_9_), custom_call_target="tpu_custom_call" | custom-call | flops 20000000000 | bytes 1048576 | tf_op jit(solution)/shard_map/level_2/pallas_call | solution.py:348
  20.2 2.8 %collective-permute-start.6 = (f32[64,128]{1,0:T(8,128)S(1)}, f32[64,128]{1,0:T(8,128)S(1)}, u32[]{:S(2)}, u32[]{:S(2)}) collective-permute-start(f32[64,128]{1,0:T(8,128)S(1)} %get-tuple-element.45.own_ref), channel_id=1, source_target_pairs={{0,8},{1,9},{2,10},{3,11},{4,12},{5,13},{6,14},{7,15},{8,0},{9,1},... | collective-permute-start | bytes 98312 | tf_op jit(solution)/shard_map/ppermute | solution.py:318
  23.0 0.5 %collective-permute-done.7.got_ref.refs_6_.refs_10_ = f32[384,128]{1,0:T(8,128)S(1)} collective-permute-done((f32[384,128]{1,0:T(8,128)S(1)}, f32[384,128]{1,0:T(8,128)S(1)}, u32[]{:S(2)}, u32[]{:S(2)}) %collective-permute-start.7) | collective-permute-done | bytes 196640 | tf_op jit(solution)/shard_map/ppermute | solution.py:318
  23.5 1.7 %collective-permute-start.9 = (f32[96,128]{1,0:T(8,128)S(1)}, f32[96,128]{1,0:T(8,128)S(1)}, u32[]{:S(2)}, u32[]{:S(2)}) collective-permute-start(f32[96,128]{1,0:T(8,128)S(1)} %side_top.1.refs_0_.refs_11_), channel_id=1, source_target_pairs={{0,4},{1,5},{2,6},{3,7},{4,0},{5,1},{6,2},{7,3},{8,12},{9,13},{10,... | collective-permute-start | bytes 147464 | tf_op jit(solution)/shard_map/ppermute | solution.py:318
  25.2 0.0 collective-permute-done.6.sib_ref.refs_3_
  25.2 0.2 level_3.1.refs_3_.refs_7_
  25.5 0.1 collective-permute-start.8
  25.5 2.1 %collective-permute-done.9.refs_12_ = f32[96,128]{1,0:T(8,128)S(1)} collective-permute-done((f32[96,128]{1,0:T(8,128)S(1)}, f32[96,128]{1,0:T(8,128)S(1)}, u32[]{:S(2)}, u32[]{:S(2)}) %collective-permute-start.9) | collective-permute-done | bytes 49184 | tf_op jit(solution)/shard_map/ppermute | solution.py:318
  27.7 0.3 end_factors.1
  27.9 0.1 collective-permute-start.10
  28.0 0.0 collective-permute-done.8.other_ref.low_other
  28.0 1.3 %solution_rows.1.x_ref = f32[2048,256]{1,0:T(8,128)S(1)} custom-call(s32[8,128]{1,0:T(8,128)S(1)} %broadcast_in_dim.9.count_ref, f32[448,128]{1,0:T(8,128)S(1)} %get-tuple-element.46.own_ref.low_own, f32[448,128]{1,0:T(8,128)S(1)} %collective-permute-done.8.other_ref.low_other, f32[2048,256]{1,0:T(8,128)S(1)} %get-tuple-element.50.x_ref, ...), custom_call_target="tpu_custom_call" | custom-call | flops 2000000000 | bytes 1048576 | tf_op jit(solution)/shard_map/solution_rows/pallas_call | solution.py:348
  29.4 0.0 collective-permute-done.10.top_other
  29.4 2.7 %factor_rows.1 = (f32[2048,256]{1,0:T(8,128)}, bf16[256,2048]{1,0:T(8,128)(2,1)}, bf16[256,2048]{1,0:T(8,128)(2,1)}) custom-call(s32[8,128]{1,0:T(8,128)S(1)} %broadcast_in_dim.9.count_ref, f32[448,128]{1,0:T(8,128)S(1)} %get-tuple-element.46.own_ref.low_own, f32[448,128]{1,0:T(8,128)S(1)} %collective-permute-done.8.other_ref.low_other, ...), custom_call_target="tpu_custom_call" | custom-call | tf_op jit(solution)/shard_map/factor_rows/pallas_call | solution.py:348
  (5 shorter events, 0.1 us)
Async XLA Ops:
  5.3 1.8 %collective-permute-start = (f32[448,128]{1,0:T(8,128)S(1)}, f32[448,128]{1,0:T(8,128)S(1)}, u32[]{:S(2)}, u32[]{:S(2)}) collective-permute-start(f32[448,128]{1,0:T(8,128)S(1)} %get-tuple-element.30), channel_id=1, source_target_pairs={{0,1},{1,0},{2,3},{3,2},{4,5},{5,4},{6,7},{7,6},{8,9},{9,8},{10,11... | collective-permute-start | bytes 688136 | tf_op jit(solution)/shard_map/ppermute | solution.py:318
  7.6 3.1 %collective-permute-start.3 = (f32[576,128]{1,0:T(8,128)S(1)}, f32[576,128]{1,0:T(8,128)S(1)}, u32[]{:S(2)}, u32[]{:S(2)}) collective-permute-start(f32[576,128]{1,0:T(8,128)S(1)} %get-tuple-element.40), channel_id=1, source_target_pairs={{0,1},{1,0},{2,3},{3,2},{4,5},{5,4},{6,7},{7,6},{8,9},{9,8},{10,11... | collective-permute-start | bytes 884744 | tf_op jit(solution)/shard_map/ppermute | solution.py:318
  7.9 7.1 %collective-permute-start.1 = (f32[288,128]{1,0:T(8,128)S(1)}, f32[288,128]{1,0:T(8,128)S(1)}, u32[]{:S(2)}, u32[]{:S(2)}) collective-permute-start(f32[288,128]{1,0:T(8,128)S(1)} %get-tuple-element.33.own_ref), channel_id=1, source_target_pairs={{0,2},{1,3},{2,0},{3,1},{4,6},{5,7},{6,4},{7,5},{8,10},{9,11},{10,... | collective-permute-start | bytes 442376 | tf_op jit(solution)/shard_map/ppermute | solution.py:318
  10.7 6.4 %collective-permute-start.5 = (f32[96,128]{1,0:T(8,128)S(1)}, f32[96,128]{1,0:T(8,128)S(1)}, u32[]{:S(2)}, u32[]{:S(2)}) collective-permute-start(f32[96,128]{1,0:T(8,128)S(1)} %get-tuple-element.43), channel_id=1, source_target_pairs={{0,8},{1,9},{2,10},{3,11},{4,12},{5,13},{6,14},{7,15},{8,0},{9,1},... | collective-permute-start | bytes 147464 | tf_op jit(solution)/shard_map/ppermute | solution.py:318
  13.4 4.3 %collective-permute-start.4 = (f32[128,128]{1,0:T(8,128)S(1)}, f32[128,128]{1,0:T(8,128)S(1)}, u32[]{:S(2)}, u32[]{:S(2)}) collective-permute-start(f32[128,128]{1,0:T(8,128)S(1)} %get-tuple-element.42.sent_ref), channel_id=1, source_target_pairs={{0,4},{1,5},{2,6},{3,7},{4,0},{5,1},{6,2},{7,3},{8,12},{9,13},{10,... | collective-permute-start | bytes 196616 | tf_op jit(solution)/shard_map/ppermute | solution.py:318
  15.4 4.5 %collective-permute-start.2 = (f32[160,128]{1,0:T(8,128)S(1)}, f32[160,128]{1,0:T(8,128)S(1)}, u32[]{:S(2)}, u32[]{:S(2)}) collective-permute-start(f32[160,128]{1,0:T(8,128)S(1)} %get-tuple-element.35.own_ref), channel_id=1, source_target_pairs={{0,4},{1,5},{2,6},{3,7},{4,0},{5,1},{6,2},{7,3},{8,12},{9,13},{10,... | collective-permute-start | bytes 245768 | tf_op jit(solution)/shard_map/ppermute | solution.py:318
  17.8 5.7 %collective-permute-start.7 = (f32[384,128]{1,0:T(8,128)S(1)}, f32[384,128]{1,0:T(8,128)S(1)}, u32[]{:S(2)}, u32[]{:S(2)}) collective-permute-start(f32[384,128]{1,0:T(8,128)S(1)} %side_join_1.1.refs_0_.sent_ref.refs_5_.refs_9_), channel_id=1, source_target_pairs={{0,2},{1,3},{2,0},{3,1},{4,6},{5,7},{6,4},{7,5},{8,10},{9,11},{10,... | collective-permute-start | bytes 589832 | tf_op jit(solution)/shard_map/ppermute | solution.py:318
  20.2 5.0 %collective-permute-start.6 = (f32[64,128]{1,0:T(8,128)S(1)}, f32[64,128]{1,0:T(8,128)S(1)}, u32[]{:S(2)}, u32[]{:S(2)}) collective-permute-start(f32[64,128]{1,0:T(8,128)S(1)} %get-tuple-element.45.own_ref), channel_id=1, source_target_pairs={{0,8},{1,9},{2,10},{3,11},{4,12},{5,13},{6,14},{7,15},{8,0},{9,1},... | collective-permute-start | bytes 98312 | tf_op jit(solution)/shard_map/ppermute | solution.py:318
  23.5 4.2 %collective-permute-start.9 = (f32[96,128]{1,0:T(8,128)S(1)}, f32[96,128]{1,0:T(8,128)S(1)}, u32[]{:S(2)}, u32[]{:S(2)}) collective-permute-start(f32[96,128]{1,0:T(8,128)S(1)} %side_top.1.refs_0_.refs_11_), channel_id=1, source_target_pairs={{0,4},{1,5},{2,6},{3,7},{4,0},{5,1},{6,2},{7,3},{8,12},{9,13},{10,... | collective-permute-start | bytes 147464 | tf_op jit(solution)/shard_map/ppermute | solution.py:318
  25.5 2.6 %collective-permute-start.8 = (f32[448,128]{1,0:T(8,128)S(1)}, f32[448,128]{1,0:T(8,128)S(1)}, u32[]{:S(2)}, u32[]{:S(2)}) collective-permute-start(f32[448,128]{1,0:T(8,128)S(1)} %get-tuple-element.47), channel_id=1, source_target_pairs={{0,1},{1,0},{2,3},{3,2},{4,5},{5,4},{6,7},{7,6},{8,9},{9,8},{10,11... | collective-permute-start | bytes 688136 | tf_op jit(solution)/shard_map/ppermute | solution.py:318
  27.9 1.5 %collective-permute-start.10 = (f32[320,128]{1,0:T(8,128)S(1)}, f32[320,128]{1,0:T(8,128)S(1)}, u32[]{:S(2)}, u32[]{:S(2)}) collective-permute-start(f32[320,128]{1,0:T(8,128)S(1)} %get-tuple-element.49), channel_id=1, source_target_pairs={{0,1},{1,0},{2,3},{3,2},{4,5},{5,4},{6,7},{7,6},{8,9},{9,8},{10,11... | collective-permute-start | bytes 491528 | tf_op jit(solution)/shard_map/ppermute | solution.py:318

commit v4 on v3

--- a/solution.py
+++ b/solution.py
@@ -52,6 +52,15 @@
     return rank + pack_rows(levels - 1 - level, rank)
 
 
+def holds_first():
+    return lax.axis_index("leaf") % 2 == 0
+
+
+def half_lanes(own, half):
+    lane = jnp.where(holds_first(), 0 if own else half, half if own else 0)
+    return pl.ds(pl.multiple_of(lane, half), half)
+
+
 def row_parts(row_count):
     eighth = row_count // 8
     if eighth % 128:
@@ -62,7 +71,7 @@
 
 def write_state(keep, send, acc, rank, blocks_of):
     half = acc.shape[1] // 2
-    is_first = lax.axis_index("leaf") % 2 == 0
+    is_first = holds_first()
     at = 0
     for k in range(acc.shape[0] // rank):
         low = acc[k * rank : (k + 1) * rank, :half]
@@ -211,60 +220,46 @@
 
 
 def end_low_kernel(dims, pair, *refs):
-    levels, rank, scale = dims
-    z_refs, (sib_side, side_sent, side_got, own_side) = refs[:levels], refs[levels : levels + 4]
-    out_refs = refs[levels + 4 :]
-    for n, out_ref in enumerate(out_refs):
-        crossed = pair and n == 0
-        at = 0
-        for k in range(levels):
-            z = z_refs[k][rank:, :] if crossed and k == 0 else z_refs[k][:rank, :]
-            out_ref[k * rank : (k + 1) * rank, :] = z
-            if k == levels - 1:
-                continue
-            if k == 0:
-                term = (own_side if crossed else sib_side)[:rank, :]
-            else:
-                term = side_got[at : at + rank, :]
-                if k > 1:
-                    term = term + side_sent[at : at + rank, :]
-                at += side_rows(k, levels, rank)
-            out_ref[(levels + k) * rank : (levels + k + 1) * rank, :] = term * scale
-
-
-def end_kernel(dims, pair, *refs):
     levels, rank, _ = dims
-    solves, z_refs = refs[:levels], refs[levels : 2 * levels]
-    sib_side, side_sent, side_got, top_sent, top_got, own_solve, own_side = refs[2 * levels : 2 * levels + 7]
-    *out_refs, side_sum, top_side = refs[2 * levels + 7 :]
-    top_side[...] = top_sent[...] + top_got[...]
+    solves, z_refs = refs[: levels - 1], refs[levels - 1 : 2 * levels - 1]
+    sib_side, side_sent, side_got, own_solve, own_side = refs[2 * levels - 1 : 2 * levels + 4]
+    *out_refs, side_sum = refs[2 * levels + 4 :]
     z_own = [z_ref[:rank, :] for z_ref in z_refs]
 
-    low = side_rows(1, levels, rank)
-    rows = side_sum.shape[0]
+    low, rows = side_rows(1, levels, rank), side_sum.shape[0]
     side_sum[:low, :] = side_got[:low, :]
     side_sum[low:, :] = side_got[low:rows, :] + side_sent[low:rows, :]
+
+    def write(out_ref, k, z_term, l_term, k_term):
+        out_ref[k * rank : (k + 1) * rank, :] = z_term
+        out_ref[(levels + k) * rank : (levels + k + 1) * rank, :] = l_term
+        out_ref[(2 * levels - 1 + k) * rank : (2 * levels + k) * rank, :] = k_term
+
     at = 0
-    for k in range(levels):
-        where = (side_sum, at)
-        if k == 0:
-            where = (sib_side, 0)
-        elif k == levels - 1:
-            where = (top_side, 0)
-        else:
-            at += side_rows(k, levels, rank)
-        l_term, k_term = factor_terms(dims, k, solves[k][:rank, :], *where, z_refs[k][rank:, :], z_own[k + 1 :])
-        out_refs[-1][k * rank : (k + 1) * rank, :] = l_term
+    for k in range(levels - 1):
+        z_sib = z_refs[k][rank:, :]
+        where = (sib_side, 0) if k == 0 else (side_sum, at)
+        at += side_rows(k, levels, rank) if k > 0 else 0
+        parts = (z_own[k], *factor_terms(dims, k, solves[k][:rank, :], *where, z_sib, z_own[k + 1 :]))
+        write(out_refs[-1], k, *parts)
         if pair:
             if k == 0:
-                l_term, _ = factor_terms(dims, 0, own_solve[:rank, :], own_side, 0, z_own[0], z_own[1:])
-            out_refs[0][k * rank : (k + 1) * rank, :] = l_term
+                parts = (z_sib, *factor_terms(dims, 0, own_solve[:rank, :], own_side, 0, z_own[0], z_own[1:]))
+            write(out_refs[0], k, *parts)
     for out_ref in out_refs:
-        out_ref[levels * rank :, :] = k_term
+        out_ref[(levels - 1) * rank : levels * rank, :] = z_own[-1]
+
+
+def end_top_kernel(dims, solve_ref, z_ref, sent_ref, got_ref, out_ref, side_ref):
+    levels, rank, _ = dims
+    side_ref[...] = sent_ref[...] + got_ref[...]
+    l_term, k_term = factor_terms(dims, levels - 1, solve_ref[:rank, :], side_ref, 0, z_ref[rank:, :], [])
+    out_ref[:rank, :] = l_term
+    out_ref[rank:, :] = k_term
 
 
 def whole(own_ref, other_ref, start, rows):
-    is_first = lax.axis_index("leaf") % 2 == 0
+    is_first = holds_first()
     own, other = own_ref[start : start + rows, :], other_ref[start : start + rows, :]
     return jnp.concatenate([jnp.where(is_first, own, other), jnp.where(is_first, other, own)], 1)
 
@@ -283,31 +278,56 @@
             copy.wait()
 
 
-def solution_kernel(dims, count_ref, own_ref, other_ref, x_ref, q_ref, sol):
-    wide, chunk = dims
-    z = whole(own_ref, other_ref, 0, wide)
+def halves(value):
+    high = value.astype(jnp.bfloat16)
+    return high, (value - high.astype(F32)).astype(jnp.bfloat16)
+
+
+def solution_kernel(dims, count_ref, x_ref, q_ref, *refs):
+    own, rank, chunk = dims
+    *z_refs, sol = refs
+    half = sol.shape[1]
+    if own:
+        z = jnp.concatenate([z_ref[:rank, :] for z_ref in z_refs], 0)
+    else:
+        z = z_refs[0][: q_ref.shape[0], :]
+    z_high, z_low = halves(z)
+    z_both = jnp.concatenate([z_high, z_low], 1)
+    lanes = half_lanes(own, half)
+    dims = (((0,), (0,)), ((), ()))
     for i in range(x_ref.shape[0] // chunk):
         part = slice(i * chunk, (i + 1) * chunk)
         live = i * chunk + lax.broadcasted_iota(jnp.int32, (chunk, 1), 0) < count_ref[:1, :1]
-        x = x_ref[part, :] - dot(q_ref[:, part], z, ((0,), (0,)))
+        q_high, q_low = halves(q_ref[:, part])
+        both = lax.dot_general(q_high, z_both, dims, preferred_element_type=F32)
+        rest = lax.dot_general(q_low, z_high, dims, preferred_element_type=F32)
+        x = x_ref[part, lanes] - (both[:, :half] + (both[:, half:] + rest))
         sol[part, :] = jnp.where(live, x, 0.0)
 
 
-def factor_kernel(dims, count_ref, low_own, low_other, top_own, top_other, x_ref, w_ref, *refs):
+def factor_kernel(dims, count_ref, low_own, low_other, top_own, top_other, x_own, x_other, w_ref, *refs):
     wide, chunk = dims
     sol_out, left_out, right_out, left, right, sems = refs
     sender = Sender(sems)
-    sender.send(x_ref, sol_out)
-    low = low_own.shape[0] - wide
-    l = whole(top_own, top_other, 0, wide)
-    k = jnp.concatenate([whole(low_own, low_other, wide, low), whole(top_own, top_other, wide, wide - low)], 0)
-    for i in range(x_ref.shape[0] // chunk):
+    half = x_own.shape[1]
+    sender.send(x_own, sol_out.at[:, half_lanes(True, half)])
+    sender.send(x_other, sol_out.at[:, half_lanes(False, half)])
+    rank = top_own.shape[0] // 2
+    low = wide - rank
+
+    def joined(own_ref, other_ref, start, rows):
+        return jnp.concatenate([own_ref[start : start + rows, :], other_ref[start : start + rows, :]], 1)
+
+    l = jnp.concatenate([whole(low_own, low_other, wide, low), whole(top_own, top_other, 0, rank)], 0)
+    k = jnp.concatenate([joined(low_own, low_other, wide + low, low), joined(top_own, top_other, rank, rank)], 0)
+    for i in range(w_ref.shape[0] // chunk):
         part, place = slice(i * chunk, (i + 1) * chunk), pl.ds(i * chunk, chunk)
         live = i * chunk + lax.broadcasted_iota(jnp.int32, (1, chunk), 1) < count_ref[:1, :1]
         left_now = dot(l, w_ref[part, :], ((1,), (1,)))
         left[:, part] = jnp.where(live, left_now, 0.0).astype(left.dtype)
         sender.send(left.at[:, place], left_out.at[:, place])
-        right[:, part] = dot(k, x_ref[part, :], ((1,), (1,))).astype(right.dtype)
+        x = jnp.concatenate([x_own[part, :], x_other[part, :]], 1)
+        right[:, part] = dot(k, x, ((1,), (1,))).astype(right.dtype)
         sender.send(right.at[:, place], right_out.at[:, place])
     sender.wait()
 
@@ -468,43 +488,51 @@
     *low_other, low_own = call(
         functools.partial(end_low_kernel, dims, pair),
         "end_low",
-        [shape(wide + low, half)] * copies,
+        [shape(wide + 2 * low, half)] * copies,
+        *solves[:top],
         *zs,
         sib_side,
         sent,
         got,
+        own_solve,
         side,
+        scratch=[pltpu.VMEM((sum(n_side[1:top]), half), F32)],
     )
     low_other = swapped(low_other[0] if pair else low_own, 0)
-    *top_other, top_own = call(
-        functools.partial(end_kernel, dims, pair),
-        "end_factors",
-        [shape(wide + rank, half)] * copies,
-        *solves,
-        *zs,
-        sib_side,
-        sent,
-        got,
+    top_own = call(
+        functools.partial(end_top_kernel, dims),
+        "end_top",
+        shape(order, half),
+        solves[top],
+        zs[top],
         top_sum,
         top_got,
-        own_solve,
-        side,
-        scratch=[pltpu.VMEM((sum(n_side[1:top]), half), F32), pltpu.VMEM((n_side[top], half), F32)],
+        scratch=[pltpu.VMEM((n_side[top], half), F32)],
         cost=2 * 10**10,
     )
-    top_other = swapped(top_other[0] if pair else top_own, 0)
-
-    sol_vmem = call(
-        functools.partial(solution_kernel, (wide, chunk)),
-        "solution_rows",
-        shape(row_count, col_count),
+    top_other = swapped(top_own, 0)
+
+    sol_own = call(
+        functools.partial(solution_kernel, (True, rank, chunk)),
+        "solution_own",
+        shape(row_count, half),
         count,
-        low_own,
-        low_other,
         x_vmem,
         q_vmem,
+        *zs,
         params=large,
-        cost=2 * 10**9,
+        cost=10**9,
+    )
+    sol_other = call(
+        functools.partial(solution_kernel, (False, rank, chunk)),
+        "solution_other",
+        shape(row_count, half),
+        count,
+        x_vmem,
+        q_vmem,
+        low_other,
+        params=large,
+        cost=10**9,
     )
     grad = shape(wide, row_count, dtype=jnp.bfloat16)
     sol, left, right = call(
@@ -516,10 +544,11 @@
         low_other,
         top_own,
         top_other,
-        sol_vmem,
+        sol_own,
+        sol_other,
         w_vmem,
         out_specs=[anywhere] * 3,
-        scratch=[pltpu.VMEM(grad.shape, grad.dtype)] * 2 + [pltpu.SemaphoreType.DMA((2 * steps + 1,))],
+        scratch=[pltpu.VMEM(grad.shape, grad.dtype)] * 2 + [pltpu.SemaphoreType.DMA((2 * steps + 2,))],
         params=large,
     )
     return sol, left.reshape(coeff_basis.shape), right.reshape(coeff_basis.shape)

time: 32.3 us -> 31.8 us (0.985)
  waiting for transfers between devices: 4.09 us -> 2.77 us
  Pallas kernels: 11.1 us -> 11.8 us
    ppermute x11, waiting for transfers between devices: 4.09 us -> 2.77 us  [swapped(): return lax.ppermute(value, 'leaf', pairs)]
    pallas_call x13 -> x14, Pallas kernels: 7.06 us -> 7.82 us  [call(): pl.pallas_call(kernel, out_shape=out_shape, in_specs=[vmem] * len(operand...]
  transfers between devices with their start and end apart: 11 -> 11, of which waited for: 4 -> 6; matrix products, arithmetic and copies ran while one was open for 0% -> 0% of each run, Pallas kernels for 12% -> 15%
where the time goes in v4:
time: 31.8 us; the launch traced here: 31.6 us
  starting transfers between devices  15.6 us (49%)
  Pallas kernels  11.8 us (37%)
  waiting for transfers between devices  2.77 us (9%)
  between operations  1.41 us (4%)
    ppermute x11, starting transfers between devices, swapped(): return lax.ppermute(value, 'leaf', pairs)  15.6 us
    pallas_call x14, Pallas kernels, call(): pl.pallas_call(kernel, out_shape=out_shape, in_specs=[vmem] * len(operand...  7.82 us
    pallas_call x1, Pallas kernels, body(): pl.pallas_call(functools.partial(local_kernel, (levels, rank, base_bits),...  3.99 us
    ppermute x11, waiting for transfers between devices, swapped(): return lax.ppermute(value, 'leaf', pairs)  2.77 us
  transfers between devices with their start and end apart: 11, of which 6 were waited for; matrix products, arithmetic and copies ran while one was open for 0% of the time, Pallas kernels for 15%

profile of v4, /device:TPU:0, one launch (start us, length us, event | category | flops | bytes accessed | tf_op | source)
XLA Modules:
  0.0 31.6 jit_solution(12895480399509021571)
XLA Ops:
  1.3 4.0 %local_sums.1 = (f32[448,128]{1,0:T(8,128)S(1)}, f32[448,128]{1,0:T(8,128)S(1)}, f32[256,256]{1,0:T(8,128)S(1)}, f32[4,128,128]{2,1,0:T(8,128)S(1)}, f32[2048,25...) custom-call(s32[8,128]{1,0:T(8,128)S(1)} %broadcast_in_dim.9.count_ref, ...), custom_call_target="tpu_custom_call" | custom-call | tf_op jit(solution)/shard_map/local_sums/pallas_call | solution.py:386
  5.3 0.5 %collective-permute-start = (f32[448,128]{1,0:T(8,128)S(1)}, f32[448,128]{1,0:T(8,128)S(1)}, u32[]{:S(2)}, u32[]{:S(2)}) collective-permute-start(f32[448,128]{1,0:T(8,128)S(1)} %get-tuple-element.27), channel_id=1, source_target_pairs={{0,1},{1,0},{2,3},{3,2},{4,5},{5,4},{6,7},{7,6},{8,9},{9,8},{10,11... | collective-permute-start | bytes 688136 | tf_op jit(solution)/shard_map/ppermute | solution.py:338
  5.8 1.3 %side_sums.1.k_ref = f32[256,256]{1,0:T(8,128)S(1)} custom-call(s32[8,128]{1,0:T(8,128)S(1)} %broadcast_in_dim.9.count_ref, f32[2048,256]{1,0:T(8,128)S(1)} %get-tuple-element.34.w_ref, f32[256,2048]{1,0:T(8,128)S(1)} %get-tuple-element.35.u_ref), custom_call_target="tpu_custom_call" | custom-call | flops 805306368 | bytes 1048576 | tf_op jit(solution)/shard_map/side_sums/pallas_call | solution.py:368
  7.1 0.0 collective-permute-done.sib_ref.refs_0_
  7.1 0.4 %level_0.1 = (f32[128,128]{1,0:T(8,128)S(1)}, f32[288,128]{1,0:T(8,128)S(1)}) custom-call(f32[448,128]{1,0:T(8,128)S(1)} %get-tuple-element.28.own_ref.refs_10_, f32[448,128]{1,0:T(8,128)S(1)} %collective-permute-done.sib_ref.refs_0_, f32[4,128,128]{2,1,0:T(8,128)S(1)} %get-tuple-element.29.nodes_ref), custom_call_target="tpu_custom_call" | custom-call | flops 20000000000 | bytes 1048576 | tf_op jit(solution)/shard_map/level_0/pallas_call | solution.py:368
  7.5 0.1 side_state.1
  7.6 0.3 collective-permute-start.3
  7.9 2.8 %collective-permute-start.1 = (f32[288,128]{1,0:T(8,128)S(1)}, f32[288,128]{1,0:T(8,128)S(1)}, u32[]{:S(2)}, u32[]{:S(2)}) collective-permute-start(f32[288,128]{1,0:T(8,128)S(1)} %get-tuple-element.30.own_ref), channel_id=1, source_target_pairs={{0,2},{1,3},{2,0},{3,1},{4,6},{5,7},{6,4},{7,5},{8,10},{9,11},{10,... | collective-permute-start | bytes 442376 | tf_op jit(solution)/shard_map/ppermute | solution.py:338
  10.7 0.0 collective-permute-done.3.sib_ref.refs_7_
  10.7 1.6 %collective-permute-start.4 = (f32[128,128]{1,0:T(8,128)S(1)}, f32[128,128]{1,0:T(8,128)S(1)}, u32[]{:S(2)}, u32[]{:S(2)}) collective-permute-start(f32[128,128]{1,0:T(8,128)S(1)} %get-tuple-element.40.sent_ref), channel_id=1, source_target_pairs={{0,4},{1,5},{2,6},{3,7},{4,0},{5,1},{6,2},{7,3},{8,12},{9,13},{10,... | collective-permute-start | bytes 196616 | tf_op jit(solution)/shard_map/ppermute | solution.py:338
  12.4 2.6 %collective-permute-start.5 = (f32[96,128]{1,0:T(8,128)S(1)}, f32[96,128]{1,0:T(8,128)S(1)}, u32[]{:S(2)}, u32[]{:S(2)}) collective-permute-start(f32[96,128]{1,0:T(8,128)S(1)} %get-tuple-element.41), channel_id=1, source_target_pairs={{0,8},{1,9},{2,10},{3,11},{4,12},{5,13},{6,14},{7,15},{8,0},{9,1},... | collective-permute-start | bytes 147464 | tf_op jit(solution)/shard_map/ppermute | solution.py:338
  15.0 0.0 collective-permute-done.1.sib_ref.refs_1_
  15.0 0.4 %level_1.1 = (f32[128,128]{1,0:T(8,128)S(1)}, f32[160,128]{1,0:T(8,128)S(1)}) custom-call(f32[288,128]{1,0:T(8,128)S(1)} %get-tuple-element.30.own_ref, f32[288,128]{1,0:T(8,128)S(1)} %collective-permute-done.1.sib_ref.refs_1_, f32[4,128,128]{2,1,0:T(8,128)S(1)} %get-tuple-element.29.nodes_ref), custom_call_target="tpu_custom_call" | custom-call | flops 20000000000 | bytes 1048576 | tf_op jit(solution)/shard_map/level_1/pallas_call | solution.py:368
  15.3 1.8 %collective-permute-start.2 = (f32[160,128]{1,0:T(8,128)S(1)}, f32[160,128]{1,0:T(8,128)S(1)}, u32[]{:S(2)}, u32[]{:S(2)}) collective-permute-start(f32[160,128]{1,0:T(8,128)S(1)} %get-tuple-element.31.own_ref), channel_id=1, source_target_pairs={{0,4},{1,5},{2,6},{3,7},{4,0},{5,1},{6,2},{7,3},{8,12},{9,13},{10,... | collective-permute-start | bytes 245768 | tf_op jit(solution)/shard_map/ppermute | solution.py:338
  17.1 0.3 %collective-permute-done.5.refs_0_ = f32[96,128]{1,0:T(8,128)S(1)} collective-permute-done((f32[96,128]{1,0:T(8,128)S(1)}, f32[96,128]{1,0:T(8,128)S(1)}, u32[]{:S(2)}, u32[]{:S(2)}) %collective-permute-start.5) | collective-permute-done | bytes 49184 | tf_op jit(solution)/shard_map/ppermute | solution.py:338
  17.5 0.0 collective-permute-done.4.got_ref
  17.5 1.6 %collective-permute-start.7 = (f32[384,128]{1,0:T(8,128)S(1)}, f32[384,128]{1,0:T(8,128)S(1)}, u32[]{:S(2)}, u32[]{:S(2)}) collective-permute-start(f32[384,128]{1,0:T(8,128)S(1)} %side_join_1.1.refs_0_.sent_ref.refs_8_), channel_id=1, source_target_pairs={{0,2},{1,3},{2,0},{3,1},{4,6},{5,7},{6,4},{7,5},{8,10},{9,11},{10,... | collective-permute-start | bytes 589832 | tf_op jit(solution)/shard_map/ppermute | solution.py:338
  19.1 0.8 %collective-permute-done.2.sib_ref.refs_2_ = f32[160,128]{1,0:T(8,128)S(1)} collective-permute-done((f32[160,128]{1,0:T(8,128)S(1)}, f32[160,128]{1,0:T(8,128)S(1)}, u32[]{:S(2)}, u32[]{:S(2)}) %collective-permute-start.2) | collective-permute-done | bytes 81952 | tf_op jit(solution)/shard_map/ppermute | solution.py:338
  19.9 0.4 %level_2.1 = (f32[128,128]{1,0:T(8,128)S(1)}, f32[64,128]{1,0:T(8,128)S(1)}) custom-call(f32[160,128]{1,0:T(8,128)S(1)} %get-tuple-element.31.own_ref, f32[160,128]{1,0:T(8,128)S(1)} %collective-permute-done.2.sib_ref.refs_2_, f32[4,128,128]{2,1,0:T(8,128)S(1)} %get-tuple-element.29.nodes_ref, f32[384,128]{1,0:T(8,128)S(1)} %side_join_1.1.refs_0_.sent_ref.refs_8_), custom_call_target="tpu_custom_call" | custom-call | flops 20000000000 | bytes 1048576 | tf_op jit(solution)/shard_map/level_2/pallas_call | solution.py:368
  20.2 2.8 %collective-permute-start.6 = (f32[64,128]{1,0:T(8,128)S(1)}, f32[64,128]{1,0:T(8,128)S(1)}, u32[]{:S(2)}, u32[]{:S(2)}) collective-permute-start(f32[64,128]{1,0:T(8,128)S(1)} %get-tuple-element.43.own_ref), channel_id=1, source_target_pairs={{0,8},{1,9},{2,10},{3,11},{4,12},{5,13},{6,14},{7,15},{8,0},{9,1},... | collective-permute-start | bytes 98312 | tf_op jit(solution)/shard_map/ppermute | solution.py:338
  23.0 0.2 collective-permute-done.7.got_ref.refs_9_
  23.2 1.4 %collective-permute-start.9 = (f32[96,128]{1,0:T(8,128)S(1)}, f32[96,128]{1,0:T(8,128)S(1)}, u32[]{:S(2)}, u32[]{:S(2)}) collective-permute-start(f32[96,128]{1,0:T(8,128)S(1)} %side_top.1.refs_0_.sent_ref), channel_id=1, source_target_pairs={{0,4},{1,5},{2,6},{3,7},{4,0},{5,1},{6,2},{7,3},{8,12},{9,13},{10,... | collective-permute-start | bytes 147464 | tf_op jit(solution)/shard_map/ppermute | solution.py:338
  24.7 0.4 %collective-permute-done.6.sib_ref.solve_ref = f32[64,128]{1,0:T(8,128)S(1)} collective-permute-done((f32[64,128]{1,0:T(8,128)S(1)}, f32[64,128]{1,0:T(8,128)S(1)}, u32[]{:S(2)}, u32[]{:S(2)}) %collective-permute-start.6) | collective-permute-done | bytes 32800 | tf_op jit(solution)/shard_map/ppermute | solution.py:338
  25.1 0.2 level_3.1.refs_6_.z_ref.refs_3_
  25.2 0.3 end_low.1
  25.5 0.1 collective-permute-start.8
  25.6 1.0 %solution_own.1.x_own = f32[2048,128]{1,0:T(8,128)S(1)} custom-call(s32[8,128]{1,0:T(8,128)S(1)} %broadcast_in_dim.9.count_ref, f32[2048,256]{1,0:T(8,128)S(1)} %get-tuple-element.46.x_ref, f32[256,2048]{1,0:T(8,128)S(1)} %get-tuple-element.47.q_ref, f32[128,128]{1,0:T(8,128)S(1)} %get-tuple-element.32.after_ref.refs_3_.refs_0_, ...), custom_call_target="tpu_custom_call" | custom-call | flops 1000000000 | bytes 1048576 | tf_op jit(solution)/shard_map/solution_own/pallas_call | solution.py:368
  26.6 0.8 %collective-permute-done.9.got_ref = f32[96,128]{1,0:T(8,128)S(1)} collective-permute-done((f32[96,128]{1,0:T(8,128)S(1)}, f32[96,128]{1,0:T(8,128)S(1)}, u32[]{:S(2)}, u32[]{:S(2)}) %collective-permute-start.9) | collective-permute-done | bytes 49184 | tf_op jit(solution)/shard_map/ppermute | solution.py:338
  27.4 0.2 end_top.1.top_own
  27.6 0.1 collective-permute-start.10
  27.7 0.0 collective-permute-done.8.refs_0_.low_other
  27.7 1.0 %solution_other.1.x_other = f32[2048,128]{1,0:T(8,128)S(1)} custom-call(s32[8,128]{1,0:T(8,128)S(1)} %broadcast_in_dim.9.count_ref, f32[2048,256]{1,0:T(8,128)S(1)} %get-tuple-element.46.x_ref, f32[256,2048]{1,0:T(8,128)S(1)} %get-tuple-element.47.q_ref, f32[640,128]{1,0:T(8,128)S(1)} %collective-permute-done.8.refs_0_.low_other), custom_call_target="tpu_custom_call" | custom-call | flops 1000000000 | bytes 1048576 | tf_op jit(solution)/shard_map/solution_other/pallas_call | solution.py:368
  28.7 0.3 collective-permute-done.10.top_other
  28.9 2.7 %factor_rows.1 = (f32[2048,256]{1,0:T(8,128)}, bf16[256,2048]{1,0:T(8,128)(2,1)}, bf16[256,2048]{1,0:T(8,128)(2,1)}) custom-call(s32[8,128]{1,0:T(8,128)S(1)} %broadcast_in_dim.9.count_ref, f32[640,128]{1,0:T(8,128)S(1)} %get-tuple-element.44.low_own, f32[640,128]{1,0:T(8,128)S(1)} %collective-permute-done.8.refs_0_.low_other, ...), custom_call_target="tpu_custom_call" | custom-call | tf_op jit(solution)/shard_map/factor_rows/pallas_call | solution.py:368
  (4 shorter events, 0.0 us)
Async XLA Ops:
  5.3 1.8 %collective-permute-start = (f32[448,128]{1,0:T(8,128)S(1)}, f32[448,128]{1,0:T(8,128)S(1)}, u32[]{:S(2)}, u32[]{:S(2)}) collective-permute-start(f32[448,128]{1,0:T(8,128)S(1)} %get-tuple-element.27), channel_id=1, source_target_pairs={{0,1},{1,0},{2,3},{3,2},{4,5},{5,4},{6,7},{7,6},{8,9},{9,8},{10,11... | collective-permute-start | bytes 688136 | tf_op jit(solution)/shard_map/ppermute | solution.py:338
  7.6 3.1 %collective-permute-start.3 = (f32[576,128]{1,0:T(8,128)S(1)}, f32[576,128]{1,0:T(8,128)S(1)}, u32[]{:S(2)}, u32[]{:S(2)}) collective-permute-start(f32[576,128]{1,0:T(8,128)S(1)} %get-tuple-element.38), channel_id=1, source_target_pairs={{0,1},{1,0},{2,3},{3,2},{4,5},{5,4},{6,7},{7,6},{8,9},{9,8},{10,11... | collective-permute-start | bytes 884744 | tf_op jit(solution)/shard_map/ppermute | solution.py:338
  7.9 7.1 %collective-permute-start.1 = (f32[288,128]{1,0:T(8,128)S(1)}, f32[288,128]{1,0:T(8,128)S(1)}, u32[]{:S(2)}, u32[]{:S(2)}) collective-permute-start(f32[288,128]{1,0:T(8,128)S(1)} %get-tuple-element.30.own_ref), channel_id=1, source_target_pairs={{0,2},{1,3},{2,0},{3,1},{4,6},{5,7},{6,4},{7,5},{8,10},{9,11},{10,... | collective-permute-start | bytes 442376 | tf_op jit(solution)/shard_map/ppermute | solution.py:338
  10.7 6.7 %collective-permute-start.4 = (f32[128,128]{1,0:T(8,128)S(1)}, f32[128,128]{1,0:T(8,128)S(1)}, u32[]{:S(2)}, u32[]{:S(2)}) collective-permute-start(f32[128,128]{1,0:T(8,128)S(1)} %get-tuple-element.40.sent_ref), channel_id=1, source_target_pairs={{0,4},{1,5},{2,6},{3,7},{4,0},{5,1},{6,2},{7,3},{8,12},{9,13},{10,... | collective-permute-start | bytes 196616 | tf_op jit(solution)/shard_map/ppermute | solution.py:338
  12.4 5.1 %collective-permute-start.5 = (f32[96,128]{1,0:T(8,128)S(1)}, f32[96,128]{1,0:T(8,128)S(1)}, u32[]{:S(2)}, u32[]{:S(2)}) collective-permute-start(f32[96,128]{1,0:T(8,128)S(1)} %get-tuple-element.41), channel_id=1, source_target_pairs={{0,8},{1,9},{2,10},{3,11},{4,12},{5,13},{6,14},{7,15},{8,0},{9,1},... | collective-permute-start | bytes 147464 | tf_op jit(solution)/shard_map/ppermute | solution.py:338
  15.3 4.5 %collective-permute-start.2 = (f32[160,128]{1,0:T(8,128)S(1)}, f32[160,128]{1,0:T(8,128)S(1)}, u32[]{:S(2)}, u32[]{:S(2)}) collective-permute-start(f32[160,128]{1,0:T(8,128)S(1)} %get-tuple-element.31.own_ref), channel_id=1, source_target_pairs={{0,4},{1,5},{2,6},{3,7},{4,0},{5,1},{6,2},{7,3},{8,12},{9,13},{10,... | collective-permute-start | bytes 245768 | tf_op jit(solution)/shard_map/ppermute | solution.py:338
  17.5 5.7 %collective-permute-start.7 = (f32[384,128]{1,0:T(8,128)S(1)}, f32[384,128]{1,0:T(8,128)S(1)}, u32[]{:S(2)}, u32[]{:S(2)}) collective-permute-start(f32[384,128]{1,0:T(8,128)S(1)} %side_join_1.1.refs_0_.sent_ref.refs_8_), channel_id=1, source_target_pairs={{0,2},{1,3},{2,0},{3,1},{4,6},{5,7},{6,4},{7,5},{8,10},{9,11},{10,... | collective-permute-start | bytes 589832 | tf_op jit(solution)/shard_map/ppermute | solution.py:338
  20.2 4.9 %collective-permute-start.6 = (f32[64,128]{1,0:T(8,128)S(1)}, f32[64,128]{1,0:T(8,128)S(1)}, u32[]{:S(2)}, u32[]{:S(2)}) collective-permute-start(f32[64,128]{1,0:T(8,128)S(1)} %get-tuple-element.43.own_ref), channel_id=1, source_target_pairs={{0,8},{1,9},{2,10},{3,11},{4,12},{5,13},{6,14},{7,15},{8,0},{9,1},... | collective-permute-start | bytes 98312 | tf_op jit(solution)/shard_map/ppermute | solution.py:338
  23.2 4.2 %collective-permute-start.9 = (f32[96,128]{1,0:T(8,128)S(1)}, f32[96,128]{1,0:T(8,128)S(1)}, u32[]{:S(2)}, u32[]{:S(2)}) collective-permute-start(f32[96,128]{1,0:T(8,128)S(1)} %side_top.1.refs_0_.sent_ref), channel_id=1, source_target_pairs={{0,4},{1,5},{2,6},{3,7},{4,0},{5,1},{6,2},{7,3},{8,12},{9,13},{10,... | collective-permute-start | bytes 147464 | tf_op jit(solution)/shard_map/ppermute | solution.py:338
  25.5 2.1 %collective-permute-start.8 = (f32[640,128]{1,0:T(8,128)S(1)}, f32[640,128]{1,0:T(8,128)S(1)}, u32[]{:S(2)}, u32[]{:S(2)}) collective-permute-start(f32[640,128]{1,0:T(8,128)S(1)} %get-tuple-element.45), channel_id=1, source_target_pairs={{0,1},{1,0},{2,3},{3,2},{4,5},{5,4},{6,7},{7,6},{8,9},{9,8},{10,11... | collective-permute-start | bytes 983048 | tf_op jit(solution)/shard_map/ppermute | solution.py:338
  27.6 1.3 %collective-permute-start.10 = (f32[128,128]{1,0:T(8,128)S(1)}, f32[128,128]{1,0:T(8,128)S(1)}, u32[]{:S(2)}, u32[]{:S(2)}) collective-permute-start(f32[128,128]{1,0:T(8,128)S(1)} %end_top.1.top_own), channel_id=1, source_target_pairs={{0,1},{1,0},{2,3},{3,2},{4,5},{5,4},{6,7},{7,6},{8,9},{9,8},{10,11... | collective-permute-start | bytes 196616 | tf_op jit(solution)/shard_map/ppermute | solution.py:338

commit v5 on v4

--- a/solution.py
+++ b/solution.py
@@ -221,9 +221,9 @@
 
 def end_low_kernel(dims, pair, *refs):
     levels, rank, _ = dims
-    solves, z_refs = refs[: levels - 1], refs[levels - 1 : 2 * levels - 1]
-    sib_side, side_sent, side_got, own_solve, own_side = refs[2 * levels - 1 : 2 * levels + 4]
-    *out_refs, side_sum = refs[2 * levels + 4 :]
+    solves, z_refs = refs[:levels], refs[levels : 2 * levels]
+    sib_side, side_sent, side_got, own_solve, own_side = refs[2 * levels : 2 * levels + 5]
+    *out_refs, side_sum = refs[2 * levels + 5 :]
     z_own = [z_ref[:rank, :] for z_ref in z_refs]
 
     low, rows = side_rows(1, levels, rank), side_sum.shape[0]
@@ -248,14 +248,14 @@
             write(out_refs[0], k, *parts)
     for out_ref in out_refs:
         out_ref[(levels - 1) * rank : levels * rank, :] = z_own[-1]
-
-
-def end_top_kernel(dims, solve_ref, z_ref, sent_ref, got_ref, out_ref, side_ref):
-    levels, rank, _ = dims
-    side_ref[...] = sent_ref[...] + got_ref[...]
-    l_term, k_term = factor_terms(dims, levels - 1, solve_ref[:rank, :], side_ref, 0, z_ref[rank:, :], [])
-    out_ref[:rank, :] = l_term
-    out_ref[rank:, :] = k_term
+        out_ref[(3 * levels - 2) * rank : (3 * levels - 1) * rank, :] = solves[-1][:rank, :]
+        out_ref[(3 * levels - 1) * rank :, :] = z_refs[-1][rank:, :]
+
+
+def end_top_kernel(sent_ref, got_ref, k_ref, h_ref):
+    rank = k_ref.shape[0]
+    k_ref[...] = sent_ref[:rank, :] + got_ref[:rank, :]
+    h_ref[...] = sent_ref[rank:, :] + got_ref[rank:, :]
 
 
 def whole(own_ref, other_ref, start, rows):
@@ -305,21 +305,21 @@
         sol[part, :] = jnp.where(live, x, 0.0)
 
 
-def factor_kernel(dims, count_ref, low_own, low_other, top_own, top_other, x_own, x_other, w_ref, *refs):
-    wide, chunk = dims
+def factor_kernel(dims, count_ref, low_own, low_other, k_own, k_other, h_ref, x_own, x_other, w_ref, *refs):
+    wide, scale, chunk = dims
     sol_out, left_out, right_out, left, right, sems = refs
     sender = Sender(sems)
     half = x_own.shape[1]
     sender.send(x_own, sol_out.at[:, half_lanes(True, half)])
     sender.send(x_other, sol_out.at[:, half_lanes(False, half)])
-    rank = top_own.shape[0] // 2
+    rank = k_own.shape[0]
     low = wide - rank
-
-    def joined(own_ref, other_ref, start, rows):
-        return jnp.concatenate([own_ref[start : start + rows, :], other_ref[start : start + rows, :]], 1)
-
-    l = jnp.concatenate([whole(low_own, low_other, wide, low), whole(top_own, top_other, 0, rank)], 0)
-    k = jnp.concatenate([joined(low_own, low_other, wide + low, low), joined(top_own, top_other, rank, rank)], 0)
+    at = wide + 2 * low
+    (block,) = unpack(h_ref, 0, 1, rank)
+    l_top = whole(low_own, low_other, at, rank) - dot(block, whole(low_own, low_other, at + rank, rank))
+    l = jnp.concatenate([whole(low_own, low_other, wide, low), l_top * scale], 0)
+    k_low = jnp.concatenate([low_own[wide + low : at, :], low_other[wide + low : at, :]], 1)
+    k = jnp.concatenate([k_low, jnp.concatenate([k_own[...], k_other[...]], 1) * scale], 0)
     for i in range(w_ref.shape[0] // chunk):
         part, place = slice(i * chunk, (i + 1) * chunk), pl.ds(i * chunk, chunk)
         live = i * chunk + lax.broadcasted_iota(jnp.int32, (1, chunk), 1) < count_ref[:1, :1]
@@ -488,8 +488,8 @@
     *low_other, low_own = call(
         functools.partial(end_low_kernel, dims, pair),
         "end_low",
-        [shape(wide + 2 * low, half)] * copies,
-        *solves[:top],
+        [shape(wide + 2 * low + order, half)] * copies,
+        *solves,
         *zs,
         sib_side,
         sent,
@@ -499,18 +499,15 @@
         scratch=[pltpu.VMEM((sum(n_side[1:top]), half), F32)],
     )
     low_other = swapped(low_other[0] if pair else low_own, 0)
-    top_own = call(
-        functools.partial(end_top_kernel, dims),
+    k_own, h_top = call(
+        end_top_kernel,
         "end_top",
-        shape(order, half),
-        solves[top],
-        zs[top],
+        [shape(rank, half), shape(n_side[top] - rank, half)],
         top_sum,
         top_got,
-        scratch=[pltpu.VMEM((n_side[top], half), F32)],
         cost=2 * 10**10,
     )
-    top_other = swapped(top_own, 0)
+    k_other = swapped(k_own, 0)
 
     sol_own = call(
         functools.partial(solution_kernel, (True, rank, chunk)),
@@ -536,14 +533,15 @@
     )
     grad = shape(wide, row_count, dtype=jnp.bfloat16)
     sol, left, right = call(
-        functools.partial(factor_kernel, (wide, chunk)),
+        functools.partial(factor_kernel, (wide, dims[2], chunk)),
         "factor_rows",
         [shape(row_count, col_count), grad, grad],
         count,
         low_own,
         low_other,
-        top_own,
-        top_other,
+        k_own,
+        k_other,
+        h_top,
         sol_own,
         sol_other,
         w_vmem,

time: 31.8 us -> 31.6 us (level)
  transfers between devices with their start and end apart: 11 -> 11, of which waited for: 6 -> 6; matrix products, arithmetic and copies ran while one was open for 0% -> 0% of each run, Pallas kernels for 15% -> 14%
where the time goes in v5:
time: 31.6 us; the launch traced here: 31.4 us
  starting transfers between devices  15.6 us (49%)
  Pallas kernels  11.7 us (37%)
  waiting for transfers between devices  2.72 us (9%)
  between operations  1.41 us (4%)
    ppermute x11, starting transfers between devices, swapped(): return lax.ppermute(value, 'leaf', pairs)  15.6 us
    pallas_call x14, Pallas kernels, call(): pl.pallas_call(kernel, out_shape=out_shape, in_specs=[vmem] * len(operand...  7.72 us
    pallas_call x1, Pallas kernels, body(): pl.pallas_call(functools.partial(local_kernel, (levels, rank, base_bits),...  3.99 us
    ppermute x11, waiting for transfers between devices, swapped(): return lax.ppermute(value, 'leaf', pairs)  2.72 us
  transfers between devices with their start and end apart: 11, of which 6 were waited for; matrix products, arithmetic and copies ran while one was open for 0% of the time, Pallas kernels for 14%

profile of v5, /device:TPU:0, one launch (start us, length us, event | category | flops | bytes accessed | tf_op | source)
XLA Modules:
  0.0 31.4 jit_solution(12863486939474465349)
XLA Ops:
  1.3 4.0 %local_sums.1 = (f32[448,128]{1,0:T(8,128)S(1)}, f32[448,128]{1,0:T(8,128)S(1)}, f32[256,256]{1,0:T(8,128)S(1)}, f32[4,128,128]{2,1,0:T(8,128)S(1)}, f32[2048,25...) custom-call(s32[8,128]{1,0:T(8,128)S(1)} %broadcast_in_dim.9.count_ref, ...), custom_call_target="tpu_custom_call" | custom-call | tf_op jit(solution)/shard_map/local_sums/pallas_call | solution.py:386
  5.3 0.5 %collective-permute-start = (f32[448,128]{1,0:T(8,128)S(1)}, f32[448,128]{1,0:T(8,128)S(1)}, u32[]{:S(2)}, u32[]{:S(2)}) collective-permute-start(f32[448,128]{1,0:T(8,128)S(1)} %get-tuple-element.29), channel_id=1, source_target_pairs={{0,1},{1,0},{2,3},{3,2},{4,5},{5,4},{6,7},{7,6},{8,9},{9,8},{10,11... | collective-permute-start | bytes 688136 | tf_op jit(solution)/shard_map/ppermute | solution.py:338
  5.8 1.3 %side_sums.1.k_ref = f32[256,256]{1,0:T(8,128)S(1)} custom-call(s32[8,128]{1,0:T(8,128)S(1)} %broadcast_in_dim.9.count_ref, f32[2048,256]{1,0:T(8,128)S(1)} %get-tuple-element.34.w_ref, f32[256,2048]{1,0:T(8,128)S(1)} %get-tuple-element.35.u_ref), custom_call_target="tpu_custom_call" | custom-call | flops 805306368 | bytes 1048576 | tf_op jit(solution)/shard_map/side_sums/pallas_call | solution.py:368
  7.1 0.0 collective-permute-done.sib_ref.refs_0_
  7.1 0.4 %level_0.1 = (f32[128,128]{1,0:T(8,128)S(1)}, f32[288,128]{1,0:T(8,128)S(1)}) custom-call(f32[448,128]{1,0:T(8,128)S(1)} %get-tuple-element.30.own_ref.refs_11_, f32[448,128]{1,0:T(8,128)S(1)} %collective-permute-done.sib_ref.refs_0_, f32[4,128,128]{2,1,0:T(8,128)S(1)} %get-tuple-element.31.nodes_ref), custom_call_target="tpu_custom_call" | custom-call | flops 20000000000 | bytes 1048576 | tf_op jit(solution)/shard_map/level_0/pallas_call | solution.py:368
  7.5 0.1 side_state.1
  7.6 0.3 collective-permute-start.3
  7.9 2.8 %collective-permute-start.1 = (f32[288,128]{1,0:T(8,128)S(1)}, f32[288,128]{1,0:T(8,128)S(1)}, u32[]{:S(2)}, u32[]{:S(2)}) collective-permute-start(f32[288,128]{1,0:T(8,128)S(1)} %get-tuple-element.32.own_ref), channel_id=1, source_target_pairs={{0,2},{1,3},{2,0},{3,1},{4,6},{5,7},{6,4},{7,5},{8,10},{9,11},{10,... | collective-permute-start | bytes 442376 | tf_op jit(solution)/shard_map/ppermute | solution.py:338
  10.7 0.0 collective-permute-done.3.sib_ref.refs_8_
  10.7 1.6 %collective-permute-start.4 = (f32[128,128]{1,0:T(8,128)S(1)}, f32[128,128]{1,0:T(8,128)S(1)}, u32[]{:S(2)}, u32[]{:S(2)}) collective-permute-start(f32[128,128]{1,0:T(8,128)S(1)} %get-tuple-element.41.sent_ref), channel_id=1, source_target_pairs={{0,4},{1,5},{2,6},{3,7},{4,0},{5,1},{6,2},{7,3},{8,12},{9,13},{10,... | collective-permute-start | bytes 196616 | tf_op jit(solution)/shard_map/ppermute | solution.py:338
  12.4 2.6 %collective-permute-start.5 = (f32[96,128]{1,0:T(8,128)S(1)}, f32[96,128]{1,0:T(8,128)S(1)}, u32[]{:S(2)}, u32[]{:S(2)}) collective-permute-start(f32[96,128]{1,0:T(8,128)S(1)} %get-tuple-element.43), channel_id=1, source_target_pairs={{0,8},{1,9},{2,10},{3,11},{4,12},{5,13},{6,14},{7,15},{8,0},{9,1},... | collective-permute-start | bytes 147464 | tf_op jit(solution)/shard_map/ppermute | solution.py:338
  15.0 0.0 collective-permute-done.1.sib_ref.refs_1_
  15.0 0.4 %level_1.1 = (f32[128,128]{1,0:T(8,128)S(1)}, f32[160,128]{1,0:T(8,128)S(1)}) custom-call(f32[288,128]{1,0:T(8,128)S(1)} %get-tuple-element.32.own_ref, f32[288,128]{1,0:T(8,128)S(1)} %collective-permute-done.1.sib_ref.refs_1_, f32[4,128,128]{2,1,0:T(8,128)S(1)} %get-tuple-element.31.nodes_ref), custom_call_target="tpu_custom_call" | custom-call | flops 20000000000 | bytes 1048576 | tf_op jit(solution)/shard_map/level_1/pallas_call | solution.py:368
  15.3 1.8 %collective-permute-start.2 = (f32[160,128]{1,0:T(8,128)S(1)}, f32[160,128]{1,0:T(8,128)S(1)}, u32[]{:S(2)}, u32[]{:S(2)}) collective-permute-start(f32[160,128]{1,0:T(8,128)S(1)} %get-tuple-element.33.own_ref), channel_id=1, source_target_pairs={{0,4},{1,5},{2,6},{3,7},{4,0},{5,1},{6,2},{7,3},{8,12},{9,13},{10,... | collective-permute-start | bytes 245768 | tf_op jit(solution)/shard_map/ppermute | solution.py:338
  17.1 0.3 %collective-permute-done.5.refs_0_ = f32[96,128]{1,0:T(8,128)S(1)} collective-permute-done((f32[96,128]{1,0:T(8,128)S(1)}, f32[96,128]{1,0:T(8,128)S(1)}, u32[]{:S(2)}, u32[]{:S(2)}) %collective-permute-start.5) | collective-permute-done | bytes 49184 | tf_op jit(solution)/shard_map/ppermute | solution.py:338
  17.5 0.0 collective-permute-done.4.got_ref
  17.5 1.6 %collective-permute-start.7 = (f32[384,128]{1,0:T(8,128)S(1)}, f32[384,128]{1,0:T(8,128)S(1)}, u32[]{:S(2)}, u32[]{:S(2)}) collective-permute-start(f32[384,128]{1,0:T(8,128)S(1)} %side_join_1.1.refs_0_.sent_ref.refs_9_), channel_id=1, source_target_pairs={{0,2},{1,3},{2,0},{3,1},{4,6},{5,7},{6,4},{7,5},{8,10},{9,11},{10,... | collective-permute-start | bytes 589832 | tf_op jit(solution)/shard_map/ppermute | solution.py:338
  19.1 0.8 %collective-permute-done.2.sib_ref.refs_2_ = f32[160,128]{1,0:T(8,128)S(1)} collective-permute-done((f32[160,128]{1,0:T(8,128)S(1)}, f32[160,128]{1,0:T(8,128)S(1)}, u32[]{:S(2)}, u32[]{:S(2)}) %collective-permute-start.2) | collective-permute-done | bytes 81952 | tf_op jit(solution)/shard_map/ppermute | solution.py:338
  19.9 0.4 %level_2.1 = (f32[128,128]{1,0:T(8,128)S(1)}, f32[64,128]{1,0:T(8,128)S(1)}) custom-call(f32[160,128]{1,0:T(8,128)S(1)} %get-tuple-element.33.own_ref, f32[160,128]{1,0:T(8,128)S(1)} %collective-permute-done.2.sib_ref.refs_2_, f32[4,128,128]{2,1,0:T(8,128)S(1)} %get-tuple-element.31.nodes_ref, f32[384,128]{1,0:T(8,128)S(1)} %side_join_1.1.refs_0_.sent_ref.refs_9_), custom_call_target="tpu_custom_call" | custom-call | flops 20000000000 | bytes 1048576 | tf_op jit(solution)/shard_map/level_2/pallas_call | solution.py:368
  20.2 2.8 %collective-permute-start.6 = (f32[64,128]{1,0:T(8,128)S(1)}, f32[64,128]{1,0:T(8,128)S(1)}, u32[]{:S(2)}, u32[]{:S(2)}) collective-permute-start(f32[64,128]{1,0:T(8,128)S(1)} %get-tuple-element.44.own_ref), channel_id=1, source_target_pairs={{0,8},{1,9},{2,10},{3,11},{4,12},{5,13},{6,14},{7,15},{8,0},{9,1},... | collective-permute-start | bytes 98312 | tf_op jit(solution)/shard_map/ppermute | solution.py:338
  23.0 0.2 collective-permute-done.7.got_ref.refs_10_
  23.2 1.4 %collective-permute-start.9 = (f32[96,128]{1,0:T(8,128)S(1)}, f32[96,128]{1,0:T(8,128)S(1)}, u32[]{:S(2)}, u32[]{:S(2)}) collective-permute-start(f32[96,128]{1,0:T(8,128)S(1)} %side_top.1.refs_0_.sent_ref), channel_id=1, source_target_pairs={{0,4},{1,5},{2,6},{3,7},{4,0},{5,1},{6,2},{7,3},{8,12},{9,13},{10,... | collective-permute-start | bytes 147464 | tf_op jit(solution)/shard_map/ppermute | solution.py:338
  24.7 0.4 %collective-permute-done.6.sib_ref.refs_3_ = f32[64,128]{1,0:T(8,128)S(1)} collective-permute-done((f32[64,128]{1,0:T(8,128)S(1)}, f32[64,128]{1,0:T(8,128)S(1)}, u32[]{:S(2)}, u32[]{:S(2)}) %collective-permute-start.6) | collective-permute-done | bytes 32800 | tf_op jit(solution)/shard_map/ppermute | solution.py:338
  25.1 0.2 level_3.1.refs_7_.refs_3_
  25.2 0.3 end_low.1
  25.5 0.1 collective-permute-start.8
  25.6 1.0 %solution_own.1.x_own = f32[2048,128]{1,0:T(8,128)S(1)} custom-call(s32[8,128]{1,0:T(8,128)S(1)} %broadcast_in_dim.9.count_ref, f32[2048,256]{1,0:T(8,128)S(1)} %get-tuple-element.50.x_ref, f32[256,2048]{1,0:T(8,128)S(1)} %get-tuple-element.51.q_ref, f32[128,128]{1,0:T(8,128)S(1)} %get-tuple-element.37.after_ref.refs_4_.refs_0_, ...), custom_call_target="tpu_custom_call" | custom-call | flops 1000000000 | bytes 1048576 | tf_op jit(solution)/shard_map/solution_own/pallas_call | solution.py:368
  26.6 0.8 %collective-permute-done.9.got_ref = f32[96,128]{1,0:T(8,128)S(1)} collective-permute-done((f32[96,128]{1,0:T(8,128)S(1)}, f32[96,128]{1,0:T(8,128)S(1)}, u32[]{:S(2)}, u32[]{:S(2)}) %collective-permute-start.9) | collective-permute-done | bytes 49184 | tf_op jit(solution)/shard_map/ppermute | solution.py:338
  27.4 0.1 collective-permute-start.10
  27.5 0.0 collective-permute-done.8.refs_0_.low_other
  27.5 1.0 %solution_other.1.x_other = f32[2048,128]{1,0:T(8,128)S(1)} custom-call(s32[8,128]{1,0:T(8,128)S(1)} %broadcast_in_dim.9.count_ref, f32[2048,256]{1,0:T(8,128)S(1)} %get-tuple-element.50.x_ref, f32[256,2048]{1,0:T(8,128)S(1)} %get-tuple-element.51.q_ref, f32[768,128]{1,0:T(8,128)S(1)} %collective-permute-done.8.refs_0_.low_other), custom_call_target="tpu_custom_call" | custom-call | flops 1000000000 | bytes 1048576 | tf_op jit(solution)/shard_map/solution_other/pallas_call | solution.py:368
  28.5 0.2 collective-permute-done.10.k_other
  28.7 2.8 %factor_rows.1 = (f32[2048,256]{1,0:T(8,128)}, bf16[256,2048]{1,0:T(8,128)(2,1)}, bf16[256,2048]{1,0:T(8,128)(2,1)}) custom-call(s32[8,128]{1,0:T(8,128)S(1)} %broadcast_in_dim.9.count_ref, f32[768,128]{1,0:T(8,128)S(1)} %get-tuple-element.46.low_own, f32[768,128]{1,0:T(8,128)S(1)} %collective-permute-done.8.refs_0_.low_other, ...), custom_call_target="tpu_custom_call" | custom-call | tf_op jit(solution)/shard_map/factor_rows/pallas_call | solution.py:368
  (5 shorter events, 0.1 us)
Async XLA Ops:
  5.3 1.8 %collective-permute-start = (f32[448,128]{1,0:T(8,128)S(1)}, f32[448,128]{1,0:T(8,128)S(1)}, u32[]{:S(2)}, u32[]{:S(2)}) collective-permute-start(f32[448,128]{1,0:T(8,128)S(1)} %get-tuple-element.29), channel_id=1, source_target_pairs={{0,1},{1,0},{2,3},{3,2},{4,5},{5,4},{6,7},{7,6},{8,9},{9,8},{10,11... | collective-permute-start | bytes 688136 | tf_op jit(solution)/shard_map/ppermute | solution.py:338
  7.6 3.1 %collective-permute-start.3 = (f32[576,128]{1,0:T(8,128)S(1)}, f32[576,128]{1,0:T(8,128)S(1)}, u32[]{:S(2)}, u32[]{:S(2)}) collective-permute-start(f32[576,128]{1,0:T(8,128)S(1)} %get-tuple-element.39), channel_id=1, source_target_pairs={{0,1},{1,0},{2,3},{3,2},{4,5},{5,4},{6,7},{7,6},{8,9},{9,8},{10,11... | collective-permute-start | bytes 884744 | tf_op jit(solution)/shard_map/ppermute | solution.py:338
  7.9 7.1 %collective-permute-start.1 = (f32[288,128]{1,0:T(8,128)S(1)}, f32[288,128]{1,0:T(8,128)S(1)}, u32[]{:S(2)}, u32[]{:S(2)}) collective-permute-start(f32[288,128]{1,0:T(8,128)S(1)} %get-tuple-element.32.own_ref), channel_id=1, source_target_pairs={{0,2},{1,3},{2,0},{3,1},{4,6},{5,7},{6,4},{7,5},{8,10},{9,11},{10,... | collective-permute-start | bytes 442376 | tf_op jit(solution)/shard_map/ppermute | solution.py:338
  10.7 6.7 %collective-permute-start.4 = (f32[128,128]{1,0:T(8,128)S(1)}, f32[128,128]{1,0:T(8,128)S(1)}, u32[]{:S(2)}, u32[]{:S(2)}) collective-permute-start(f32[128,128]{1,0:T(8,128)S(1)} %get-tuple-element.41.sent_ref), channel_id=1, source_target_pairs={{0,4},{1,5},{2,6},{3,7},{4,0},{5,1},{6,2},{7,3},{8,12},{9,13},{10,... | collective-permute-start | bytes 196616 | tf_op jit(solution)/shard_map/ppermute | solution.py:338
  12.4 5.1 %collective-permute-start.5 = (f32[96,128]{1,0:T(8,128)S(1)}, f32[96,128]{1,0:T(8,128)S(1)}, u32[]{:S(2)}, u32[]{:S(2)}) collective-permute-start(f32[96,128]{1,0:T(8,128)S(1)} %get-tuple-element.43), channel_id=1, source_target_pairs={{0,8},{1,9},{2,10},{3,11},{4,12},{5,13},{6,14},{7,15},{8,0},{9,1},... | collective-permute-start | bytes 147464 | tf_op jit(solution)/shard_map/ppermute | solution.py:338
  15.3 4.5 %collective-permute-start.2 = (f32[160,128]{1,0:T(8,128)S(1)}, f32[160,128]{1,0:T(8,128)S(1)}, u32[]{:S(2)}, u32[]{:S(2)}) collective-permute-start(f32[160,128]{1,0:T(8,128)S(1)} %get-tuple-element.33.own_ref), channel_id=1, source_target_pairs={{0,4},{1,5},{2,6},{3,7},{4,0},{5,1},{6,2},{7,3},{8,12},{9,13},{10,... | collective-permute-start | bytes 245768 | tf_op jit(solution)/shard_map/ppermute | solution.py:338
  17.5 5.7 %collective-permute-start.7 = (f32[384,128]{1,0:T(8,128)S(1)}, f32[384,128]{1,0:T(8,128)S(1)}, u32[]{:S(2)}, u32[]{:S(2)}) collective-permute-start(f32[384,128]{1,0:T(8,128)S(1)} %side_join_1.1.refs_0_.sent_ref.refs_9_), channel_id=1, source_target_pairs={{0,2},{1,3},{2,0},{3,1},{4,6},{5,7},{6,4},{7,5},{8,10},{9,11},{10,... | collective-permute-start | bytes 589832 | tf_op jit(solution)/shard_map/ppermute | solution.py:338
  20.2 4.9 %collective-permute-start.6 = (f32[64,128]{1,0:T(8,128)S(1)}, f32[64,128]{1,0:T(8,128)S(1)}, u32[]{:S(2)}, u32[]{:S(2)}) collective-permute-start(f32[64,128]{1,0:T(8,128)S(1)} %get-tuple-element.44.own_ref), channel_id=1, source_target_pairs={{0,8},{1,9},{2,10},{3,11},{4,12},{5,13},{6,14},{7,15},{8,0},{9,1},... | collective-permute-start | bytes 98312 | tf_op jit(solution)/shard_map/ppermute | solution.py:338
  23.2 4.2 %collective-permute-start.9 = (f32[96,128]{1,0:T(8,128)S(1)}, f32[96,128]{1,0:T(8,128)S(1)}, u32[]{:S(2)}, u32[]{:S(2)}) collective-permute-start(f32[96,128]{1,0:T(8,128)S(1)} %side_top.1.refs_0_.sent_ref), channel_id=1, source_target_pairs={{0,4},{1,5},{2,6},{3,7},{4,0},{5,1},{6,2},{7,3},{8,12},{9,13},{10,... | collective-permute-start | bytes 147464 | tf_op jit(solution)/shard_map/ppermute | solution.py:338
  25.5 1.9 %collective-permute-start.8 = (f32[768,128]{1,0:T(8,128)S(1)}, f32[768,128]{1,0:T(8,128)S(1)}, u32[]{:S(2)}, u32[]{:S(2)}) collective-permute-start(f32[768,128]{1,0:T(8,128)S(1)} %get-tuple-element.47), channel_id=1, source_target_pairs={{0,1},{1,0},{2,3},{3,2},{4,5},{5,4},{6,7},{7,6},{8,9},{9,8},{10,11... | collective-permute-start | bytes 1179656 | tf_op jit(solution)/shard_map/ppermute | solution.py:338
  27.4 1.3 %collective-permute-start.10 = (f32[64,128]{1,0:T(8,128)S(1)}, f32[64,128]{1,0:T(8,128)S(1)}, u32[]{:S(2)}, u32[]{:S(2)}) collective-permute-start(f32[64,128]{1,0:T(8,128)S(1)} %get-tuple-element.48.k_own), channel_id=1, source_target_pairs={{0,1},{1,0},{2,3},{3,2},{4,5},{5,4},{6,7},{7,6},{8,9},{9,8},{10,11... | collective-permute-start | bytes 98312 | tf_op jit(solution)/shard_map/ppermute | solution.py:338

commit v6 on v5

--- a/solution.py
+++ b/solution.py
@@ -281,6 +281,18 @@
 def halves(value):
     high = value.astype(jnp.bfloat16)
     return high, (value - high.astype(F32)).astype(jnp.bfloat16)
+
+
+def stacked(value):
+    return jnp.concatenate(halves(value), 0)
+
+
+def dot_stacked(both, b, dims):
+    rows = both.shape[0] // 2
+    b_high, b_low = halves(b)
+    wide = lax.dot_general(both, b_high, (dims, ((), ())), preferred_element_type=F32)
+    rest = lax.dot_general(both[:rows], b_low, (dims, ((), ())), preferred_element_type=F32)
+    return wide[:rows] + (wide[rows:] + rest)
 
 
 def solution_kernel(dims, count_ref, x_ref, q_ref, *refs):
@@ -305,7 +317,18 @@
         sol[part, :] = jnp.where(live, x, 0.0)
 
 
-def factor_kernel(dims, count_ref, low_own, low_other, k_own, k_other, h_ref, x_own, x_other, w_ref, *refs):
+def other_kernel(dims, scale, count_ref, x_ref, q_ref, low_own, low_other, h_ref, sol, l_ref):
+    solution_kernel(dims, count_ref, x_ref, q_ref, low_other, sol)
+    wide, rank = l_ref.shape[0], dims[1]
+    low = wide - rank
+    at = wide + 2 * low
+    (block,) = unpack(h_ref, 0, 1, rank)
+    l_top = whole(low_own, low_other, at, rank) - dot(block, whole(low_own, low_other, at + rank, rank))
+    l_ref[:low, :] = whole(low_own, low_other, wide, low)
+    l_ref[low:, :] = l_top * scale
+
+
+def factor_kernel(dims, count_ref, low_own, low_other, k_own, k_other, l_ref, x_own, x_other, w_ref, *refs):
     wide, scale, chunk = dims
     sol_out, left_out, right_out, left, right, sems = refs
     sender = Sender(sems)
@@ -315,19 +338,17 @@
     rank = k_own.shape[0]
     low = wide - rank
     at = wide + 2 * low
-    (block,) = unpack(h_ref, 0, 1, rank)
-    l_top = whole(low_own, low_other, at, rank) - dot(block, whole(low_own, low_other, at + rank, rank))
-    l = jnp.concatenate([whole(low_own, low_other, wide, low), l_top * scale], 0)
     k_low = jnp.concatenate([low_own[wide + low : at, :], low_other[wide + low : at, :]], 1)
     k = jnp.concatenate([k_low, jnp.concatenate([k_own[...], k_other[...]], 1) * scale], 0)
+    l, k = stacked(l_ref[...]), stacked(k)
     for i in range(w_ref.shape[0] // chunk):
         part, place = slice(i * chunk, (i + 1) * chunk), pl.ds(i * chunk, chunk)
         live = i * chunk + lax.broadcasted_iota(jnp.int32, (1, chunk), 1) < count_ref[:1, :1]
-        left_now = dot(l, w_ref[part, :], ((1,), (1,)))
+        left_now = dot_stacked(l, w_ref[part, :], ((1,), (1,)))
         left[:, part] = jnp.where(live, left_now, 0.0).astype(left.dtype)
         sender.send(left.at[:, place], left_out.at[:, place])
         x = jnp.concatenate([x_own[part, :], x_other[part, :]], 1)
-        right[:, part] = dot(k, x, ((1,), (1,))).astype(right.dtype)
+        right[:, part] = dot_stacked(k, x, ((1,), (1,))).astype(right.dtype)
         sender.send(right.at[:, place], right_out.at[:, place])
     sender.wait()
 
@@ -520,14 +541,16 @@
         params=large,
         cost=10**9,
     )
-    sol_other = call(
-        functools.partial(solution_kernel, (False, rank, chunk)),
+    sol_other, l_all = call(
+        functools.partial(other_kernel, (False, rank, chunk), dims[2]),
         "solution_other",
-        shape(row_count, half),
+        [shape(row_count, half), shape(wide, col_count)],
         count,
         x_vmem,
         q_vmem,
+        low_own,
         low_other,
+        h_top,
         params=large,
         cost=10**9,
     )
@@ -541,7 +564,7 @@
         low_other,
         k_own,
         k_other,
-        h_top,
+        l_all,
         sol_own,
         sol_other,
         w_vmem,

time: 31.6 us -> 31.7 us (level)
  transfers between devices with their start and end apart: 11 -> 11, of which waited for: 6 -> 5; matrix products, arithmetic and copies ran while one was open for 0% -> 0% of each run, Pallas kernels for 14% -> 14%
where the time goes in v6:
time: 31.7 us; the launch traced here: 31.6 us
  starting transfers between devices  15.5 us (49%)
  Pallas kernels  11.7 us (37%)
  waiting for transfers between devices  2.93 us (9%)
  between operations  1.41 us (4%)
    ppermute x11, starting transfers between devices, swapped(): return lax.ppermute(value, 'leaf', pairs)  15.5 us
    pallas_call x14, Pallas kernels, call(): pl.pallas_call(kernel, out_shape=out_shape, in_specs=[vmem] * len(operand...  7.7 us
    pallas_call x1, Pallas kernels, body(): pl.pallas_call(functools.partial(local_kernel, (levels, rank, base_bits),...  3.99 us
    ppermute x11, waiting for transfers between devices, swapped(): return lax.ppermute(value, 'leaf', pairs)  2.93 us
  transfers between devices with their start and end apart: 11, of which 5 were waited for; matrix products, arithmetic and copies ran while one was open for 0% of the time, Pallas kernels for 14%

profile of v6, /device:TPU:0, one launch (start us, length us, event | category | flops | bytes accessed | tf_op | source)
XLA Modules:
  0.0 31.6 jit_solution(6052783901552362189)
XLA Ops:
  1.3 4.0 %local_sums.1 = (f32[448,128]{1,0:T(8,128)S(1)}, f32[448,128]{1,0:T(8,128)S(1)}, f32[256,256]{1,0:T(8,128)S(1)}, f32[4,128,128]{2,1,0:T(8,128)S(1)}, f32[2048,25...) custom-call(s32[8,128]{1,0:T(8,128)S(1)} %broadcast_in_dim.9.count_ref, ...), custom_call_target="tpu_custom_call" | custom-call | tf_op jit(solution)/shard_map/local_sums/pallas_call | solution.py:407
  5.3 0.5 %collective-permute-start = (f32[448,128]{1,0:T(8,128)S(1)}, f32[448,128]{1,0:T(8,128)S(1)}, u32[]{:S(2)}, u32[]{:S(2)}) collective-permute-start(f32[448,128]{1,0:T(8,128)S(1)} %get-tuple-element.31), channel_id=1, source_target_pairs={{0,1},{1,0},{2,3},{3,2},{4,5},{5,4},{6,7},{7,6},{8,9},{9,8},{10,11... | collective-permute-start | bytes 688136 | tf_op jit(solution)/shard_map/ppermute | solution.py:359
  5.8 1.3 %side_sums.1.k_ref = f32[256,256]{1,0:T(8,128)S(1)} custom-call(s32[8,128]{1,0:T(8,128)S(1)} %broadcast_in_dim.9.count_ref, f32[2048,256]{1,0:T(8,128)S(1)} %get-tuple-element.36.w_ref, f32[256,2048]{1,0:T(8,128)S(1)} %get-tuple-element.37.u_ref), custom_call_target="tpu_custom_call" | custom-call | flops 805306368 | bytes 1048576 | tf_op jit(solution)/shard_map/side_sums/pallas_call | solution.py:389
  7.1 0.0 collective-permute-done.sib_ref.refs_0_
  7.1 0.4 %level_0.1 = (f32[128,128]{1,0:T(8,128)S(1)}, f32[288,128]{1,0:T(8,128)S(1)}) custom-call(f32[448,128]{1,0:T(8,128)S(1)} %get-tuple-element.32.own_ref.refs_11_, f32[448,128]{1,0:T(8,128)S(1)} %collective-permute-done.sib_ref.refs_0_, f32[4,128,128]{2,1,0:T(8,128)S(1)} %get-tuple-element.33.nodes_ref), custom_call_target="tpu_custom_call" | custom-call | flops 20000000000 | bytes 1048576 | tf_op jit(solution)/shard_map/level_0/pallas_call | solution.py:389
  7.5 0.1 side_state.1
  7.6 0.3 collective-permute-start.3
  7.9 2.8 %collective-permute-start.1 = (f32[288,128]{1,0:T(8,128)S(1)}, f32[288,128]{1,0:T(8,128)S(1)}, u32[]{:S(2)}, u32[]{:S(2)}) collective-permute-start(f32[288,128]{1,0:T(8,128)S(1)} %get-tuple-element.34.own_ref), channel_id=1, source_target_pairs={{0,2},{1,3},{2,0},{3,1},{4,6},{5,7},{6,4},{7,5},{8,10},{9,11},{10,... | collective-permute-start | bytes 442376 | tf_op jit(solution)/shard_map/ppermute | solution.py:359
  10.7 0.0 collective-permute-done.3.sib_ref.refs_8_
  10.7 2.7 %collective-permute-start.5 = (f32[96,128]{1,0:T(8,128)S(1)}, f32[96,128]{1,0:T(8,128)S(1)}, u32[]{:S(2)}, u32[]{:S(2)}) collective-permute-start(f32[96,128]{1,0:T(8,128)S(1)} %get-tuple-element.45), channel_id=1, source_target_pairs={{0,8},{1,9},{2,10},{3,11},{4,12},{5,13},{6,14},{7,15},{8,0},{9,1},... | collective-permute-start | bytes 147464 | tf_op jit(solution)/shard_map/ppermute | solution.py:359
  13.4 1.6 %collective-permute-start.4 = (f32[128,128]{1,0:T(8,128)S(1)}, f32[128,128]{1,0:T(8,128)S(1)}, u32[]{:S(2)}, u32[]{:S(2)}) collective-permute-start(f32[128,128]{1,0:T(8,128)S(1)} %get-tuple-element.43.sent_ref), channel_id=1, source_target_pairs={{0,4},{1,5},{2,6},{3,7},{4,0},{5,1},{6,2},{7,3},{8,12},{9,13},{10,... | collective-permute-start | bytes 196616 | tf_op jit(solution)/shard_map/ppermute | solution.py:359
  15.0 0.0 collective-permute-done.1.sib_ref.refs_1_
  15.0 0.4 %level_1.1 = (f32[128,128]{1,0:T(8,128)S(1)}, f32[160,128]{1,0:T(8,128)S(1)}) custom-call(f32[288,128]{1,0:T(8,128)S(1)} %get-tuple-element.34.own_ref, f32[288,128]{1,0:T(8,128)S(1)} %collective-permute-done.1.sib_ref.refs_1_, f32[4,128,128]{2,1,0:T(8,128)S(1)} %get-tuple-element.33.nodes_ref), custom_call_target="tpu_custom_call" | custom-call | flops 20000000000 | bytes 1048576 | tf_op jit(solution)/shard_map/level_1/pallas_call | solution.py:389
  15.3 1.8 %collective-permute-start.2 = (f32[160,128]{1,0:T(8,128)S(1)}, f32[160,128]{1,0:T(8,128)S(1)}, u32[]{:S(2)}, u32[]{:S(2)}) collective-permute-start(f32[160,128]{1,0:T(8,128)S(1)} %get-tuple-element.35.own_ref), channel_id=1, source_target_pairs={{0,4},{1,5},{2,6},{3,7},{4,0},{5,1},{6,2},{7,3},{8,12},{9,13},{10,... | collective-permute-start | bytes 245768 | tf_op jit(solution)/shard_map/ppermute | solution.py:359
  17.1 0.0 collective-permute-done.5.refs_0_
  17.1 0.6 %collective-permute-done.4.got_ref = f32[128,128]{1,0:T(8,128)S(1)} collective-permute-done((f32[128,128]{1,0:T(8,128)S(1)}, f32[128,128]{1,0:T(8,128)S(1)}, u32[]{:S(2)}, u32[]{:S(2)}) %collective-permute-start.4) | collective-permute-done | bytes 65568 | tf_op jit(solution)/shard_map/ppermute | solution.py:359
  17.7 1.2 %collective-permute-start.7 = (f32[384,128]{1,0:T(8,128)S(1)}, f32[384,128]{1,0:T(8,128)S(1)}, u32[]{:S(2)}, u32[]{:S(2)}) collective-permute-start(f32[384,128]{1,0:T(8,128)S(1)} %side_join_1.1.refs_0_.sent_ref.refs_9_), channel_id=1, source_target_pairs={{0,2},{1,3},{2,0},{3,1},{4,6},{5,7},{6,4},{7,5},{8,10},{9,11},{10,... | collective-permute-start | bytes 589832 | tf_op jit(solution)/shard_map/ppermute | solution.py:359
  19.0 0.9 %collective-permute-done.2.sib_ref.refs_2_ = f32[160,128]{1,0:T(8,128)S(1)} collective-permute-done((f32[160,128]{1,0:T(8,128)S(1)}, f32[160,128]{1,0:T(8,128)S(1)}, u32[]{:S(2)}, u32[]{:S(2)}) %collective-permute-start.2) | collective-permute-done | bytes 81952 | tf_op jit(solution)/shard_map/ppermute | solution.py:359
  19.9 0.4 %level_2.1 = (f32[128,128]{1,0:T(8,128)S(1)}, f32[64,128]{1,0:T(8,128)S(1)}) custom-call(f32[160,128]{1,0:T(8,128)S(1)} %get-tuple-element.35.own_ref, f32[160,128]{1,0:T(8,128)S(1)} %collective-permute-done.2.sib_ref.refs_2_, f32[4,128,128]{2,1,0:T(8,128)S(1)} %get-tuple-element.33.nodes_ref, f32[384,128]{1,0:T(8,128)S(1)} %side_join_1.1.refs_0_.sent_ref.refs_9_), custom_call_target="tpu_custom_call" | custom-call | flops 20000000000 | bytes 1048576 | tf_op jit(solution)/shard_map/level_2/pallas_call | solution.py:389
  20.2 2.8 %collective-permute-start.6 = (f32[64,128]{1,0:T(8,128)S(1)}, f32[64,128]{1,0:T(8,128)S(1)}, u32[]{:S(2)}, u32[]{:S(2)}) collective-permute-start(f32[64,128]{1,0:T(8,128)S(1)} %get-tuple-element.46.own_ref), channel_id=1, source_target_pairs={{0,8},{1,9},{2,10},{3,11},{4,12},{5,13},{6,14},{7,15},{8,0},{9,1},... | collective-permute-start | bytes 98312 | tf_op jit(solution)/shard_map/ppermute | solution.py:359
  23.0 0.5 %collective-permute-done.7.got_ref.refs_10_ = f32[384,128]{1,0:T(8,128)S(1)} collective-permute-done((f32[384,128]{1,0:T(8,128)S(1)}, f32[384,128]{1,0:T(8,128)S(1)}, u32[]{:S(2)}, u32[]{:S(2)}) %collective-permute-start.7) | collective-permute-done | bytes 196640 | tf_op jit(solution)/shard_map/ppermute | solution.py:359
  23.5 1.7 %collective-permute-start.9 = (f32[96,128]{1,0:T(8,128)S(1)}, f32[96,128]{1,0:T(8,128)S(1)}, u32[]{:S(2)}, u32[]{:S(2)}) collective-permute-start(f32[96,128]{1,0:T(8,128)S(1)} %side_top.1.refs_0_.sent_ref), channel_id=1, source_target_pairs={{0,4},{1,5},{2,6},{3,7},{4,0},{5,1},{6,2},{7,3},{8,12},{9,13},{10,... | collective-permute-start | bytes 147464 | tf_op jit(solution)/shard_map/ppermute | solution.py:359
  25.2 0.0 collective-permute-done.6.sib_ref.refs_3_
  25.2 0.2 level_3.1.refs_7_.refs_3_
  25.4 0.3 end_low.1
  25.7 0.1 collective-permute-start.8
  25.8 1.0 %solution_own.1.x_own = f32[2048,128]{1,0:T(8,128)S(1)} custom-call(s32[8,128]{1,0:T(8,128)S(1)} %broadcast_in_dim.9.count_ref, f32[2048,256]{1,0:T(8,128)S(1)} %get-tuple-element.51.x_ref, f32[256,2048]{1,0:T(8,128)S(1)} %get-tuple-element.52.q_ref, f32[128,128]{1,0:T(8,128)S(1)} %get-tuple-element.39.after_ref.refs_4_.refs_0_, ...), custom_call_target="tpu_custom_call" | custom-call | flops 1000000000 | bytes 1048576 | tf_op jit(solution)/shard_map/solution_own/pallas_call | solution.py:389
  26.8 0.9 %collective-permute-done.9.got_ref = f32[96,128]{1,0:T(8,128)S(1)} collective-permute-done((f32[96,128]{1,0:T(8,128)S(1)}, f32[96,128]{1,0:T(8,128)S(1)}, u32[]{:S(2)}, u32[]{:S(2)}) %collective-permute-start.9) | collective-permute-done | bytes 49184 | tf_op jit(solution)/shard_map/ppermute | solution.py:359
  27.7 0.1 collective-permute-start.10
  27.7 0.0 collective-permute-done.8.low_other
  27.7 1.1 %solution_other.1 = (f32[2048,128]{1,0:T(8,128)S(1)}, f32[256,256]{1,0:T(8,128)S(1)}) custom-call(s32[8,128]{1,0:T(8,128)S(1)} %broadcast_in_dim.9.count_ref, f32[2048,256]{1,0:T(8,128)S(1)} %get-tuple-element.51.x_ref, f32[256,2048]{1,0:T(8,128)S(1)} %get-tuple-element.52.q_ref, f32[768,128]{1,0:T(8,128)S(1)} %get-tuple-element.48.low_own, ...), custom_call_target="tpu_custom_call" | custom-call | flops 1000000000 | bytes 1048576 | tf_op jit(solution)/shard_map/solution_other/pallas_call | solution.py:389
  28.8 0.1 collective-permute-done.10.k_other
  28.9 2.6 %factor_rows.1 = (f32[2048,256]{1,0:T(8,128)}, bf16[256,2048]{1,0:T(8,128)(2,1)}, bf16[256,2048]{1,0:T(8,128)(2,1)}) custom-call(s32[8,128]{1,0:T(8,128)S(1)} %broadcast_in_dim.9.count_ref, f32[768,128]{1,0:T(8,128)S(1)} %get-tuple-element.48.low_own, f32[768,128]{1,0:T(8,128)S(1)} %collective-permute-done.8.low_other, ...), custom_call_target="tpu_custom_call" | custom-call | tf_op jit(solution)/shard_map/factor_rows/pallas_call | solution.py:389
  (5 shorter events, 0.1 us)
Async XLA Ops:
  5.3 1.8 %collective-permute-start = (f32[448,128]{1,0:T(8,128)S(1)}, f32[448,128]{1,0:T(8,128)S(1)}, u32[]{:S(2)}, u32[]{:S(2)}) collective-permute-start(f32[448,128]{1,0:T(8,128)S(1)} %get-tuple-element.31), channel_id=1, source_target_pairs={{0,1},{1,0},{2,3},{3,2},{4,5},{5,4},{6,7},{7,6},{8,9},{9,8},{10,11... | collective-permute-start | bytes 688136 | tf_op jit(solution)/shard_map/ppermute | solution.py:359
  7.6 3.1 %collective-permute-start.3 = (f32[576,128]{1,0:T(8,128)S(1)}, f32[576,128]{1,0:T(8,128)S(1)}, u32[]{:S(2)}, u32[]{:S(2)}) collective-permute-start(f32[576,128]{1,0:T(8,128)S(1)} %get-tuple-element.41), channel_id=1, source_target_pairs={{0,1},{1,0},{2,3},{3,2},{4,5},{5,4},{6,7},{7,6},{8,9},{9,8},{10,11... | collective-permute-start | bytes 884744 | tf_op jit(solution)/shard_map/ppermute | solution.py:359
  7.9 7.1 %collective-permute-start.1 = (f32[288,128]{1,0:T(8,128)S(1)}, f32[288,128]{1,0:T(8,128)S(1)}, u32[]{:S(2)}, u32[]{:S(2)}) collective-permute-start(f32[288,128]{1,0:T(8,128)S(1)} %get-tuple-element.34.own_ref), channel_id=1, source_target_pairs={{0,2},{1,3},{2,0},{3,1},{4,6},{5,7},{6,4},{7,5},{8,10},{9,11},{10,... | collective-permute-start | bytes 442376 | tf_op jit(solution)/shard_map/ppermute | solution.py:359
  10.7 6.4 %collective-permute-start.5 = (f32[96,128]{1,0:T(8,128)S(1)}, f32[96,128]{1,0:T(8,128)S(1)}, u32[]{:S(2)}, u32[]{:S(2)}) collective-permute-start(f32[96,128]{1,0:T(8,128)S(1)} %get-tuple-element.45), channel_id=1, source_target_pairs={{0,8},{1,9},{2,10},{3,11},{4,12},{5,13},{6,14},{7,15},{8,0},{9,1},... | collective-permute-start | bytes 147464 | tf_op jit(solution)/shard_map/ppermute | solution.py:359
  13.4 4.3 %collective-permute-start.4 = (f32[128,128]{1,0:T(8,128)S(1)}, f32[128,128]{1,0:T(8,128)S(1)}, u32[]{:S(2)}, u32[]{:S(2)}) collective-permute-start(f32[128,128]{1,0:T(8,128)S(1)} %get-tuple-element.43.sent_ref), channel_id=1, source_target_pairs={{0,4},{1,5},{2,6},{3,7},{4,0},{5,1},{6,2},{7,3},{8,12},{9,13},{10,... | collective-permute-start | bytes 196616 | tf_op jit(solution)/shard_map/ppermute | solution.py:359
  15.3 4.5 %collective-permute-start.2 = (f32[160,128]{1,0:T(8,128)S(1)}, f32[160,128]{1,0:T(8,128)S(1)}, u32[]{:S(2)}, u32[]{:S(2)}) collective-permute-start(f32[160,128]{1,0:T(8,128)S(1)} %get-tuple-element.35.own_ref), channel_id=1, source_target_pairs={{0,4},{1,5},{2,6},{3,7},{4,0},{5,1},{6,2},{7,3},{8,12},{9,13},{10,... | collective-permute-start | bytes 245768 | tf_op jit(solution)/shard_map/ppermute | solution.py:359
  17.7 5.7 %collective-permute-start.7 = (f32[384,128]{1,0:T(8,128)S(1)}, f32[384,128]{1,0:T(8,128)S(1)}, u32[]{:S(2)}, u32[]{:S(2)}) collective-permute-start(f32[384,128]{1,0:T(8,128)S(1)} %side_join_1.1.refs_0_.sent_ref.refs_9_), channel_id=1, source_target_pairs={{0,2},{1,3},{2,0},{3,1},{4,6},{5,7},{6,4},{7,5},{8,10},{9,11},{10,... | collective-permute-start | bytes 589832 | tf_op jit(solution)/shard_map/ppermute | solution.py:359
  20.2 5.0 %collective-permute-start.6 = (f32[64,128]{1,0:T(8,128)S(1)}, f32[64,128]{1,0:T(8,128)S(1)}, u32[]{:S(2)}, u32[]{:S(2)}) collective-permute-start(f32[64,128]{1,0:T(8,128)S(1)} %get-tuple-element.46.own_ref), channel_id=1, source_target_pairs={{0,8},{1,9},{2,10},{3,11},{4,12},{5,13},{6,14},{7,15},{8,0},{9,1},... | collective-permute-start | bytes 98312 | tf_op jit(solution)/shard_map/ppermute | solution.py:359
  23.5 4.2 %collective-permute-start.9 = (f32[96,128]{1,0:T(8,128)S(1)}, f32[96,128]{1,0:T(8,128)S(1)}, u32[]{:S(2)}, u32[]{:S(2)}) collective-permute-start(f32[96,128]{1,0:T(8,128)S(1)} %side_top.1.refs_0_.sent_ref), channel_id=1, source_target_pairs={{0,4},{1,5},{2,6},{3,7},{4,0},{5,1},{6,2},{7,3},{8,12},{9,13},{10,... | collective-permute-start | bytes 147464 | tf_op jit(solution)/shard_map/ppermute | solution.py:359
  25.7 2.0 %collective-permute-start.8 = (f32[768,128]{1,0:T(8,128)S(1)}, f32[768,128]{1,0:T(8,128)S(1)}, u32[]{:S(2)}, u32[]{:S(2)}) collective-permute-start(f32[768,128]{1,0:T(8,128)S(1)} %get-tuple-element.49), channel_id=1, source_target_pairs={{0,1},{1,0},{2,3},{3,2},{4,5},{5,4},{6,7},{7,6},{8,9},{9,8},{10,11... | collective-permute-start | bytes 1179656 | tf_op jit(solution)/shard_map/ppermute | solution.py:359
  27.7 1.3 %collective-permute-start.10 = (f32[64,128]{1,0:T(8,128)S(1)}, f32[64,128]{1,0:T(8,128)S(1)}, u32[]{:S(2)}, u32[]{:S(2)}) collective-permute-start(f32[64,128]{1,0:T(8,128)S(1)} %get-tuple-element.50.k_own), channel_id=1, source_target_pairs={{0,1},{1,0},{2,3},{3,2},{4,5},{5,4},{6,7},{7,6},{8,9},{9,8},{10,11... | collective-permute-start | bytes 98312 | tf_op jit(solution)/shard_map/ppermute | solution.py:359

commit v7 on v5

--- a/solution.py
+++ b/solution.py
@@ -15,6 +15,19 @@
 
 def dot(a, b, dims=((1,), (0,))):
     return lax.dot_general(a, b, (dims, ((), ())), precision=HIGH, preferred_element_type=F32)
+
+
+def halves(value):
+    high = value.astype(jnp.bfloat16)
+    return high, (value - high.astype(F32)).astype(jnp.bfloat16)
+
+
+def dot_joined(a, b):
+    a_high, a_low = halves(a)
+    b_high, b_low = halves(b)
+    left = jnp.concatenate([a_high, a_high, a_low], 1)
+    right = jnp.concatenate([b_high, b_low, b_high], 0)
+    return jnp.dot(left, right, preferred_element_type=F32)
 
 
 def pack(blocks):
@@ -183,7 +196,7 @@
     is_lower = jnp.right_shift(lax.axis_index("leaf"), base_bits + level) % 2 == 0
     own, sib = own_ref[:rank, :], sib_ref[:rank, :]
     both = jnp.concatenate([jnp.where(is_lower, own, sib), jnp.where(is_lower, sib, own)], 0)
-    mixed = dot(nodes_ref[level], both)
+    mixed = dot_joined(nodes_ref[level], both)
     z_own = jnp.where(is_lower, mixed[:rank], mixed[rank:])
     z_sib = jnp.where(is_lower, mixed[rank:], mixed[:rank])
     z_ref[:rank, :] = z_own
@@ -195,7 +208,7 @@
     h_own = unpack(own_ref, rank, count, rank)
     h_sib = unpack(sib_ref, rank, count, rank)
     h_both = jnp.concatenate([jnp.concatenate(h_own, 0), jnp.concatenate(h_sib, 0)], 1)
-    drop = dot(h_both, jnp.concatenate([z_own, z_sib], 0))
+    drop = dot_joined(h_both, jnp.concatenate([z_own, z_sib], 0))
 
     def total(at, rows):
         return own_ref[at : at + rows, :] + sib_ref[at : at + rows, :]
@@ -276,11 +289,6 @@
     def wait(self):
         for copy in self.copies:
             copy.wait()
-
-
-def halves(value):
-    high = value.astype(jnp.bfloat16)
-    return high, (value - high.astype(F32)).astype(jnp.bfloat16)
 
 
 def solution_kernel(dims, count_ref, x_ref, q_ref, *refs):

time: 31.6 us -> 31.6 us (level)
  no operation moved by 1% of the time
where the time goes in v7:
time: 31.6 us; the launch traced here: 31.4 us
  starting transfers between devices  15.6 us (49%)
  Pallas kernels  11.7 us (37%)
  waiting for transfers between devices  2.75 us (9%)
  between operations  1.41 us (4%)
    ppermute x11, starting transfers between devices, swapped(): return lax.ppermute(value, 'leaf', pairs)  15.6 us
    pallas_call x14, Pallas kernels, call(): pl.pallas_call(kernel, out_shape=out_shape, in_specs=[vmem] * len(operand...  7.68 us
    pallas_call x1, Pallas kernels, body(): pl.pallas_call(functools.partial(local_kernel, (levels, rank, base_bits),...  3.99 us
    ppermute x11, waiting for transfers between devices, swapped(): return lax.ppermute(value, 'leaf', pairs)  2.75 us
  transfers between devices with their start and end apart: 11, of which 6 were waited for; matrix products, arithmetic and copies ran while one was open for 0% of the time, Pallas kernels for 14%

profile of v7, /device:TPU:0, one launch (start us, length us, event | category | flops | bytes accessed | tf_op | source)
XLA Modules:
  0.0 31.4 jit_solution(3071705049976553331)
XLA Ops:
  1.3 4.0 %local_sums.1 = (f32[448,128]{1,0:T(8,128)S(1)}, f32[448,128]{1,0:T(8,128)S(1)}, f32[256,256]{1,0:T(8,128)S(1)}, f32[4,128,128]{2,1,0:T(8,128)S(1)}, f32[2048,25...) custom-call(s32[8,128]{1,0:T(8,128)S(1)} %broadcast_in_dim.9.count_ref, ...), custom_call_target="tpu_custom_call" | custom-call | tf_op jit(solution)/shard_map/local_sums/pallas_call | solution.py:394
  5.3 0.5 %collective-permute-start = (f32[448,128]{1,0:T(8,128)S(1)}, f32[448,128]{1,0:T(8,128)S(1)}, u32[]{:S(2)}, u32[]{:S(2)}) collective-permute-start(f32[448,128]{1,0:T(8,128)S(1)} %get-tuple-element.29), channel_id=1, source_target_pairs={{0,1},{1,0},{2,3},{3,2},{4,5},{5,4},{6,7},{7,6},{8,9},{9,8},{10,11... | collective-permute-start | bytes 688136 | tf_op jit(solution)/shard_map/ppermute | solution.py:346
  5.8 1.3 %side_sums.1.k_ref = f32[256,256]{1,0:T(8,128)S(1)} custom-call(s32[8,128]{1,0:T(8,128)S(1)} %broadcast_in_dim.9.count_ref, f32[2048,256]{1,0:T(8,128)S(1)} %get-tuple-element.34.w_ref, f32[256,2048]{1,0:T(8,128)S(1)} %get-tuple-element.35.u_ref), custom_call_target="tpu_custom_call" | custom-call | flops 805306368 | bytes 1048576 | tf_op jit(solution)/shard_map/side_sums/pallas_call | solution.py:376
  7.1 0.0 collective-permute-done.sib_ref.refs_0_
  7.1 0.4 %level_0.1 = (f32[128,128]{1,0:T(8,128)S(1)}, f32[288,128]{1,0:T(8,128)S(1)}) custom-call(f32[448,128]{1,0:T(8,128)S(1)} %get-tuple-element.30.own_ref.refs_11_, f32[448,128]{1,0:T(8,128)S(1)} %collective-permute-done.sib_ref.refs_0_, f32[4,128,128]{2,1,0:T(8,128)S(1)} %get-tuple-element.31.nodes_ref), custom_call_target="tpu_custom_call" | custom-call | flops 20000000000 | bytes 1048576 | tf_op jit(solution)/shard_map/level_0/pallas_call | solution.py:376
  7.5 0.1 side_state.1
  7.6 0.3 collective-permute-start.3
  7.8 2.8 %collective-permute-start.1 = (f32[288,128]{1,0:T(8,128)S(1)}, f32[288,128]{1,0:T(8,128)S(1)}, u32[]{:S(2)}, u32[]{:S(2)}) collective-permute-start(f32[288,128]{1,0:T(8,128)S(1)} %get-tuple-element.32.own_ref), channel_id=1, source_target_pairs={{0,2},{1,3},{2,0},{3,1},{4,6},{5,7},{6,4},{7,5},{8,10},{9,11},{10,... | collective-permute-start | bytes 442376 | tf_op jit(solution)/shard_map/ppermute | solution.py:346
  10.7 0.0 collective-permute-done.3.sib_ref.refs_8_
  10.7 1.6 %collective-permute-start.4 = (f32[128,128]{1,0:T(8,128)S(1)}, f32[128,128]{1,0:T(8,128)S(1)}, u32[]{:S(2)}, u32[]{:S(2)}) collective-permute-start(f32[128,128]{1,0:T(8,128)S(1)} %get-tuple-element.41.sent_ref), channel_id=1, source_target_pairs={{0,4},{1,5},{2,6},{3,7},{4,0},{5,1},{6,2},{7,3},{8,12},{9,13},{10,... | collective-permute-start | bytes 196616 | tf_op jit(solution)/shard_map/ppermute | solution.py:346
  12.4 2.6 %collective-permute-start.5 = (f32[96,128]{1,0:T(8,128)S(1)}, f32[96,128]{1,0:T(8,128)S(1)}, u32[]{:S(2)}, u32[]{:S(2)}) collective-permute-start(f32[96,128]{1,0:T(8,128)S(1)} %get-tuple-element.43), channel_id=1, source_target_pairs={{0,8},{1,9},{2,10},{3,11},{4,12},{5,13},{6,14},{7,15},{8,0},{9,1},... | collective-permute-start | bytes 147464 | tf_op jit(solution)/shard_map/ppermute | solution.py:346
  14.9 0.0 collective-permute-done.1.sib_ref.refs_1_
  14.9 0.4 %level_1.1 = (f32[128,128]{1,0:T(8,128)S(1)}, f32[160,128]{1,0:T(8,128)S(1)}) custom-call(f32[288,128]{1,0:T(8,128)S(1)} %get-tuple-element.32.own_ref, f32[288,128]{1,0:T(8,128)S(1)} %collective-permute-done.1.sib_ref.refs_1_, f32[4,128,128]{2,1,0:T(8,128)S(1)} %get-tuple-element.31.nodes_ref), custom_call_target="tpu_custom_call" | custom-call | flops 20000000000 | bytes 1048576 | tf_op jit(solution)/shard_map/level_1/pallas_call | solution.py:376
  15.3 1.8 %collective-permute-start.2 = (f32[160,128]{1,0:T(8,128)S(1)}, f32[160,128]{1,0:T(8,128)S(1)}, u32[]{:S(2)}, u32[]{:S(2)}) collective-permute-start(f32[160,128]{1,0:T(8,128)S(1)} %get-tuple-element.33.own_ref), channel_id=1, source_target_pairs={{0,4},{1,5},{2,6},{3,7},{4,0},{5,1},{6,2},{7,3},{8,12},{9,13},{10,... | collective-permute-start | bytes 245768 | tf_op jit(solution)/shard_map/ppermute | solution.py:346
  17.1 0.3 %collective-permute-done.5.refs_0_ = f32[96,128]{1,0:T(8,128)S(1)} collective-permute-done((f32[96,128]{1,0:T(8,128)S(1)}, f32[96,128]{1,0:T(8,128)S(1)}, u32[]{:S(2)}, u32[]{:S(2)}) %collective-permute-start.5) | collective-permute-done | bytes 49184 | tf_op jit(solution)/shard_map/ppermute | solution.py:346
  17.5 0.0 collective-permute-done.4.got_ref
  17.5 1.6 %collective-permute-start.7 = (f32[384,128]{1,0:T(8,128)S(1)}, f32[384,128]{1,0:T(8,128)S(1)}, u32[]{:S(2)}, u32[]{:S(2)}) collective-permute-start(f32[384,128]{1,0:T(8,128)S(1)} %side_join_1.1.refs_0_.sent_ref.refs_9_), channel_id=1, source_target_pairs={{0,2},{1,3},{2,0},{3,1},{4,6},{5,7},{6,4},{7,5},{8,10},{9,11},{10,... | collective-permute-start | bytes 589832 | tf_op jit(solution)/shard_map/ppermute | solution.py:346
  19.1 0.7 %collective-permute-done.2.sib_ref.refs_2_ = f32[160,128]{1,0:T(8,128)S(1)} collective-permute-done((f32[160,128]{1,0:T(8,128)S(1)}, f32[160,128]{1,0:T(8,128)S(1)}, u32[]{:S(2)}, u32[]{:S(2)}) %collective-permute-start.2) | collective-permute-done | bytes 81952 | tf_op jit(solution)/shard_map/ppermute | solution.py:346
  19.8 0.3 %level_2.1 = (f32[128,128]{1,0:T(8,128)S(1)}, f32[64,128]{1,0:T(8,128)S(1)}) custom-call(f32[160,128]{1,0:T(8,128)S(1)} %get-tuple-element.33.own_ref, f32[160,128]{1,0:T(8,128)S(1)} %collective-permute-done.2.sib_ref.refs_2_, f32[4,128,128]{2,1,0:T(8,128)S(1)} %get-tuple-element.31.nodes_ref, f32[384,128]{1,0:T(8,128)S(1)} %side_join_1.1.refs_0_.sent_ref.refs_9_), custom_call_target="tpu_custom_call" | custom-call | flops 20000000000 | bytes 1048576 | tf_op jit(solution)/shard_map/level_2/pallas_call | solution.py:376
  20.1 2.8 %collective-permute-start.6 = (f32[64,128]{1,0:T(8,128)S(1)}, f32[64,128]{1,0:T(8,128)S(1)}, u32[]{:S(2)}, u32[]{:S(2)}) collective-permute-start(f32[64,128]{1,0:T(8,128)S(1)} %get-tuple-element.44.own_ref), channel_id=1, source_target_pairs={{0,8},{1,9},{2,10},{3,11},{4,12},{5,13},{6,14},{7,15},{8,0},{9,1},... | collective-permute-start | bytes 98312 | tf_op jit(solution)/shard_map/ppermute | solution.py:346
  23.0 0.2 collective-permute-done.7.got_ref.refs_10_
  23.2 1.4 %collective-permute-start.9 = (f32[96,128]{1,0:T(8,128)S(1)}, f32[96,128]{1,0:T(8,128)S(1)}, u32[]{:S(2)}, u32[]{:S(2)}) collective-permute-start(f32[96,128]{1,0:T(8,128)S(1)} %side_top.1.refs_0_.sent_ref), channel_id=1, source_target_pairs={{0,4},{1,5},{2,6},{3,7},{4,0},{5,1},{6,2},{7,3},{8,12},{9,13},{10,... | collective-permute-start | bytes 147464 | tf_op jit(solution)/shard_map/ppermute | solution.py:346
  24.6 0.4 %collective-permute-done.6.sib_ref.refs_3_ = f32[64,128]{1,0:T(8,128)S(1)} collective-permute-done((f32[64,128]{1,0:T(8,128)S(1)}, f32[64,128]{1,0:T(8,128)S(1)}, u32[]{:S(2)}, u32[]{:S(2)}) %collective-permute-start.6) | collective-permute-done | bytes 32800 | tf_op jit(solution)/shard_map/ppermute | solution.py:346
  25.0 0.2 level_3.1.refs_7_.refs_3_
  25.2 0.3 end_low.1
  25.5 0.1 collective-permute-start.8
  25.6 1.0 %solution_own.1.x_own = f32[2048,128]{1,0:T(8,128)S(1)} custom-call(s32[8,128]{1,0:T(8,128)S(1)} %broadcast_in_dim.9.count_ref, f32[2048,256]{1,0:T(8,128)S(1)} %get-tuple-element.50.x_ref, f32[256,2048]{1,0:T(8,128)S(1)} %get-tuple-element.51.q_ref, f32[128,128]{1,0:T(8,128)S(1)} %get-tuple-element.37.after_ref.refs_4_.refs_0_, ...), custom_call_target="tpu_custom_call" | custom-call | flops 1000000000 | bytes 1048576 | tf_op jit(solution)/shard_map/solution_own/pallas_call | solution.py:376
  26.6 0.8 %collective-permute-done.9.got_ref = f32[96,128]{1,0:T(8,128)S(1)} collective-permute-done((f32[96,128]{1,0:T(8,128)S(1)}, f32[96,128]{1,0:T(8,128)S(1)}, u32[]{:S(2)}, u32[]{:S(2)}) %collective-permute-start.9) | collective-permute-done | bytes 49184 | tf_op jit(solution)/shard_map/ppermute | solution.py:346
  27.4 0.1 collective-permute-start.10
  27.5 0.0 collective-permute-done.8.refs_0_.low_other
  27.5 1.0 %solution_other.1.x_other = f32[2048,128]{1,0:T(8,128)S(1)} custom-call(s32[8,128]{1,0:T(8,128)S(1)} %broadcast_in_dim.9.count_ref, f32[2048,256]{1,0:T(8,128)S(1)} %get-tuple-element.50.x_ref, f32[256,2048]{1,0:T(8,128)S(1)} %get-tuple-element.51.q_ref, f32[768,128]{1,0:T(8,128)S(1)} %collective-permute-done.8.refs_0_.low_other), custom_call_target="tpu_custom_call" | custom-call | flops 1000000000 | bytes 1048576 | tf_op jit(solution)/shard_map/solution_other/pallas_call | solution.py:376
  28.4 0.2 collective-permute-done.10.k_other
  28.6 2.8 %factor_rows.1 = (f32[2048,256]{1,0:T(8,128)}, bf16[256,2048]{1,0:T(8,128)(2,1)}, bf16[256,2048]{1,0:T(8,128)(2,1)}) custom-call(s32[8,128]{1,0:T(8,128)S(1)} %broadcast_in_dim.9.count_ref, f32[768,128]{1,0:T(8,128)S(1)} %get-tuple-element.46.low_own, f32[768,128]{1,0:T(8,128)S(1)} %collective-permute-done.8.refs_0_.low_other, ...), custom_call_target="tpu_custom_call" | custom-call | tf_op jit(solution)/shard_map/factor_rows/pallas_call | solution.py:376
  (5 shorter events, 0.1 us)
Async XLA Ops:
  5.3 1.8 %collective-permute-start = (f32[448,128]{1,0:T(8,128)S(1)}, f32[448,128]{1,0:T(8,128)S(1)}, u32[]{:S(2)}, u32[]{:S(2)}) collective-permute-start(f32[448,128]{1,0:T(8,128)S(1)} %get-tuple-element.29), channel_id=1, source_target_pairs={{0,1},{1,0},{2,3},{3,2},{4,5},{5,4},{6,7},{7,6},{8,9},{9,8},{10,11... | collective-permute-start | bytes 688136 | tf_op jit(solution)/shard_map/ppermute | solution.py:346
  7.6 3.1 %collective-permute-start.3 = (f32[576,128]{1,0:T(8,128)S(1)}, f32[576,128]{1,0:T(8,128)S(1)}, u32[]{:S(2)}, u32[]{:S(2)}) collective-permute-start(f32[576,128]{1,0:T(8,128)S(1)} %get-tuple-element.39), channel_id=1, source_target_pairs={{0,1},{1,0},{2,3},{3,2},{4,5},{5,4},{6,7},{7,6},{8,9},{9,8},{10,11... | collective-permute-start | bytes 884744 | tf_op jit(solution)/shard_map/ppermute | solution.py:346
  7.8 7.1 %collective-permute-start.1 = (f32[288,128]{1,0:T(8,128)S(1)}, f32[288,128]{1,0:T(8,128)S(1)}, u32[]{:S(2)}, u32[]{:S(2)}) collective-permute-start(f32[288,128]{1,0:T(8,128)S(1)} %get-tuple-element.32.own_ref), channel_id=1, source_target_pairs={{0,2},{1,3},{2,0},{3,1},{4,6},{5,7},{6,4},{7,5},{8,10},{9,11},{10,... | collective-permute-start | bytes 442376 | tf_op jit(solution)/shard_map/ppermute | solution.py:346
  10.7 6.7 %collective-permute-start.4 = (f32[128,128]{1,0:T(8,128)S(1)}, f32[128,128]{1,0:T(8,128)S(1)}, u32[]{:S(2)}, u32[]{:S(2)}) collective-permute-start(f32[128,128]{1,0:T(8,128)S(1)} %get-tuple-element.41.sent_ref), channel_id=1, source_target_pairs={{0,4},{1,5},{2,6},{3,7},{4,0},{5,1},{6,2},{7,3},{8,12},{9,13},{10,... | collective-permute-start | bytes 196616 | tf_op jit(solution)/shard_map/ppermute | solution.py:346
  12.4 5.1 %collective-permute-start.5 = (f32[96,128]{1,0:T(8,128)S(1)}, f32[96,128]{1,0:T(8,128)S(1)}, u32[]{:S(2)}, u32[]{:S(2)}) collective-permute-start(f32[96,128]{1,0:T(8,128)S(1)} %get-tuple-element.43), channel_id=1, source_target_pairs={{0,8},{1,9},{2,10},{3,11},{4,12},{5,13},{6,14},{7,15},{8,0},{9,1},... | collective-permute-start | bytes 147464 | tf_op jit(solution)/shard_map/ppermute | solution.py:346
  15.3 4.5 %collective-permute-start.2 = (f32[160,128]{1,0:T(8,128)S(1)}, f32[160,128]{1,0:T(8,128)S(1)}, u32[]{:S(2)}, u32[]{:S(2)}) collective-permute-start(f32[160,128]{1,0:T(8,128)S(1)} %get-tuple-element.33.own_ref), channel_id=1, source_target_pairs={{0,4},{1,5},{2,6},{3,7},{4,0},{5,1},{6,2},{7,3},{8,12},{9,13},{10,... | collective-permute-start | bytes 245768 | tf_op jit(solution)/shard_map/ppermute | solution.py:346
  17.5 5.7 %collective-permute-start.7 = (f32[384,128]{1,0:T(8,128)S(1)}, f32[384,128]{1,0:T(8,128)S(1)}, u32[]{:S(2)}, u32[]{:S(2)}) collective-permute-start(f32[384,128]{1,0:T(8,128)S(1)} %side_join_1.1.refs_0_.sent_ref.refs_9_), channel_id=1, source_target_pairs={{0,2},{1,3},{2,0},{3,1},{4,6},{5,7},{6,4},{7,5},{8,10},{9,11},{10,... | collective-permute-start | bytes 589832 | tf_op jit(solution)/shard_map/ppermute | solution.py:346
  20.1 4.9 %collective-permute-start.6 = (f32[64,128]{1,0:T(8,128)S(1)}, f32[64,128]{1,0:T(8,128)S(1)}, u32[]{:S(2)}, u32[]{:S(2)}) collective-permute-start(f32[64,128]{1,0:T(8,128)S(1)} %get-tuple-element.44.own_ref), channel_id=1, source_target_pairs={{0,8},{1,9},{2,10},{3,11},{4,12},{5,13},{6,14},{7,15},{8,0},{9,1},... | collective-permute-start | bytes 98312 | tf_op jit(solution)/shard_map/ppermute | solution.py:346
  23.2 4.2 %collective-permute-start.9 = (f32[96,128]{1,0:T(8,128)S(1)}, f32[96,128]{1,0:T(8,128)S(1)}, u32[]{:S(2)}, u32[]{:S(2)}) collective-permute-start(f32[96,128]{1,0:T(8,128)S(1)} %side_top.1.refs_0_.sent_ref), channel_id=1, source_target_pairs={{0,4},{1,5},{2,6},{3,7},{4,0},{5,1},{6,2},{7,3},{8,12},{9,13},{10,... | collective-permute-start | bytes 147464 | tf_op jit(solution)/shard_map/ppermute | solution.py:346
  25.5 1.9 %collective-permute-start.8 = (f32[768,128]{1,0:T(8,128)S(1)}, f32[768,128]{1,0:T(8,128)S(1)}, u32[]{:S(2)}, u32[]{:S(2)}) collective-permute-start(f32[768,128]{1,0:T(8,128)S(1)} %get-tuple-element.47), channel_id=1, source_target_pairs={{0,1},{1,0},{2,3},{3,2},{4,5},{5,4},{6,7},{7,6},{8,9},{9,8},{10,11... | collective-permute-start | bytes 1179656 | tf_op jit(solution)/shard_map/ppermute | solution.py:346
  27.4 1.3 %collective-permute-start.10 = (f32[64,128]{1,0:T(8,128)S(1)}, f32[64,128]{1,0:T(8,128)S(1)}, u32[]{:S(2)}, u32[]{:S(2)}) collective-permute-start(f32[64,128]{1,0:T(8,128)S(1)} %get-tuple-element.48.k_own), channel_id=1, source_target_pairs={{0,1},{1,0},{2,3},{3,2},{4,5},{5,4},{6,7},{7,6},{8,9},{9,8},{10,11... | collective-permute-start | bytes 98312 | tf_op jit(solution)/shard_map/ppermute | solution.py:346

commit v8 on v7

--- a/solution.py
+++ b/solution.py
@@ -79,6 +79,14 @@
     if eighth % 128:
         return [(0, row_count)]
     sizes = [eighth, 2 * eighth, 2 * eighth, 2 * eighth, eighth]
+    return [(sum(sizes[:n]), size) for n, size in enumerate(sizes)]
+
+
+def last_row_parts(row_count):
+    eighth = row_count // 8
+    if eighth % 128:
+        return [(0, row_count)]
+    sizes = [2 * eighth, 2 * eighth, 3 * eighth, eighth]
     return [(sum(sizes[:n]), size) for n, size in enumerate(sizes)]
 
 
@@ -314,7 +322,7 @@
 
 
 def factor_kernel(dims, count_ref, low_own, low_other, k_own, k_other, h_ref, x_own, x_other, w_ref, *refs):
-    wide, scale, chunk = dims
+    wide, scale, parts = dims
     sol_out, left_out, right_out, left, right, sems = refs
     sender = Sender(sems)
     half = x_own.shape[1]
@@ -328,9 +336,9 @@
     l = jnp.concatenate([whole(low_own, low_other, wide, low), l_top * scale], 0)
     k_low = jnp.concatenate([low_own[wide + low : at, :], low_other[wide + low : at, :]], 1)
     k = jnp.concatenate([k_low, jnp.concatenate([k_own[...], k_other[...]], 1) * scale], 0)
-    for i in range(w_ref.shape[0] // chunk):
-        part, place = slice(i * chunk, (i + 1) * chunk), pl.ds(i * chunk, chunk)
-        live = i * chunk + lax.broadcasted_iota(jnp.int32, (1, chunk), 1) < count_ref[:1, :1]
+    for first, size in parts:
+        part, place = slice(first, first + size), pl.ds(first, size)
+        live = first + lax.broadcasted_iota(jnp.int32, (1, size), 1) < count_ref[:1, :1]
         left_now = dot(l, w_ref[part, :], ((1,), (1,)))
         left[:, part] = jnp.where(live, left_now, 0.0).astype(left.dtype)
         sender.send(left.at[:, place], left_out.at[:, place])
@@ -360,6 +368,7 @@
     chunk = min(512, row_count)
     steps = row_count // chunk
     parts = row_parts(row_count)
+    last_parts = last_row_parts(row_count)
     u_all = coeff_basis.reshape(wide, row_count)
     q_all = saved_basis.reshape(wide, row_count)
 
@@ -541,7 +550,7 @@
     )
     grad = shape(wide, row_count, dtype=jnp.bfloat16)
     sol, left, right = call(
-        functools.partial(factor_kernel, (wide, dims[2], chunk)),
+        functools.partial(factor_kernel, (wide, dims[2], last_parts)),
         "factor_rows",
         [shape(row_count, col_count), grad, grad],
         count,
@@ -554,7 +563,7 @@
         sol_other,
         w_vmem,
         out_specs=[anywhere] * 3,
-        scratch=[pltpu.VMEM(grad.shape, grad.dtype)] * 2 + [pltpu.SemaphoreType.DMA((2 * steps + 2,))],
+        scratch=[pltpu.VMEM(grad.shape, grad.dtype)] * 2 + [pltpu.SemaphoreType.DMA((2 * len(last_parts) + 2,))],
         params=large,
     )
     return sol, left.reshape(coeff_basis.shape), right.reshape(coeff_basis.shape)

time: 31.6 us -> 31.6 us (level)
  no operation moved by 1% of the time
where the time goes in v8:
time: 31.6 us; the launch traced here: 31.4 us
  starting transfers between devices  15.6 us (49%)
  Pallas kernels  11.6 us (37%)
  waiting for transfers between devices  2.75 us (9%)
  between operations  1.41 us (4%)
    ppermute x11, starting transfers between devices, swapped(): return lax.ppermute(value, 'leaf', pairs)  15.6 us
    pallas_call x14, Pallas kernels, call(): pl.pallas_call(kernel, out_shape=out_shape, in_specs=[vmem] * len(operand...  7.66 us
    pallas_call x1, Pallas kernels, body(): pl.pallas_call(functools.partial(local_kernel, (levels, rank, base_bits),...  3.99 us
    ppermute x11, waiting for transfers between devices, swapped(): return lax.ppermute(value, 'leaf', pairs)  2.75 us
  transfers between devices with their start and end apart: 11, of which 6 were waited for; matrix products, arithmetic and copies ran while one was open for 0% of the time, Pallas kernels for 14%

profile of v8, /device:TPU:0, one launch (start us, length us, event | category | flops | bytes accessed | tf_op | source)
XLA Modules:
  0.0 31.4 jit_solution(13637415744981117545)
XLA Ops:
  1.3 4.0 %local_sums.1 = (f32[448,128]{1,0:T(8,128)S(1)}, f32[448,128]{1,0:T(8,128)S(1)}, f32[256,256]{1,0:T(8,128)S(1)}, f32[4,128,128]{2,1,0:T(8,128)S(1)}, f32[2048,25...) custom-call(s32[8,128]{1,0:T(8,128)S(1)} %broadcast_in_dim.9.count_ref, ...), custom_call_target="tpu_custom_call" | custom-call | tf_op jit(solution)/shard_map/local_sums/pallas_call | solution.py:403
  5.3 0.5 %collective-permute-start = (f32[448,128]{1,0:T(8,128)S(1)}, f32[448,128]{1,0:T(8,128)S(1)}, u32[]{:S(2)}, u32[]{:S(2)}) collective-permute-start(f32[448,128]{1,0:T(8,128)S(1)} %get-tuple-element.29), channel_id=1, source_target_pairs={{0,1},{1,0},{2,3},{3,2},{4,5},{5,4},{6,7},{7,6},{8,9},{9,8},{10,11... | collective-permute-start | bytes 688136 | tf_op jit(solution)/shard_map/ppermute | solution.py:354
  5.8 1.3 %side_sums.1.k_ref = f32[256,256]{1,0:T(8,128)S(1)} custom-call(s32[8,128]{1,0:T(8,128)S(1)} %broadcast_in_dim.9.count_ref, f32[2048,256]{1,0:T(8,128)S(1)} %get-tuple-element.34.w_ref, f32[256,2048]{1,0:T(8,128)S(1)} %get-tuple-element.35.u_ref), custom_call_target="tpu_custom_call" | custom-call | flops 805306368 | bytes 1048576 | tf_op jit(solution)/shard_map/side_sums/pallas_call | solution.py:385
  7.1 0.0 collective-permute-done.sib_ref.refs_0_
  7.1 0.4 %level_0.1 = (f32[128,128]{1,0:T(8,128)S(1)}, f32[288,128]{1,0:T(8,128)S(1)}) custom-call(f32[448,128]{1,0:T(8,128)S(1)} %get-tuple-element.30.own_ref.refs_11_, f32[448,128]{1,0:T(8,128)S(1)} %collective-permute-done.sib_ref.refs_0_, f32[4,128,128]{2,1,0:T(8,128)S(1)} %get-tuple-element.31.nodes_ref), custom_call_target="tpu_custom_call" | custom-call | flops 20000000000 | bytes 1048576 | tf_op jit(solution)/shard_map/level_0/pallas_call | solution.py:385
  7.5 0.1 side_state.1
  7.6 0.3 collective-permute-start.3
  7.8 2.8 %collective-permute-start.1 = (f32[288,128]{1,0:T(8,128)S(1)}, f32[288,128]{1,0:T(8,128)S(1)}, u32[]{:S(2)}, u32[]{:S(2)}) collective-permute-start(f32[288,128]{1,0:T(8,128)S(1)} %get-tuple-element.32.own_ref), channel_id=1, source_target_pairs={{0,2},{1,3},{2,0},{3,1},{4,6},{5,7},{6,4},{7,5},{8,10},{9,11},{10,... | collective-permute-start | bytes 442376 | tf_op jit(solution)/shard_map/ppermute | solution.py:354
  10.7 0.0 collective-permute-done.3.sib_ref.refs_8_
  10.7 1.6 %collective-permute-start.4 = (f32[128,128]{1,0:T(8,128)S(1)}, f32[128,128]{1,0:T(8,128)S(1)}, u32[]{:S(2)}, u32[]{:S(2)}) collective-permute-start(f32[128,128]{1,0:T(8,128)S(1)} %get-tuple-element.41.sent_ref), channel_id=1, source_target_pairs={{0,4},{1,5},{2,6},{3,7},{4,0},{5,1},{6,2},{7,3},{8,12},{9,13},{10,... | collective-permute-start | bytes 196616 | tf_op jit(solution)/shard_map/ppermute | solution.py:354
  12.4 2.6 %collective-permute-start.5 = (f32[96,128]{1,0:T(8,128)S(1)}, f32[96,128]{1,0:T(8,128)S(1)}, u32[]{:S(2)}, u32[]{:S(2)}) collective-permute-start(f32[96,128]{1,0:T(8,128)S(1)} %get-tuple-element.43), channel_id=1, source_target_pairs={{0,8},{1,9},{2,10},{3,11},{4,12},{5,13},{6,14},{7,15},{8,0},{9,1},... | collective-permute-start | bytes 147464 | tf_op jit(solution)/shard_map/ppermute | solution.py:354
  14.9 0.0 collective-permute-done.1.sib_ref.refs_1_
  14.9 0.4 %level_1.1 = (f32[128,128]{1,0:T(8,128)S(1)}, f32[160,128]{1,0:T(8,128)S(1)}) custom-call(f32[288,128]{1,0:T(8,128)S(1)} %get-tuple-element.32.own_ref, f32[288,128]{1,0:T(8,128)S(1)} %collective-permute-done.1.sib_ref.refs_1_, f32[4,128,128]{2,1,0:T(8,128)S(1)} %get-tuple-element.31.nodes_ref), custom_call_target="tpu_custom_call" | custom-call | flops 20000000000 | bytes 1048576 | tf_op jit(solution)/shard_map/level_1/pallas_call | solution.py:385
  15.3 1.8 %collective-permute-start.2 = (f32[160,128]{1,0:T(8,128)S(1)}, f32[160,128]{1,0:T(8,128)S(1)}, u32[]{:S(2)}, u32[]{:S(2)}) collective-permute-start(f32[160,128]{1,0:T(8,128)S(1)} %get-tuple-element.33.own_ref), channel_id=1, source_target_pairs={{0,4},{1,5},{2,6},{3,7},{4,0},{5,1},{6,2},{7,3},{8,12},{9,13},{10,... | collective-permute-start | bytes 245768 | tf_op jit(solution)/shard_map/ppermute | solution.py:354
  17.1 0.3 %collective-permute-done.5.refs_0_ = f32[96,128]{1,0:T(8,128)S(1)} collective-permute-done((f32[96,128]{1,0:T(8,128)S(1)}, f32[96,128]{1,0:T(8,128)S(1)}, u32[]{:S(2)}, u32[]{:S(2)}) %collective-permute-start.5) | collective-permute-done | bytes 49184 | tf_op jit(solution)/shard_map/ppermute | solution.py:354
  17.5 0.0 collective-permute-done.4.got_ref
  17.5 1.6 %collective-permute-start.7 = (f32[384,128]{1,0:T(8,128)S(1)}, f32[384,128]{1,0:T(8,128)S(1)}, u32[]{:S(2)}, u32[]{:S(2)}) collective-permute-start(f32[384,128]{1,0:T(8,128)S(1)} %side_join_1.1.refs_0_.sent_ref.refs_9_), channel_id=1, source_target_pairs={{0,2},{1,3},{2,0},{3,1},{4,6},{5,7},{6,4},{7,5},{8,10},{9,11},{10,... | collective-permute-start | bytes 589832 | tf_op jit(solution)/shard_map/ppermute | solution.py:354
  19.1 0.7 %collective-permute-done.2.sib_ref.refs_2_ = f32[160,128]{1,0:T(8,128)S(1)} collective-permute-done((f32[160,128]{1,0:T(8,128)S(1)}, f32[160,128]{1,0:T(8,128)S(1)}, u32[]{:S(2)}, u32[]{:S(2)}) %collective-permute-start.2) | collective-permute-done | bytes 81952 | tf_op jit(solution)/shard_map/ppermute | solution.py:354
  19.8 0.3 %level_2.1 = (f32[128,128]{1,0:T(8,128)S(1)}, f32[64,128]{1,0:T(8,128)S(1)}) custom-call(f32[160,128]{1,0:T(8,128)S(1)} %get-tuple-element.33.own_ref, f32[160,128]{1,0:T(8,128)S(1)} %collective-permute-done.2.sib_ref.refs_2_, f32[4,128,128]{2,1,0:T(8,128)S(1)} %get-tuple-element.31.nodes_ref, f32[384,128]{1,0:T(8,128)S(1)} %side_join_1.1.refs_0_.sent_ref.refs_9_), custom_call_target="tpu_custom_call" | custom-call | flops 20000000000 | bytes 1048576 | tf_op jit(solution)/shard_map/level_2/pallas_call | solution.py:385
  20.1 2.8 %collective-permute-start.6 = (f32[64,128]{1,0:T(8,128)S(1)}, f32[64,128]{1,0:T(8,128)S(1)}, u32[]{:S(2)}, u32[]{:S(2)}) collective-permute-start(f32[64,128]{1,0:T(8,128)S(1)} %get-tuple-element.44.own_ref), channel_id=1, source_target_pairs={{0,8},{1,9},{2,10},{3,11},{4,12},{5,13},{6,14},{7,15},{8,0},{9,1},... | collective-permute-start | bytes 98312 | tf_op jit(solution)/shard_map/ppermute | solution.py:354
  23.0 0.2 collective-permute-done.7.got_ref.refs_10_
  23.2 1.4 %collective-permute-start.9 = (f32[96,128]{1,0:T(8,128)S(1)}, f32[96,128]{1,0:T(8,128)S(1)}, u32[]{:S(2)}, u32[]{:S(2)}) collective-permute-start(f32[96,128]{1,0:T(8,128)S(1)} %side_top.1.refs_0_.sent_ref), channel_id=1, source_target_pairs={{0,4},{1,5},{2,6},{3,7},{4,0},{5,1},{6,2},{7,3},{8,12},{9,13},{10,... | collective-permute-start | bytes 147464 | tf_op jit(solution)/shard_map/ppermute | solution.py:354
  24.6 0.4 %collective-permute-done.6.sib_ref.refs_3_ = f32[64,128]{1,0:T(8,128)S(1)} collective-permute-done((f32[64,128]{1,0:T(8,128)S(1)}, f32[64,128]{1,0:T(8,128)S(1)}, u32[]{:S(2)}, u32[]{:S(2)}) %collective-permute-start.6) | collective-permute-done | bytes 32800 | tf_op jit(solution)/shard_map/ppermute | solution.py:354
  25.0 0.2 level_3.1.refs_7_.refs_3_
  25.2 0.3 end_low.1
  25.5 0.1 collective-permute-start.8
  25.6 1.0 %solution_own.1.x_own = f32[2048,128]{1,0:T(8,128)S(1)} custom-call(s32[8,128]{1,0:T(8,128)S(1)} %broadcast_in_dim.9.count_ref, f32[2048,256]{1,0:T(8,128)S(1)} %get-tuple-element.50.x_ref, f32[256,2048]{1,0:T(8,128)S(1)} %get-tuple-element.51.q_ref, f32[128,128]{1,0:T(8,128)S(1)} %get-tuple-element.37.after_ref.refs_4_.refs_0_, ...), custom_call_target="tpu_custom_call" | custom-call | flops 1000000000 | bytes 1048576 | tf_op jit(solution)/shard_map/solution_own/pallas_call | solution.py:385
  26.6 0.8 %collective-permute-done.9.got_ref = f32[96,128]{1,0:T(8,128)S(1)} collective-permute-done((f32[96,128]{1,0:T(8,128)S(1)}, f32[96,128]{1,0:T(8,128)S(1)}, u32[]{:S(2)}, u32[]{:S(2)}) %collective-permute-start.9) | collective-permute-done | bytes 49184 | tf_op jit(solution)/shard_map/ppermute | solution.py:354
  27.4 0.1 collective-permute-start.10
  27.5 0.0 collective-permute-done.8.refs_0_.low_other
  27.5 1.0 %solution_other.1.x_other = f32[2048,128]{1,0:T(8,128)S(1)} custom-call(s32[8,128]{1,0:T(8,128)S(1)} %broadcast_in_dim.9.count_ref, f32[2048,256]{1,0:T(8,128)S(1)} %get-tuple-element.50.x_ref, f32[256,2048]{1,0:T(8,128)S(1)} %get-tuple-element.51.q_ref, f32[768,128]{1,0:T(8,128)S(1)} %collective-permute-done.8.refs_0_.low_other), custom_call_target="tpu_custom_call" | custom-call | flops 1000000000 | bytes 1048576 | tf_op jit(solution)/shard_map/solution_other/pallas_call | solution.py:385
  28.4 0.2 collective-permute-done.10.k_other
  28.6 2.8 %factor_rows.1 = (f32[2048,256]{1,0:T(8,128)}, bf16[256,2048]{1,0:T(8,128)(2,1)}, bf16[256,2048]{1,0:T(8,128)(2,1)}) custom-call(s32[8,128]{1,0:T(8,128)S(1)} %broadcast_in_dim.9.count_ref, f32[768,128]{1,0:T(8,128)S(1)} %get-tuple-element.46.low_own, f32[768,128]{1,0:T(8,128)S(1)} %collective-permute-done.8.refs_0_.low_other, ...), custom_call_target="tpu_custom_call" | custom-call | tf_op jit(solution)/shard_map/factor_rows/pallas_call | solution.py:385
  (5 shorter events, 0.1 us)
Async XLA Ops:
  5.3 1.8 %collective-permute-start = (f32[448,128]{1,0:T(8,128)S(1)}, f32[448,128]{1,0:T(8,128)S(1)}, u32[]{:S(2)}, u32[]{:S(2)}) collective-permute-start(f32[448,128]{1,0:T(8,128)S(1)} %get-tuple-element.29), channel_id=1, source_target_pairs={{0,1},{1,0},{2,3},{3,2},{4,5},{5,4},{6,7},{7,6},{8,9},{9,8},{10,11... | collective-permute-start | bytes 688136 | tf_op jit(solution)/shard_map/ppermute | solution.py:354
  7.6 3.1 %collective-permute-start.3 = (f32[576,128]{1,0:T(8,128)S(1)}, f32[576,128]{1,0:T(8,128)S(1)}, u32[]{:S(2)}, u32[]{:S(2)}) collective-permute-start(f32[576,128]{1,0:T(8,128)S(1)} %get-tuple-element.39), channel_id=1, source_target_pairs={{0,1},{1,0},{2,3},{3,2},{4,5},{5,4},{6,7},{7,6},{8,9},{9,8},{10,11... | collective-permute-start | bytes 884744 | tf_op jit(solution)/shard_map/ppermute | solution.py:354
  7.8 7.1 %collective-permute-start.1 = (f32[288,128]{1,0:T(8,128)S(1)}, f32[288,128]{1,0:T(8,128)S(1)}, u32[]{:S(2)}, u32[]{:S(2)}) collective-permute-start(f32[288,128]{1,0:T(8,128)S(1)} %get-tuple-element.32.own_ref), channel_id=1, source_target_pairs={{0,2},{1,3},{2,0},{3,1},{4,6},{5,7},{6,4},{7,5},{8,10},{9,11},{10,... | collective-permute-start | bytes 442376 | tf_op jit(solution)/shard_map/ppermute | solution.py:354
  10.7 6.7 %collective-permute-start.4 = (f32[128,128]{1,0:T(8,128)S(1)}, f32[128,128]{1,0:T(8,128)S(1)}, u32[]{:S(2)}, u32[]{:S(2)}) collective-permute-start(f32[128,128]{1,0:T(8,128)S(1)} %get-tuple-element.41.sent_ref), channel_id=1, source_target_pairs={{0,4},{1,5},{2,6},{3,7},{4,0},{5,1},{6,2},{7,3},{8,12},{9,13},{10,... | collective-permute-start | bytes 196616 | tf_op jit(solution)/shard_map/ppermute | solution.py:354
  12.4 5.1 %collective-permute-start.5 = (f32[96,128]{1,0:T(8,128)S(1)}, f32[96,128]{1,0:T(8,128)S(1)}, u32[]{:S(2)}, u32[]{:S(2)}) collective-permute-start(f32[96,128]{1,0:T(8,128)S(1)} %get-tuple-element.43), channel_id=1, source_target_pairs={{0,8},{1,9},{2,10},{3,11},{4,12},{5,13},{6,14},{7,15},{8,0},{9,1},... | collective-permute-start | bytes 147464 | tf_op jit(solution)/shard_map/ppermute | solution.py:354
  15.3 4.5 %collective-permute-start.2 = (f32[160,128]{1,0:T(8,128)S(1)}, f32[160,128]{1,0:T(8,128)S(1)}, u32[]{:S(2)}, u32[]{:S(2)}) collective-permute-start(f32[160,128]{1,0:T(8,128)S(1)} %get-tuple-element.33.own_ref), channel_id=1, source_target_pairs={{0,4},{1,5},{2,6},{3,7},{4,0},{5,1},{6,2},{7,3},{8,12},{9,13},{10,... | collective-permute-start | bytes 245768 | tf_op jit(solution)/shard_map/ppermute | solution.py:354
  17.5 5.7 %collective-permute-start.7 = (f32[384,128]{1,0:T(8,128)S(1)}, f32[384,128]{1,0:T(8,128)S(1)}, u32[]{:S(2)}, u32[]{:S(2)}) collective-permute-start(f32[384,128]{1,0:T(8,128)S(1)} %side_join_1.1.refs_0_.sent_ref.refs_9_), channel_id=1, source_target_pairs={{0,2},{1,3},{2,0},{3,1},{4,6},{5,7},{6,4},{7,5},{8,10},{9,11},{10,... | collective-permute-start | bytes 589832 | tf_op jit(solution)/shard_map/ppermute | solution.py:354
  20.1 4.9 %collective-permute-start.6 = (f32[64,128]{1,0:T(8,128)S(1)}, f32[64,128]{1,0:T(8,128)S(1)}, u32[]{:S(2)}, u32[]{:S(2)}) collective-permute-start(f32[64,128]{1,0:T(8,128)S(1)} %get-tuple-element.44.own_ref), channel_id=1, source_target_pairs={{0,8},{1,9},{2,10},{3,11},{4,12},{5,13},{6,14},{7,15},{8,0},{9,1},... | collective-permute-start | bytes 98312 | tf_op jit(solution)/shard_map/ppermute | solution.py:354
  23.2 4.2 %collective-permute-start.9 = (f32[96,128]{1,0:T(8,128)S(1)}, f32[96,128]{1,0:T(8,128)S(1)}, u32[]{:S(2)}, u32[]{:S(2)}) collective-permute-start(f32[96,128]{1,0:T(8,128)S(1)} %side_top.1.refs_0_.sent_ref), channel_id=1, source_target_pairs={{0,4},{1,5},{2,6},{3,7},{4,0},{5,1},{6,2},{7,3},{8,12},{9,13},{10,... | collective-permute-start | bytes 147464 | tf_op jit(solution)/shard_map/ppermute | solution.py:354
  25.5 1.9 %collective-permute-start.8 = (f32[768,128]{1,0:T(8,128)S(1)}, f32[768,128]{1,0:T(8,128)S(1)}, u32[]{:S(2)}, u32[]{:S(2)}) collective-permute-start(f32[768,128]{1,0:T(8,128)S(1)} %get-tuple-element.47), channel_id=1, source_target_pairs={{0,1},{1,0},{2,3},{3,2},{4,5},{5,4},{6,7},{7,6},{8,9},{9,8},{10,11... | collective-permute-start | bytes 1179656 | tf_op jit(solution)/shard_map/ppermute | solution.py:354
  27.4 1.3 %collective-permute-start.10 = (f32[64,128]{1,0:T(8,128)S(1)}, f32[64,128]{1,0:T(8,128)S(1)}, u32[]{:S(2)}, u32[]{:S(2)}) collective-permute-start(f32[64,128]{1,0:T(8,128)S(1)} %get-tuple-element.48.k_own), channel_id=1, source_target_pairs={{0,1},{1,0},{2,3},{3,2},{4,5},{5,4},{6,7},{7,6},{8,9},{9,8},{10,11... | collective-permute-start | bytes 98312 | tf_op jit(solution)/shard_map/ppermute | solution.py:354
